TPU v7x, 32 devices: a whole 2x2x4 slice. The times are simulated.
32 devices in a mesh: groups: 2 (over y), ep: 8 (over z, x), tp: 2 (over core).
Axes of the slice: x: 2, y: 2, z: 4, core: 2. Of those that a mesh axis runs over, the one named last changes fastest.
Arguments:
- hidden: bfloat16 [64, 3584], P(('groups', 'ep')), parts along dimension 0, may hold values from -6 to 6
- expert_ids: int32 [64, 2], P(('groups', 'ep')), parts along dimension 0, may hold values from 0 to 1, all different within a row; in each aligned block of 4 rows (0 to 3, 4 to 7, ...) at most 4 rows name the same one
- gate_scores: float32 [64, 2], P(('groups', 'ep')), parts along dimension 0, may hold values from 0.05 to 1
- w_gate: bfloat16 [8, 896, 1024], P('ep', None, 'tp'), may hold values from -0.09375 to 0.09375
- w_up: bfloat16 [8, 896, 1024], P('ep', None, 'tp'), may hold values from -0.09375 to 0.09375
- w_down: bfloat16 [8, 1024, 896], P('ep', 'tp'), may hold values from -0.1875 to 0.1875
Outputs:
- combined: bfloat16 [64, 3584], P(('groups', 'ep')), parts along dimension 0
There are 2 independent parts, one for each index of `groups`. A program takes and returns all parts, laid end to end along the dimension named above; an argument that names none is the same for every part. Nothing has to cross between parts.
Inputs may be any that keep to these rules, and one draw needn't show every extreme that they name: `expert_ids`: each row names 2 different experts. Within the rows of one device (aligned blocks of 4 tokens) no expert is named by more than 4 rows, a bound that some block reaches. Every expert is named somewhere.
All inputs are finite; a program needn't handle non-finite values.
Results may differ from a plain program's by a relative error of at most 0.0064.
Values may be sent and summed in bfloat16 or wider, within the bound.
No kernel may reach another device: no remote copies, remote signals or barrier semaphores. Data moves between devices by JAX's collectives and lax.ppermute only.
A program may use at most 64 MiB of HBM per device.

v0:
```python
import jax
import jax.numpy as jnp
from jax import lax
from jax.sharding import PartitionSpec as P

GROUP = 4


route_scale = 2.5


def swapped(value, axis, bit):
    mask = 2**bit
    pairs = [(source, source ^ mask) for source in range(lax.axis_size(axis))]
    return lax.ppermute(value, axis, pairs)


def route_tables(expert_ids, experts, capacity):
    tok_rows, route_count = expert_ids.shape
    flat_ids = expert_ids.reshape(-1)
    expert_hot = (flat_ids[:, None] == jnp.arange(experts, dtype=jnp.int32)[None, :]).astype(
        jnp.int32
    )
    ranking = jnp.sum((jnp.cumsum(expert_hot, axis=0) - expert_hot) * expert_hot, axis=1)
    slot_hot = (ranking[:, None] == jnp.arange(capacity, dtype=jnp.int32)[None, :]).astype(
        jnp.float32
    )
    expert_float = expert_hot.astype(jnp.float32).reshape(tok_rows, route_count, experts)
    return (expert_float, slot_hot.reshape(tok_rows, route_count, capacity))


def local(hidden, expert_ids, gate_scores, w_gate, w_up, w_down):
    tok_rows, width_all = hidden.shape
    route_count = expert_ids.shape[1]
    peer_count = lax.axis_size("ep")
    core_count = lax.axis_size("tp")
    core_index = lax.axis_index("tp")
    experts = peer_count // GROUP
    quarter = width_all // GROUP
    capacity = min(tok_rows, 2 * tok_rows * route_count // experts)
    half_cap = capacity // core_count
    group_bits = GROUP.bit_length() - 1
    expert_hot, slot_hot = route_tables(expert_ids, experts, capacity)
    placing = jnp.einsum("tke,tkc->ect", expert_hot, slot_hot).astype(jnp.bfloat16)
    outgoing = jnp.einsum(
        "ect,tgd->egcd",
        placing,
        hidden.reshape(tok_rows, GROUP, quarter),
        preferred_element_type=jnp.float32,
    ).astype(jnp.bfloat16)
    outgoing = outgoing.reshape(peer_count, capacity, quarter)
    arrived = lax.all_to_all(outgoing, "ep", split_axis=0, concat_axis=0, tiled=True)
    row_block = arrived.reshape(peer_count * capacity, quarter)
    gate_part = jnp.dot(row_block, w_gate[0], preferred_element_type=jnp.float32)
    up_part = jnp.dot(row_block, w_up[0], preferred_element_type=jnp.float32)
    for bit_index in range(group_bits):
        other_gate, other_up = swapped((gate_part, up_part), "ep", bit_index)
        gate_part = gate_part + other_gate
        up_part = up_part + other_up
    inner_rows = (jax.nn.silu(gate_part) * up_part).astype(jnp.bfloat16)
    partial_out = jnp.dot(inner_rows, w_down[0], preferred_element_type=jnp.float32)
    partial_out = partial_out.reshape(peer_count, capacity, quarter)
    expert_out = lax.psum_scatter(partial_out, "tp", scatter_dimension=1, tiled=True).astype(
        jnp.bfloat16
    )
    returned = lax.all_to_all(expert_out, "ep", split_axis=0, concat_axis=0, tiled=True)
    routing = (gate_scores / jnp.sum(gate_scores, axis=1, keepdims=True) * route_scale).astype(
        jnp.bfloat16
    )
    own_slots = lax.dynamic_slice_in_dim(slot_hot, core_index * half_cap, half_cap, 2)
    combining = jnp.einsum(
        "tk,tke,tkc->tec", routing.astype(jnp.float32), expert_hot, own_slots
    ).astype(jnp.bfloat16)
    combined = jnp.einsum(
        "tec,egcd->tgd",
        combining,
        returned.reshape(experts, GROUP, half_cap, quarter),
        preferred_element_type=jnp.float32,
    )
    combined = lax.psum(combined.reshape(tok_rows, width_all), "tp")
    return combined.astype(jnp.bfloat16)


def solution(mesh):
    return jax.shard_map(
        local,
        mesh=mesh,
        in_specs=(
            P(("groups", "ep"), None),
            P(("groups", "ep"), None),
            P(("groups", "ep"), None),
            P("ep", None, "tp"),
            P("ep", None, "tp"),
            P("ep", "tp", None),
        ),
        out_specs=P(("groups", "ep"), None),
        check_vma=False,
    )
```

profile of v0, /device:TPU:0, one launch (start us, length us, event | category | flops | bytes accessed | tf_op | source)
XLA Modules:
  0.0 65.8 jit_solution(10591627609937585562)
XLA Ops:
  6.5 0.9 %copy.27 = s32[4,2]{1,0:T(4,128)S(1)} copy(s32[4,2]{0,1:T(2,128)} %param.7) | data formatting | bytes 64 | tf_op args[1]
  7.5 0.2 reduce_window_sum.11
  7.8 0.2 fusion
  8.0 1.0 %convolution_convert_fusion = bf16[2,4,4,896]{3,1,2,0:T(4,128)(2,1)S(1)} fusion(bf16[4,4,896,1]{2,0,1,3:T(4,128)(2,1)} %bitcast.36, bf16[2,4,4,1]{1,0,2,3:T(2,128)(2,1)S(1)} %fusion), kind=kOutput, calls=%fused_computation.1 | convolution fusion | flops 258048 | bytes 86080 | tf_op jit(solution)/shard_map/ect,tgd->egcd/dot_general | solution.py:45
  9.0 13.9 %all_to_all.10 = bf16[8,4,896]{2,1,0:T(4,128)(2,1)S(1)} all-to-all(bf16[8,4,896]{2,1,0:T(4,128)(2,1)S(1)} %bitcast.33), channel_id=1, replica_groups=mesh['groups'=2,'ep'=8,'tp'=2] {'ep'}, dimensions={0} | all-to-all | bytes 114688 | tf_op jit(solution)/shard_map/all_to_all | solution.py:52
  22.9 1.4 %fusion.5 = f32[32,512]{1,0:T(8,128)S(1)} fusion(bf16[32,896]{1,0:T(8,128)(2,1)S(1)} %reshape.39, bf16[1,896,512]{2,1,0:T(8,128)(2,1)} %param.9), kind=kOutput, calls=%fused_computation.9 | convolution fusion | flops 29360128 | bytes 1040384 | tf_op jit(solution)/shard_map/dot_general | solution.py:54
  24.3 0.4 collective-permute-start
  24.8 0.2 fusion.3
  25.0 1.6 %collective-permute-start.2 = (f32[32,512]{1,0:T(8,128)S(1)}, f32[32,512]{1,0:T(8,128)S(1)}, u32[]{:S(2)}, u32[]{:S(2)}) collective-permute-start(f32[32,512]{1,0:T(8,128)S(1)} %fusion.3), channel_id=1, source_target_pairs={{0,2},{2,0},{4,6},{6,4},{8,10},{10,8},{12,14},{14,12},{1,3},{3,1},... | collective-permute-start | bytes 196616 | tf_op jit(solution)/shard_map/ppermute | solution.py:15
  26.7 2.0 %collective-permute-done = f32[32,512]{1,0:T(8,128)S(1)} collective-permute-done((f32[32,512]{1,0:T(8,128)S(1)}, f32[32,512]{1,0:T(8,128)S(1)}, u32[]{:S(2)}, u32[]{:S(2)}) %collective-permute-start) | collective-permute-done | bytes 65568 | tf_op jit(solution)/shard_map/ppermute | solution.py:15
  28.7 0.3 collective-permute-start.1
  29.0 0.4 collective-permute-done.2
  29.4 1.5 %collective-permute-start.3 = (f32[32,512]{1,0:T(8,128)S(1)}, f32[32,512]{1,0:T(8,128)S(1)}, u32[]{:S(2)}, u32[]{:S(2)}) collective-permute-start(f32[32,512]{1,0:T(8,128)S(1)} %add.27), channel_id=1, source_target_pairs={{0,4},{2,6},{4,0},{6,2},{8,12},{10,14},{12,8},{14,10},{1,5},{3,7},... | collective-permute-start | bytes 196616 | tf_op jit(solution)/shard_map/ppermute | solution.py:15
  30.9 2.1 %collective-permute-done.1 = f32[32,512]{1,0:T(8,128)S(1)} collective-permute-done((f32[32,512]{1,0:T(8,128)S(1)}, f32[32,512]{1,0:T(8,128)S(1)}, u32[]{:S(2)}, u32[]{:S(2)}) %collective-permute-start.1) | collective-permute-done | bytes 65568 | tf_op jit(solution)/shard_map/ppermute | solution.py:15
  33.0 0.7 %collective-permute-done.3 = f32[32,512]{1,0:T(8,128)S(1)} collective-permute-done((f32[32,512]{1,0:T(8,128)S(1)}, f32[32,512]{1,0:T(8,128)S(1)}, u32[]{:S(2)}, u32[]{:S(2)}) %collective-permute-start.3) | collective-permute-done | bytes 65568 | tf_op jit(solution)/shard_map/ppermute | solution.py:15
  33.8 0.9 %fusion.1 = f32[8,4,896]{2,0,1:T(8,128)} fusion(bf16[1,512,896]{2,1,0:T(8,128)(2,1)S(1)} %copy-done, bf16[8,4,512]{2,1,0:T(4,128)(2,1)S(1)} %dot_general.39), kind=kOutput, calls=%fused_computation.5 | convolution fusion | flops 29360128 | bytes 1064960 | tf_op jit(solution)/shard_map/dot_general | solution.py:61
  34.9 5.8 %reduce-scatter.2.cloned.1.call-done = f32[8,2,896]{2,0,1:T(8,128)} async-done(((f32[8,4,896]{2,0,1:T(8,128)}), f32[8,2,896]{2,0,1:T(8,128)}) %reduce-scatter.2.cloned.1.call-update) | async-done | bytes 57360 | tf_op jit(solution)/shard_map/reduce_scatter | solution.py:63
  40.7 0.8 %convert_element_type.49 = bf16[8,2,896]{2,0,1:T(8,128)(2,1)S(1)} convert(f32[8,2,896]{2,0,1:T(8,128)} %reduce-scatter.2.cloned.1.call-done) | non-fusion elementwise | flops 14336 | bytes 86016 | tf_op jit(solution)/shard_map/convert_element_type | solution.py:63
  41.5 0.6 copy.32
  42.1 5.7 %all-to-all-start.1 = ((bf16[8,2,896]{2,1,0:T(2,128)(2,1)}), bf16[8,2,896]{2,1,0:T(2,128)(2,1)S(1)}, u32[]{:S(2)}, u32[]{:S(2)}) async-start(bf16[8,2,896]{2,1,0:T(2,128)(2,1)} %copy.32), calls=%async_computation.2 | async-start | bytes 57344 | tf_op jit(solution)/shard_map/all_to_all | solution.py:66
  47.9 0.2 convolution_convert_fusion.2
  48.2 6.3 %all-to-all-done.1 = bf16[8,2,896]{2,1,0:T(2,128)(2,1)S(1)} async-done(((bf16[8,2,896]{2,1,0:T(2,128)(2,1)}), bf16[8,2,896]{2,1,0:T(2,128)(2,1)S(1)}, u32[]{:S(2)}, u32[]{:S(2)}) %all-to-all-start.1) | async-done | bytes 28704 | tf_op jit(solution)/shard_map/all_to_all | solution.py:66
  54.6 0.2 convolution_bitcast_fusion
  54.8 4.1 %psum.7 = bf16[4,3584]{1,0:T(4,128)(2,1)} all-reduce(f32[4,3584]{1,0:T(4,128)S(1)} %convolution_bitcast_fusion), channel_id=1, replica_groups=mesh['groups'=2,'ep'=8,'tp'=2] {'tp'}, use_global_device_ids=true, to_apply=%region_4.5 | all-reduce | flops 14336 | bytes 86016 | tf_op jit(solution)/shard_map/psum | solution.py:80
  (24 shorter events, 0.7 us)
Async XLA Ops:
  6.5 27.2 %copy-start = (bf16[1,512,896]{2,1,0:T(8,128)(2,1)S(1)}, bf16[1,512,896]{2,1,0:T(8,128)(2,1)}, u32[]{:S(2)}) copy-start(bf16[1,512,896]{2,1,0:T(8,128)(2,1)} %param.11) | copy-start | bytes 2752516
  6.5 18.2 %copy-start.1 = (bf16[1,896,512]{2,1,0:T(8,128)(2,1)S(1)}, bf16[1,896,512]{2,1,0:T(8,128)(2,1)}, u32[]{:S(2)}) copy-start(bf16[1,896,512]{2,1,0:T(8,128)(2,1)} %param.10) | copy-start | bytes 2752516
  6.5 34.1 %reduce-scatter.2.cloned.1.call-start = ((), (), s32[]{:S(2)}) async-start(), calls=%async_computation.3 | async-start | bytes 172032 | tf_op jit(solution)/shard_map/reduce_scatter | solution.py:63
  24.3 4.3 %collective-permute-start = (f32[32,512]{1,0:T(8,128)S(1)}, f32[32,512]{1,0:T(8,128)S(1)}, u32[]{:S(2)}, u32[]{:S(2)}) collective-permute-start(f32[32,512]{1,0:T(8,128)S(1)} %fusion.5), channel_id=1, source_target_pairs={{0,2},{2,0},{4,6},{6,4},{8,10},{10,8},{12,14},{14,12},{1,3},{3,1},... | collective-permute-start | bytes 196616 | tf_op jit(solution)/shard_map/ppermute | solution.py:15
  25.0 4.3 %collective-permute-start.2 = (f32[32,512]{1,0:T(8,128)S(1)}, f32[32,512]{1,0:T(8,128)S(1)}, u32[]{:S(2)}, u32[]{:S(2)}) collective-permute-start(f32[32,512]{1,0:T(8,128)S(1)} %fusion.3), channel_id=1, source_target_pairs={{0,2},{2,0},{4,6},{6,4},{8,10},{10,8},{12,14},{14,12},{1,3},{3,1},... | collective-permute-start | bytes 196616 | tf_op jit(solution)/shard_map/ppermute | solution.py:15
  28.7 2.2 %copy-start.2 = (f32[4,2]{0,1:T(2,128)S(1)}, f32[4,2]{0,1:T(2,128)}, u32[]{:S(2)}) copy-start(f32[4,2]{0,1:T(2,128)} %param.8) | copy-start | bytes 100
  28.7 4.3 %collective-permute-start.1 = (f32[32,512]{1,0:T(8,128)S(1)}, f32[32,512]{1,0:T(8,128)S(1)}, u32[]{:S(2)}, u32[]{:S(2)}) collective-permute-start(f32[32,512]{1,0:T(8,128)S(1)} %add.24), channel_id=1, source_target_pairs={{0,4},{2,6},{4,0},{6,2},{8,12},{10,14},{12,8},{14,10},{1,5},{3,7},... | collective-permute-start | bytes 196616 | tf_op jit(solution)/shard_map/ppermute | solution.py:15
  29.4 4.3 %collective-permute-start.3 = (f32[32,512]{1,0:T(8,128)S(1)}, f32[32,512]{1,0:T(8,128)S(1)}, u32[]{:S(2)}, u32[]{:S(2)}) collective-permute-start(f32[32,512]{1,0:T(8,128)S(1)} %add.27), channel_id=1, source_target_pairs={{0,4},{2,6},{4,0},{6,2},{8,12},{10,14},{12,8},{14,10},{1,5},{3,7},... | collective-permute-start | bytes 196616 | tf_op jit(solution)/shard_map/ppermute | solution.py:15
  42.1 12.4 %all-to-all-start.1 = ((bf16[8,2,896]{2,1,0:T(2,128)(2,1)}), bf16[8,2,896]{2,1,0:T(2,128)(2,1)S(1)}, u32[]{:S(2)}, u32[]{:S(2)}) async-start(bf16[8,2,896]{2,1,0:T(2,128)(2,1)} %copy.32), calls=%async_computation.2 | async-start | bytes 57344 | tf_op jit(solution)/shard_map/all_to_all | solution.py:66
Sparse Core Ops, SparseCore 0:
  34.8 5.8 reduce-scatter.1
where the time goes:
time: 66.2 us; the launch traced here: 65.8 us
  blocking collectives  18 us (27%)
  waiting for transfers between devices  17.3 us (26%)
  between operations  13.5 us (20%)
  starting transfers between devices  9.63 us (15%)
  matrix products  4.15 us (6%)
  local copies, waits for them, and re-layouts  1.99 us (3%)
  other arithmetic  1.2 us (2%)
    all_to_all x1, blocking collectives, local(): lax.all_to_all(outgoing, 'ep', split_axis=0, concat_axis=0, tiled=True)  13.9 us
    all_to_all x1, waiting for transfers between devices, local(): lax.all_to_all(expert_out, 'ep', split_axis=0, concat_axis=0, tiled=True)  6.35 us
    reduce_scatter x1, waiting for transfers between devices, local(): lax.psum_scatter(partial_out, 'tp', scatter_dimension=1, tiled=True)  5.78 us
    all_to_all x1, starting transfers between devices, local(): lax.all_to_all(expert_out, 'ep', split_axis=0, concat_axis=0, tiled=True)  5.75 us
    ppermute x4, waiting for transfers between devices, swapped(): return lax.ppermute(value, axis, pairs)  5.15 us
    psum x1, blocking collectives, local(): combined = lax.psum(combined.reshape(tok_rows, width_all), 'tp')  4.12 us
    ppermute x4, starting transfers between devices, swapped(): return lax.ppermute(value, axis, pairs)  3.88 us
    dot_general x1, matrix products, local(): jnp.dot(row_block, w_gate[0], preferred_element_type=jnp.float32)  1.43 us
  transfers between devices with their start and end apart: 6, of which 6 were waited for; matrix products, arithmetic and copies ran while one was open for 1% of the time, Pallas kernels for 0%

commit v1 on v0

v1 whole, which is shorter than its diff:
```python
import jax
import jax.numpy as jnp
from jax import lax
from jax.sharding import PartitionSpec as P

GROUP = 4


route_scale = 2.5


def swapped(value, mask, crossed):
    ranks = lax.axis_size("ep")
    cores = lax.axis_size("tp")
    pairs = []
    for source in range(ranks):
        for core in range(cores):
            target_core = (core + 1) % cores if crossed else core
            pairs.append((source * cores + core, (source ^ mask) * cores + target_core))
    return lax.ppermute(value, ("ep", "tp"), pairs)


def ordered(own, other, bit):
    return jnp.stack([jnp.where(bit, other, own), jnp.where(bit, own, other)])


def spread_tokens(hidden):
    tok_rows, width_all = hidden.shape
    peers = lax.axis_size("ep")
    rank = lax.axis_index("ep")
    quarter = width_all // GROUP
    halves = GROUP
    block = hidden.reshape(tok_rows, GROUP, quarter).transpose(1, 0, 2)[:, None]
    mask = 1
    while mask < peers:
        bit = (rank & mask) > 0
        if halves > 1:
            parts = block.reshape((halves // 2, 2) + block.shape[1:])
            own = jnp.where(bit, parts[:, 1], parts[:, 0])
            sent = jnp.where(bit, parts[:, 0], parts[:, 1])
            halves //= 2
        else:
            own = sent = block
        other = swapped(sent, mask, True)
        both = ordered(own, other, bit)
        block = jnp.moveaxis(both, 0, 1).reshape(own.shape[0], 2 * own.shape[1], tok_rows, quarter)
        mask *= 2
    return block[0]


def route_tables(expert_ids, experts, capacity):
    tok_rows, route_count = expert_ids.shape
    flat_ids = expert_ids.reshape(-1)
    expert_hot = (flat_ids[:, None] == jnp.arange(experts, dtype=jnp.int32)[None, :]).astype(
        jnp.int32
    )
    ranking = jnp.sum((jnp.cumsum(expert_hot, axis=0) - expert_hot) * expert_hot, axis=1)
    slot_hot = (ranking[:, None] == jnp.arange(capacity, dtype=jnp.int32)[None, :]).astype(
        jnp.float32
    )
    expert_float = expert_hot.astype(jnp.float32).reshape(tok_rows, route_count, experts)
    return (expert_float, slot_hot.reshape(tok_rows, route_count, capacity))


def local(hidden, expert_ids, gate_scores, w_gate, w_up, w_down):
    tok_rows, width_all = hidden.shape
    route_count = expert_ids.shape[1]
    peer_count = lax.axis_size("ep")
    core_count = lax.axis_size("tp")
    experts = peer_count // GROUP
    quarter = width_all // GROUP
    group_bits = GROUP.bit_length() - 1
    every_expert = route_count == experts
    if every_expert:
        capacity = tok_rows
        arrived = spread_tokens(hidden)
    else:
        capacity = min(tok_rows, 2 * tok_rows * route_count // experts)
        expert_hot, slot_hot = route_tables(expert_ids, experts, capacity)
        placing = jnp.einsum("tke,tkc->ect", expert_hot, slot_hot).astype(jnp.bfloat16)
        outgoing = jnp.einsum(
            "ect,tgd->egcd",
            placing,
            hidden.reshape(tok_rows, GROUP, quarter),
            preferred_element_type=jnp.float32,
        ).astype(jnp.bfloat16)
        outgoing = outgoing.reshape(peer_count, capacity, quarter)
        arrived = lax.all_to_all(outgoing, "ep", split_axis=0, concat_axis=0, tiled=True)
    row_block = arrived.reshape(peer_count * capacity, quarter)
    gate_part = jnp.dot(row_block, w_gate[0], preferred_element_type=jnp.float32)
    up_part = jnp.dot(row_block, w_up[0], preferred_element_type=jnp.float32)
    parts = jnp.concatenate([gate_part, up_part], axis=1)
    for bit_index in range(group_bits):
        other = swapped(parts.astype(jnp.bfloat16), 2**bit_index, False)
        parts = parts + other.astype(jnp.float32)
    hidden_units = gate_part.shape[1]
    inner_rows = (jax.nn.silu(parts[:, :hidden_units]) * parts[:, hidden_units:]).astype(
        jnp.bfloat16
    )
    partial_out = jnp.dot(inner_rows, w_down[0], preferred_element_type=jnp.float32)
    partial_out = partial_out.astype(jnp.bfloat16).reshape(peer_count, 1, capacity, quarter)
    leaving = jnp.broadcast_to(partial_out, (peer_count, core_count, capacity, quarter))
    returned = lax.all_to_all(
        leaving.reshape(peer_count * core_count, capacity, quarter),
        ("ep", "tp"),
        split_axis=0,
        concat_axis=0,
        tiled=True,
    ).reshape(experts, GROUP, core_count, capacity, quarter)
    routing = (gate_scores / jnp.sum(gate_scores, axis=1, keepdims=True) * route_scale).astype(
        jnp.bfloat16
    )
    routing = routing.astype(jnp.float32)
    if every_expert:
        named = expert_ids[:, :, None] == jnp.arange(experts, dtype=jnp.int32)
        share = jnp.sum(jnp.where(named, routing[:, :, None], 0.0), axis=1)
        weighted = returned.astype(jnp.float32) * share.T[:, None, None, :, None]
        combined = jnp.sum(weighted, axis=(0, 2)).transpose(1, 0, 2)
    else:
        combining = jnp.einsum("tk,tke,tkc->tec", routing, expert_hot, slot_hot)
        combined = jnp.einsum(
            "tec,egpcd->tgd",
            combining.astype(jnp.bfloat16),
            returned,
            preferred_element_type=jnp.float32,
        )
    return combined.reshape(tok_rows, width_all).astype(jnp.bfloat16)


def solution(mesh):
    return jax.shard_map(
        local,
        mesh=mesh,
        in_specs=(
            P(("groups", "ep"), None),
            P(("groups", "ep"), None),
            P(("groups", "ep"), None),
            P("ep", None, "tp"),
            P("ep", None, "tp"),
            P("ep", "tp", None),
        ),
        out_specs=P(("groups", "ep"), None),
        check_vma=False,
    )
```

time: 66.2 us -> 41 us (0.62)
  blocking collectives: 18 us -> 0 us
  between operations: 13.5 us -> 0.12 us
  starting transfers between devices: 9.63 us -> 18.2 us
  matrix products: 4.15 us -> 1.95 us
  other arithmetic: 1.2 us -> 2.63 us
  waiting for transfers between devices: 17.3 us -> 16.3 us
    all_to_all x1 -> x0, blocking collectives: 13.9 us -> none  [local(): lax.all_to_all(outgoing, 'ep', split_axis=0, concat_axis=0, tiled=True)]
    ppermute x4 -> x5, starting transfers between devices: 3.88 us -> 11.3 us  [swapped(): return lax.ppermute(value, ('ep', 'tp'), pairs)]
    reduce_scatter x1 -> x0, waiting for transfers between devices: 5.78 us -> none  [local(): lax.psum_scatter(partial_out, 'tp', scatter_dimension=1, tiled=True)]
    ppermute x4 -> x5, waiting for transfers between devices: 5.15 us -> 9.35 us  [swapped(): return lax.ppermute(value, ('ep', 'tp'), pairs)]
    psum x1 -> x0, blocking collectives: 4.12 us -> none  [local(): combined = lax.psum(combined.reshape(tok_rows, width_all), 'tp')]
    dot_general x4 -> x0, matrix products: 1.56 us -> none  [the longest x1 0.97 us: local(): jnp.einsum('ect,tgd->egcd', placing, hidden.reshape(tok_rows, GROUP, quar...]
    dot_general x1, matrix products: 0.25 us -> 1.43 us  [local(): up_part = jnp.dot(row_block, w_up[0], preferred_element_type=jnp.float32)]
    all_to_all x1, starting transfers between devices: 5.75 us -> 6.93 us  [local(): lax.all_to_all(leaving.reshape(peer_count * core_count, capacity, quarter...]
  transfers between devices with their start and end apart: 6 -> 6, of which waited for: 6 -> 6; matrix products, arithmetic and copies ran while one was open for 1% -> 0% of each run, Pallas kernels for 0% -> 0%
where the time goes in v1:
time: 41 us; the launch traced here: 40.7 us
  starting transfers between devices  18.2 us (44%)
  waiting for transfers between devices  16.3 us (40%)
  other arithmetic  2.63 us (6%)
  matrix products  1.95 us (5%)
  local copies, waits for them, and re-layouts  1.41 us (3%)
    ppermute x5, starting transfers between devices, swapped(): return lax.ppermute(value, ('ep', 'tp'), pairs)  11.3 us
    ppermute x5, waiting for transfers between devices, swapped(): return lax.ppermute(value, ('ep', 'tp'), pairs)  9.35 us
    all_to_all x1, waiting for transfers between devices, local(): lax.all_to_all(leaving.reshape(peer_count * core_count, capacity, quarter...  6.98 us
    all_to_all x1, starting transfers between devices, local(): lax.all_to_all(leaving.reshape(peer_count * core_count, capacity, quarter...  6.93 us
    dot_general x1, matrix products, local(): up_part = jnp.dot(row_block, w_up[0], preferred_element_type=jnp.float32)  1.43 us
    select_n x2, other arithmetic, spread_tokens(): sent = jnp.where(bit, parts[:, 0], parts[:, 1])  0.89 us
    another operation x5, other arithmetic, ordered(): return jnp.stack([jnp.where(bit, other, own), jnp.where(bit, own, other)])  0.86 us
  transfers between devices with their start and end apart: 6, of which 6 were waited for; matrix products, arithmetic and copies ran while one was open for 0% of the time, Pallas kernels for 0%

profile of v1, /device:TPU:0, one launch (start us, length us, event | category | flops | bytes accessed | tf_op | source)
XLA Modules:
  0.0 40.7 jit_solution(14935519528579698892)
XLA Ops:
  0.0 0.0 copy-start
  0.0 0.9 %select_bitcast_fusion.3 = bf16[2,1,4,896]{3,2,0,1:T(4,128)(2,1)S(1)} fusion(pred[]{:T(512)S(6)} %gt.11, bf16[2,2,1,4,896]{4,3,1,0,2:T(4,128)(2,1)} %bitcast.61), kind=kLoop, calls=%fused_computation.30 | loop fusion | flops 7168 | bytes 43009 | tf_op jit(solution)/shard_map/jit(_where)/select_n | solution.py:40
  0.9 2.4 %collective-permute-start = (bf16[2,1,4,896]{3,2,0,1:T(4,128)(2,1)S(1)}, bf16[2,1,4,896]{3,2,0,1:T(4,128)(2,1)S(1)}, u32[]{:S(2)}, u32[]{:S(2)}) collective-permute-start(bf16[2,1,4,896]{3,2,0,1:T(4,128)(2,1)S(1)} %select_bitcast_fusion.3), channel_id=1, source_target_pairs={{0,3},{1,2},{2,1},{3,0},{4,7},{5,6},{6,5},{7,4},{8,11},{9,10},{10,... | collective-permute-start | bytes 43016 | tf_op jit(solution)/shard_map/ppermute | solution.py:20
  3.3 1.4 %collective-permute-done = bf16[2,1,4,896]{3,2,0,1:T(4,128)(2,1)S(1)} collective-permute-done((bf16[2,1,4,896]{3,2,0,1:T(4,128)(2,1)S(1)}, bf16[2,1,4,896]{3,2,0,1:T(4,128)(2,1)S(1)}, u32[]{:S(2)}, u32[]{:S(2)}) %collective-permute-start) | collective-permute-done | bytes 14368 | tf_op jit(solution)/shard_map/ppermute | solution.py:20
  4.8 0.7 %fusion.13 = (bf16[1,2,1,4,896]{4,3,1,2,0:T(4,128)(2,1)S(1)}, bf16[1,2,1,4,896]{4,3,1,2,0:T(4,128)(2,1)S(1)}) fusion(bf16[2,1,4,896]{3,2,0,1:T(4,128)(2,1)S(1)} %collective-permute-done, pred[]{:T(512)S(6)} %gt.11, bf16[2,2,1,4,896]{4,3,1,0,2:T(4,128)(2,1)} %bitcast.62), kind=kLoop, calls=%fused_computation.27 | loop fusion | flops 21504 | bytes 72704 | tf_op jit(solution)/shard_map/stack | solution.py:24
  5.6 2.3 %collective-permute-start.1 = (bf16[1,2,4,896]{3,2,1,0:T(4,128)(2,1)S(1)}, bf16[1,2,4,896]{3,2,1,0:T(4,128)(2,1)S(1)}, u32[]{:S(2)}, u32[]{:S(2)}) collective-permute-start(bf16[1,2,4,896]{3,2,1,0:T(4,128)(2,1)S(1)} %select_bitcast_fusion.2), channel_id=1, source_target_pairs={{0,5},{1,4},{2,7},{3,6},{4,1},{5,0},{6,3},{7,2},{8,13},{9,12},{10,... | collective-permute-start | bytes 43016 | tf_op jit(solution)/shard_map/ppermute | solution.py:20
  7.8 1.4 %collective-permute-done.1 = bf16[1,2,4,896]{3,2,1,0:T(4,128)(2,1)S(1)} collective-permute-done((bf16[1,2,4,896]{3,2,1,0:T(4,128)(2,1)S(1)}, bf16[1,2,4,896]{3,2,1,0:T(4,128)(2,1)S(1)}, u32[]{:S(2)}, u32[]{:S(2)}) %collective-permute-start.1) | collective-permute-done | bytes 14368 | tf_op jit(solution)/shard_map/ppermute | solution.py:20
  9.3 2.8 %collective-permute-start.2 = (bf16[1,4,4,896]{3,2,1,0:T(4,128)(2,1)S(1)}, bf16[1,4,4,896]{3,2,1,0:T(4,128)(2,1)S(1)}, u32[]{:S(2)}, u32[]{:S(2)}) collective-permute-start(bf16[1,4,4,896]{3,2,1,0:T(4,128)(2,1)S(1)} %bitcast.59), channel_id=1, source_target_pairs={{0,9},{1,8},{2,11},{3,10},{4,13},{5,12},{6,15},{7,14},{8,1},{9,0},... | collective-permute-start | bytes 86024 | tf_op jit(solution)/shard_map/ppermute | solution.py:20
  12.1 1.6 %collective-permute-done.2 = bf16[1,4,4,896]{3,2,1,0:T(4,128)(2,1)S(1)} collective-permute-done((bf16[1,4,4,896]{3,2,1,0:T(4,128)(2,1)S(1)}, bf16[1,4,4,896]{3,2,1,0:T(4,128)(2,1)S(1)}, u32[]{:S(2)}, u32[]{:S(2)}) %collective-permute-start.2) | collective-permute-done | bytes 28704 | tf_op jit(solution)/shard_map/ppermute | solution.py:20
  13.8 1.4 %fusion.1 = f32[32,512]{1,0:T(8,128)S(1)} fusion(bf16[32,896]{1,0:T(8,128)(2,1)S(1)} %reshape_squeeze_reshape_transpose.3, bf16[1,896,512]{2,1,0:T(8,128)(2,1)} %param.10), kind=kOutput, calls=%fused_computation.2 | convolution fusion | flops 29360128 | bytes 1040384 | tf_op jit(solution)/shard_map/dot_general | solution.py:91
  15.2 0.0 copy-done.1
  15.2 0.3 fusion.3
  15.5 0.0 copy-start.2
  15.5 1.9 %collective-permute-start.3 = (bf16[32,1024]{1,0:T(8,128)(2,1)S(1)}, bf16[32,1024]{1,0:T(8,128)(2,1)S(1)}, u32[]{:S(2)}, u32[]{:S(2)}) collective-permute-start(bf16[32,1024]{1,0:T(8,128)(2,1)S(1)} %fusion.6), channel_id=1, source_target_pairs={{0,2},{1,3},{2,0},{3,1},{4,6},{5,7},{6,4},{7,5},{8,10},{9,11},{10,... | collective-permute-start | bytes 196616 | tf_op jit(solution)/shard_map/ppermute | solution.py:20
  17.4 2.5 %collective-permute-done.3 = bf16[32,1024]{1,0:T(8,128)(2,1)S(1)} collective-permute-done((bf16[32,1024]{1,0:T(8,128)(2,1)S(1)}, bf16[32,1024]{1,0:T(8,128)(2,1)S(1)}, u32[]{:S(2)}, u32[]{:S(2)}) %collective-permute-start.3) | collective-permute-done | bytes 65568 | tf_op jit(solution)/shard_map/ppermute | solution.py:20
  20.0 1.9 %collective-permute-start.4 = (bf16[32,1024]{1,0:T(8,128)(2,1)S(1)}, bf16[32,1024]{1,0:T(8,128)(2,1)S(1)}, u32[]{:S(2)}, u32[]{:S(2)}) collective-permute-start(bf16[32,1024]{1,0:T(8,128)(2,1)S(1)} %fusion.7), channel_id=1, source_target_pairs={{0,4},{1,5},{2,6},{3,7},{4,0},{5,1},{6,2},{7,3},{8,12},{9,13},{10,... | collective-permute-start | bytes 196616 | tf_op jit(solution)/shard_map/ppermute | solution.py:20
  21.9 2.4 %collective-permute-done.4 = bf16[32,1024]{1,0:T(8,128)(2,1)S(1)} collective-permute-done((bf16[32,1024]{1,0:T(8,128)(2,1)S(1)}, bf16[32,1024]{1,0:T(8,128)(2,1)S(1)}, u32[]{:S(2)}, u32[]{:S(2)}) %collective-permute-start.4) | collective-permute-done | bytes 65568 | tf_op jit(solution)/shard_map/ppermute | solution.py:20
  24.3 0.2 convolution_convert_fusion
  24.6 0.7 %broadcast_in_dim.25 = bf16[8,2,4,896]{3,2,1,0:T(4,128)(2,1)} broadcast(bf16[8,4,896]{2,1,0:T(4,128)(2,1)S(1)} %broadcast_in_dim.24), dimensions={0,2,3} | broadcast | bytes 172032 | tf_op jit(solution)/shard_map/broadcast_in_dim | solution.py:102
  25.3 6.9 %all-to-all-start = ((bf16[16,4,896]{2,1,0:T(4,128)(2,1)}), bf16[16,4,896]{2,1,0:T(4,128)(2,1)S(1)}, u32[]{:S(2)}, u32[]{:S(2)}) async-start(bf16[16,4,896]{2,1,0:T(4,128)(2,1)} %bitcast.22), calls=%async_computation | async-start | bytes 229376 | tf_op jit(solution)/shard_map/all_to_all | solution.py:103
  32.2 0.0 copy-start.3
  32.3 0.7 %copy-done.3 = s32[4,2]{0,1:T(2,128)S(1)} copy-done((s32[4,2]{0,1:T(2,128)S(1)}, s32[4,2]{0,1:T(2,128)}, u32[]{:S(2)}) %copy-start.3) | copy-done | bytes 56
  32.9 7.0 %all-to-all-done = bf16[16,4,896]{2,1,0:T(4,128)(2,1)S(1)} async-done(((bf16[16,4,896]{2,1,0:T(4,128)(2,1)}), bf16[16,4,896]{2,1,0:T(4,128)(2,1)S(1)}, u32[]{:S(2)}, u32[]{:S(2)}) %all-to-all-start) | async-done | bytes 114720 | tf_op jit(solution)/shard_map/all_to_all | solution.py:103
  39.9 0.7 %fusion.5 = bf16[4,4,896]{2,1,0:T(4,128)(2,1)} fusion(bf16[2,4,2,4,896]{4,3,2,1,0:T(4,128)(2,1)S(1)} %bitcast.58, f32[2,4]{1,0:T(2,128)S(1)} %bitcast.63), kind=kLoop, calls=%fused_computation.7 | loop fusion | flops 157696 | bytes 143392 | tf_op jit(solution)/shard_map/reduce_sum | solution.py:118
  (17 shorter events, 0.3 us)
Async XLA Ops:
  0.0 24.3 %copy-start = (bf16[1,512,896]{2,1,0:T(8,128)(2,1)S(1)}, bf16[1,512,896]{2,1,0:T(8,128)(2,1)}, u32[]{:S(2)}) copy-start(bf16[1,512,896]{2,1,0:T(8,128)(2,1)} %param.11) | copy-start | bytes 2752516
  0.0 15.2 %copy-start.1 = (bf16[1,896,512]{2,1,0:T(8,128)(2,1)S(1)}, bf16[1,896,512]{2,1,0:T(8,128)(2,1)}, u32[]{:S(2)}) copy-start(bf16[1,896,512]{2,1,0:T(8,128)(2,1)} %param.9) | copy-start | bytes 2752516
  0.9 3.9 %collective-permute-start = (bf16[2,1,4,896]{3,2,0,1:T(4,128)(2,1)S(1)}, bf16[2,1,4,896]{3,2,0,1:T(4,128)(2,1)S(1)}, u32[]{:S(2)}, u32[]{:S(2)}) collective-permute-start(bf16[2,1,4,896]{3,2,0,1:T(4,128)(2,1)S(1)} %select_bitcast_fusion.3), channel_id=1, source_target_pairs={{0,3},{1,2},{2,1},{3,0},{4,7},{5,6},{6,5},{7,4},{8,11},{9,10},{10,... | collective-permute-start | bytes 43016 | tf_op jit(solution)/shard_map/ppermute | solution.py:20
  5.6 3.7 %collective-permute-start.1 = (bf16[1,2,4,896]{3,2,1,0:T(4,128)(2,1)S(1)}, bf16[1,2,4,896]{3,2,1,0:T(4,128)(2,1)S(1)}, u32[]{:S(2)}, u32[]{:S(2)}) collective-permute-start(bf16[1,2,4,896]{3,2,1,0:T(4,128)(2,1)S(1)} %select_bitcast_fusion.2), channel_id=1, source_target_pairs={{0,5},{1,4},{2,7},{3,6},{4,1},{5,0},{6,3},{7,2},{8,13},{9,12},{10,... | collective-permute-start | bytes 43016 | tf_op jit(solution)/shard_map/ppermute | solution.py:20
  9.3 4.4 %collective-permute-start.2 = (bf16[1,4,4,896]{3,2,1,0:T(4,128)(2,1)S(1)}, bf16[1,4,4,896]{3,2,1,0:T(4,128)(2,1)S(1)}, u32[]{:S(2)}, u32[]{:S(2)}) collective-permute-start(bf16[1,4,4,896]{3,2,1,0:T(4,128)(2,1)S(1)} %bitcast.59), channel_id=1, source_target_pairs={{0,9},{1,8},{2,11},{3,10},{4,13},{5,12},{6,15},{7,14},{8,1},{9,0},... | collective-permute-start | bytes 86024 | tf_op jit(solution)/shard_map/ppermute | solution.py:20
  15.5 6.4 %copy-start.2 = (f32[4,2]{0,1:T(2,128)S(1)}, f32[4,2]{0,1:T(2,128)}, u32[]{:S(2)}) copy-start(f32[4,2]{0,1:T(2,128)} %param.8) | copy-start | bytes 100
  15.5 4.5 %collective-permute-start.3 = (bf16[32,1024]{1,0:T(8,128)(2,1)S(1)}, bf16[32,1024]{1,0:T(8,128)(2,1)S(1)}, u32[]{:S(2)}, u32[]{:S(2)}) collective-permute-start(bf16[32,1024]{1,0:T(8,128)(2,1)S(1)} %fusion.6), channel_id=1, source_target_pairs={{0,2},{1,3},{2,0},{3,1},{4,6},{5,7},{6,4},{7,5},{8,10},{9,11},{10,... | collective-permute-start | bytes 196616 | tf_op jit(solution)/shard_map/ppermute | solution.py:20
  20.0 4.3 %collective-permute-start.4 = (bf16[32,1024]{1,0:T(8,128)(2,1)S(1)}, bf16[32,1024]{1,0:T(8,128)(2,1)S(1)}, u32[]{:S(2)}, u32[]{:S(2)}) collective-permute-start(bf16[32,1024]{1,0:T(8,128)(2,1)S(1)} %fusion.7), channel_id=1, source_target_pairs={{0,4},{1,5},{2,6},{3,7},{4,0},{5,1},{6,2},{7,3},{8,12},{9,13},{10,... | collective-permute-start | bytes 196616 | tf_op jit(solution)/shard_map/ppermute | solution.py:20
  25.3 14.6 %all-to-all-start = ((bf16[16,4,896]{2,1,0:T(4,128)(2,1)}), bf16[16,4,896]{2,1,0:T(4,128)(2,1)S(1)}, u32[]{:S(2)}, u32[]{:S(2)}) async-start(bf16[16,4,896]{2,1,0:T(4,128)(2,1)} %bitcast.22), calls=%async_computation | async-start | bytes 229376 | tf_op jit(solution)/shard_map/all_to_all | solution.py:103
  32.2 0.7 %copy-start.3 = (s32[4,2]{0,1:T(2,128)S(1)}, s32[4,2]{0,1:T(2,128)}, u32[]{:S(2)}) copy-start(s32[4,2]{0,1:T(2,128)} %param.7) | copy-start | bytes 100

commit v2 on v1

--- a/solution.py
+++ b/solution.py
@@ -41,6 +41,7 @@
             halves //= 2
         else:
             own = sent = block
+        own, sent = lax.optimization_barrier((own, sent))
         other = swapped(sent, mask, True)
         both = ordered(own, other, bit)
         block = jnp.moveaxis(both, 0, 1).reshape(own.shape[0], 2 * own.shape[1], tok_rows, quarter)
@@ -87,19 +88,28 @@
         outgoing = outgoing.reshape(peer_count, capacity, quarter)
         arrived = lax.all_to_all(outgoing, "ep", split_axis=0, concat_axis=0, tiled=True)
     row_block = arrived.reshape(peer_count * capacity, quarter)
-    gate_part = jnp.dot(row_block, w_gate[0], preferred_element_type=jnp.float32)
-    up_part = jnp.dot(row_block, w_up[0], preferred_element_type=jnp.float32)
-    parts = jnp.concatenate([gate_part, up_part], axis=1)
+    weights_in = jnp.concatenate([w_gate[0], w_up[0]], axis=1)
+    parts = jnp.dot(row_block, weights_in, preferred_element_type=jnp.float32)
     for bit_index in range(group_bits):
         other = swapped(parts.astype(jnp.bfloat16), 2**bit_index, False)
         parts = parts + other.astype(jnp.float32)
-    hidden_units = gate_part.shape[1]
+    hidden_units = w_gate.shape[2]
     inner_rows = (jax.nn.silu(parts[:, :hidden_units]) * parts[:, hidden_units:]).astype(
         jnp.bfloat16
     )
     partial_out = jnp.dot(inner_rows, w_down[0], preferred_element_type=jnp.float32)
+    routing = (gate_scores / jnp.sum(gate_scores, axis=1, keepdims=True) * route_scale).astype(
+        jnp.bfloat16
+    )
+    routing = routing.astype(jnp.float32)
+    if every_expert:
+        named = expert_ids[:, :, None] == jnp.arange(experts, dtype=jnp.int32)
+        share = jnp.sum(jnp.where(named, routing[:, :, None], 0.0), axis=1)
+    else:
+        share = jnp.einsum("tk,tke,tkc->tec", routing, expert_hot, slot_hot).astype(jnp.bfloat16)
     partial_out = partial_out.astype(jnp.bfloat16).reshape(peer_count, 1, capacity, quarter)
     leaving = jnp.broadcast_to(partial_out, (peer_count, core_count, capacity, quarter))
+    leaving, share = lax.optimization_barrier((leaving, share))
     returned = lax.all_to_all(
         leaving.reshape(peer_count * core_count, capacity, quarter),
         ("ep", "tp"),
@@ -107,22 +117,12 @@
         concat_axis=0,
         tiled=True,
     ).reshape(experts, GROUP, core_count, capacity, quarter)
-    routing = (gate_scores / jnp.sum(gate_scores, axis=1, keepdims=True) * route_scale).astype(
-        jnp.bfloat16
-    )
-    routing = routing.astype(jnp.float32)
     if every_expert:
-        named = expert_ids[:, :, None] == jnp.arange(experts, dtype=jnp.int32)
-        share = jnp.sum(jnp.where(named, routing[:, :, None], 0.0), axis=1)
         weighted = returned.astype(jnp.float32) * share.T[:, None, None, :, None]
         combined = jnp.sum(weighted, axis=(0, 2)).transpose(1, 0, 2)
     else:
-        combining = jnp.einsum("tk,tke,tkc->tec", routing, expert_hot, slot_hot)
         combined = jnp.einsum(
-            "tec,egpcd->tgd",
-            combining.astype(jnp.bfloat16),
-            returned,
-            preferred_element_type=jnp.float32,
+            "tec,egpcd->tgd", share, returned, preferred_element_type=jnp.float32
         )
     return combined.reshape(tok_rows, width_all).astype(jnp.bfloat16)
 

time: 41 us -> 39.4 us (0.961)
  blocking collectives: 0 us -> 14.4 us
  waiting for transfers between devices: 16.3 us -> 8.65 us
  starting transfers between devices: 18.2 us -> 11.3 us
  local copies, waits for them, and re-layouts: 1.41 us -> 0.11 us
    all_to_all x0 -> x1, blocking collectives: none -> 14.4 us  [local(): lax.all_to_all(leaving.reshape(peer_count * core_count, capacity, quarter...]
    all_to_all x1 -> x0, waiting for transfers between devices: 6.98 us -> none  [local(): lax.all_to_all(leaving.reshape(peer_count * core_count, capacity, quarter...]
    all_to_all x1 -> x0, starting transfers between devices: 6.93 us -> none  [local(): lax.all_to_all(leaving.reshape(peer_count * core_count, capacity, quarter...]
    another operation x5, other arithmetic: 0.86 us -> 0.13 us  [ordered(): return jnp.stack([jnp.where(bit, other, own), jnp.where(bit, own, other)])]
    ppermute x5, waiting for transfers between devices: 9.35 us -> 8.65 us  [swapped(): return lax.ppermute(value, ('ep', 'tp'), pairs)]
    reduce_sum x1, other arithmetic: 0.02 us -> 0.7 us  [local(): jnp.sum(gate_scores, axis=1, keepdims=True)]
    unnamed x8 -> x6, local copies, waits for them, and re-layouts: 0.68 us -> 0.02 us
    broadcast_in_dim x2, local copies, waits for them, and re-layouts: 0.71 us -> 0.07 us  [local(): jnp.broadcast_to(partial_out, (peer_count, core_count, capacity, quarter))]
  transfers between devices with their start and end apart: 6 -> 5, of which waited for: 6 -> 5; matrix products, arithmetic and copies ran while one was open for 0% -> 2% of each run, Pallas kernels for 0% -> 0%
where the time goes in v2:
time: 39.4 us; the launch traced here: 39.2 us
  blocking collectives  14.4 us (37%)
  starting transfers between devices  11.3 us (29%)
  waiting for transfers between devices  8.65 us (22%)
  other arithmetic  2.5 us (6%)
  matrix products  2.13 us (5%)
    all_to_all x1, blocking collectives, local(): lax.all_to_all(leaving.reshape(peer_count * core_count, capacity, quarter...  14.4 us
    ppermute x5, starting transfers between devices, swapped(): return lax.ppermute(value, ('ep', 'tp'), pairs)  11.3 us
    ppermute x5, waiting for transfers between devices, swapped(): return lax.ppermute(value, ('ep', 'tp'), pairs)  8.65 us
    dot_general x1, matrix products, local(): parts = jnp.dot(row_block, weights_in, preferred_element_type=jnp.float32)  1.88 us
    select_n x2, other arithmetic, spread_tokens(): sent = jnp.where(bit, parts[:, 0], parts[:, 1])  0.85 us
  transfers between devices with their start and end apart: 5, of which 5 were waited for; matrix products, arithmetic and copies ran while one was open for 2% of the time, Pallas kernels for 0%

profile of v2, /device:TPU:0, one launch (start us, length us, event | category | flops | bytes accessed | tf_op | source)
XLA Modules:
  0.0 39.2 jit_solution(11701725034051375567)
XLA Ops:
  0.0 0.0 copy-start
  0.0 0.8 %select_bitcast_fusion.8 = (bf16[2,1,4,896]{3,2,0,1:T(4,128)(2,1)S(1)}, bf16[2,1,4,896]{3,2,0,1:T(4,128)(2,1)S(1)}) fusion(pred[]{:T(512)S(6)} %gt.11, bf16[2,2,1,4,896]{4,3,1,0,2:T(4,128)(2,1)} %bitcast.47), kind=kLoop, calls=%fused_computation.25 | loop fusion | flops 14336 | bytes 57345 | tf_op jit(solution)/shard_map/jit(_where)/select_n | solution.py:40
  0.8 2.4 %collective-permute-start = (bf16[2,1,4,896]{3,2,0,1:T(4,128)(2,1)S(1)}, bf16[2,1,4,896]{3,2,0,1:T(4,128)(2,1)S(1)}, u32[]{:S(2)}, u32[]{:S(2)}) collective-permute-start(bf16[2,1,4,896]{3,2,0,1:T(4,128)(2,1)S(1)} %get-tuple-element.13), channel_id=1, source_target_pairs={{0,3},{1,2},{2,1},{3,0},{4,7},{5,6},{6,5},{7,4},{8,11},{9,10},{10,... | collective-permute-start | bytes 43016 | tf_op jit(solution)/shard_map/ppermute | solution.py:20
  3.3 1.4 %collective-permute-done = bf16[2,1,4,896]{3,2,0,1:T(4,128)(2,1)S(1)} collective-permute-done((bf16[2,1,4,896]{3,2,0,1:T(4,128)(2,1)S(1)}, bf16[2,1,4,896]{3,2,0,1:T(4,128)(2,1)S(1)}, u32[]{:S(2)}, u32[]{:S(2)}) %collective-permute-start) | collective-permute-done | bytes 14368 | tf_op jit(solution)/shard_map/ppermute | solution.py:20
  4.8 2.3 %collective-permute-start.1 = (bf16[1,2,4,896]{3,2,1,0:T(4,128)(2,1)S(1)}, bf16[1,2,4,896]{3,2,1,0:T(4,128)(2,1)S(1)}, u32[]{:S(2)}, u32[]{:S(2)}) collective-permute-start(bf16[1,2,4,896]{3,2,1,0:T(4,128)(2,1)S(1)} %get-tuple-element.15), channel_id=1, source_target_pairs={{0,5},{1,4},{2,7},{3,6},{4,1},{5,0},{6,3},{7,2},{8,13},{9,12},{10,... | collective-permute-start | bytes 43016 | tf_op jit(solution)/shard_map/ppermute | solution.py:20
  7.0 1.4 %collective-permute-done.1 = bf16[1,2,4,896]{3,2,1,0:T(4,128)(2,1)S(1)} collective-permute-done((bf16[1,2,4,896]{3,2,1,0:T(4,128)(2,1)S(1)}, bf16[1,2,4,896]{3,2,1,0:T(4,128)(2,1)S(1)}, u32[]{:S(2)}, u32[]{:S(2)}) %collective-permute-start.1) | collective-permute-done | bytes 14368 | tf_op jit(solution)/shard_map/ppermute | solution.py:20
  8.5 2.8 %collective-permute-start.2 = (bf16[1,4,4,896]{3,2,1,0:T(4,128)(2,1)S(1)}, bf16[1,4,4,896]{3,2,1,0:T(4,128)(2,1)S(1)}, u32[]{:S(2)}, u32[]{:S(2)}) collective-permute-start(bf16[1,4,4,896]{3,2,1,0:T(4,128)(2,1)S(1)} %bitcast.45), channel_id=1, source_target_pairs={{0,9},{1,8},{2,11},{3,10},{4,13},{5,12},{6,15},{7,14},{8,1},{9,0},... | collective-permute-start | bytes 86024 | tf_op jit(solution)/shard_map/ppermute | solution.py:20
  11.3 0.7 %reduce_sum.27 = f32[4]{0:T(128)S(1)} reduce(f32[4,2]{0,1:T(2,128)} %param.8, f32[]{:T(128)} %constant.19.clone.1), dimensions={1}, to_apply=%region_0.1 | reduce | flops 4 | bytes 52 | tf_op jit(solution)/shard_map/reduce_sum | solution.py:101
  12.0 0.9 %collective-permute-done.2 = bf16[1,4,4,896]{3,2,1,0:T(4,128)(2,1)S(1)} collective-permute-done((bf16[1,4,4,896]{3,2,1,0:T(4,128)(2,1)S(1)}, bf16[1,4,4,896]{3,2,1,0:T(4,128)(2,1)S(1)}, u32[]{:S(2)}, u32[]{:S(2)}) %collective-permute-start.2) | collective-permute-done | bytes 28704 | tf_op jit(solution)/shard_map/ppermute | solution.py:20
  13.0 0.0 copy-start.1
  13.0 0.0 copy-start.2
  13.0 1.9 %fusion.14 = (bf16[32,1024]{1,0:T(8,128)(2,1)S(1)}, f32[32,1024]{1,0:T(8,128)S(1)}) fusion(bf16[32,896]{1,0:T(8,128)(2,1)S(1)} %reshape_squeeze_reshape_transpose.3, bf16[896,512]{1,0:T(8,128)(2,1)} %bitcast.49, bf16[896,512]{1,0:T(8,128)(2,1)} %bitcast.50), kind=kOutput, calls=%fused_computation.33 | convolution fusion | flops 62423040 | bytes 2088960 | tf_op jit(solution)/shard_map/dot_general | solution.py:92
  14.9 1.9 %collective-permute-start.3 = (bf16[32,1024]{1,0:T(8,128)(2,1)S(1)}, bf16[32,1024]{1,0:T(8,128)(2,1)S(1)}, u32[]{:S(2)}, u32[]{:S(2)}) collective-permute-start(bf16[32,1024]{1,0:T(8,128)(2,1)S(1)} %get-tuple-element.31), channel_id=1, source_target_pairs={{0,2},{1,3},{2,0},{3,1},{4,6},{5,7},{6,4},{7,5},{8,10},{9,11},{10,... | collective-permute-start | bytes 196616 | tf_op jit(solution)/shard_map/ppermute | solution.py:20
  16.8 0.0 copy-done.1
  16.8 2.5 %collective-permute-done.3 = bf16[32,1024]{1,0:T(8,128)(2,1)S(1)} collective-permute-done((bf16[32,1024]{1,0:T(8,128)(2,1)S(1)}, bf16[32,1024]{1,0:T(8,128)(2,1)S(1)}, u32[]{:S(2)}, u32[]{:S(2)}) %collective-permute-start.3) | collective-permute-done | bytes 65568 | tf_op jit(solution)/shard_map/ppermute | solution.py:20
  19.3 1.9 %collective-permute-start.4 = (bf16[32,1024]{1,0:T(8,128)(2,1)S(1)}, bf16[32,1024]{1,0:T(8,128)(2,1)S(1)}, u32[]{:S(2)}, u32[]{:S(2)}) collective-permute-start(bf16[32,1024]{1,0:T(8,128)(2,1)S(1)} %fusion.6), channel_id=1, source_target_pairs={{0,4},{1,5},{2,6},{3,7},{4,0},{5,1},{6,2},{7,3},{8,12},{9,13},{10,... | collective-permute-start | bytes 196616 | tf_op jit(solution)/shard_map/ppermute | solution.py:20
  21.2 0.0 copy-done.2
  21.2 2.4 %collective-permute-done.4 = bf16[32,1024]{1,0:T(8,128)(2,1)S(1)} collective-permute-done((bf16[32,1024]{1,0:T(8,128)(2,1)S(1)}, bf16[32,1024]{1,0:T(8,128)(2,1)S(1)}, u32[]{:S(2)}, u32[]{:S(2)}) %collective-permute-start.4) | collective-permute-done | bytes 65568 | tf_op jit(solution)/shard_map/ppermute | solution.py:20
  23.7 0.0 copy-done
  23.7 0.2 convolution_convert_fusion
  24.0 14.4 %all_to_all.5 = bf16[16,4,896]{2,1,0:T(4,128)(2,1)S(1)} all-to-all(bf16[16,4,896]{2,1,0:T(4,128)(2,1)S(1)} %bitcast.44), channel_id=1, replica_groups=mesh['groups'=2,'ep'=8,'tp'=2] {'ep','tp'}, dimensions={0} | all-to-all | bytes 229376 | tf_op jit(solution)/shard_map/all_to_all | solution.py:113
  38.4 0.7 %fusion.5 = bf16[4,4,896]{2,1,0:T(4,128)(2,1)} fusion(bf16[2,4,2,4,896]{4,3,2,1,0:T(4,128)(2,1)S(1)} %bitcast.43, f32[2,4]{1,0:T(2,128)S(1)} %bitcast.48), kind=kLoop, calls=%fused_computation.7 | loop fusion | flops 157696 | bytes 143392 | tf_op jit(solution)/shard_map/reduce_sum | solution.py:122
  (14 shorter events, 0.3 us)
Async XLA Ops:
  0.0 23.7 %copy-start = (bf16[1,512,896]{2,1,0:T(8,128)(2,1)S(1)}, bf16[1,512,896]{2,1,0:T(8,128)(2,1)}, u32[]{:S(2)}) copy-start(bf16[1,512,896]{2,1,0:T(8,128)(2,1)} %param.11) | copy-start | bytes 2752516
  0.8 3.9 %collective-permute-start = (bf16[2,1,4,896]{3,2,0,1:T(4,128)(2,1)S(1)}, bf16[2,1,4,896]{3,2,0,1:T(4,128)(2,1)S(1)}, u32[]{:S(2)}, u32[]{:S(2)}) collective-permute-start(bf16[2,1,4,896]{3,2,0,1:T(4,128)(2,1)S(1)} %get-tuple-element.13), channel_id=1, source_target_pairs={{0,3},{1,2},{2,1},{3,0},{4,7},{5,6},{6,5},{7,4},{8,11},{9,10},{10,... | collective-permute-start | bytes 43016 | tf_op jit(solution)/shard_map/ppermute | solution.py:20
  4.8 3.7 %collective-permute-start.1 = (bf16[1,2,4,896]{3,2,1,0:T(4,128)(2,1)S(1)}, bf16[1,2,4,896]{3,2,1,0:T(4,128)(2,1)S(1)}, u32[]{:S(2)}, u32[]{:S(2)}) collective-permute-start(bf16[1,2,4,896]{3,2,1,0:T(4,128)(2,1)S(1)} %get-tuple-element.15), channel_id=1, source_target_pairs={{0,5},{1,4},{2,7},{3,6},{4,1},{5,0},{6,3},{7,2},{8,13},{9,12},{10,... | collective-permute-start | bytes 43016 | tf_op jit(solution)/shard_map/ppermute | solution.py:20
  8.5 4.4 %collective-permute-start.2 = (bf16[1,4,4,896]{3,2,1,0:T(4,128)(2,1)S(1)}, bf16[1,4,4,896]{3,2,1,0:T(4,128)(2,1)S(1)}, u32[]{:S(2)}, u32[]{:S(2)}) collective-permute-start(bf16[1,4,4,896]{3,2,1,0:T(4,128)(2,1)S(1)} %bitcast.45), channel_id=1, source_target_pairs={{0,9},{1,8},{2,11},{3,10},{4,13},{5,12},{6,15},{7,14},{8,1},{9,0},... | collective-permute-start | bytes 86024 | tf_op jit(solution)/shard_map/ppermute | solution.py:20
  13.0 3.8 %copy-start.1 = (f32[4,2]{0,1:T(2,128)S(1)}, f32[4,2]{0,1:T(2,128)}, u32[]{:S(2)}) copy-start(f32[4,2]{0,1:T(2,128)} %param.8) | copy-start | bytes 100
  13.0 8.2 %copy-start.2 = (s32[4,2]{0,1:T(2,128)S(1)}, s32[4,2]{0,1:T(2,128)}, u32[]{:S(2)}) copy-start(s32[4,2]{0,1:T(2,128)} %param.7) | copy-start | bytes 100
  14.9 4.4 %collective-permute-start.3 = (bf16[32,1024]{1,0:T(8,128)(2,1)S(1)}, bf16[32,1024]{1,0:T(8,128)(2,1)S(1)}, u32[]{:S(2)}, u32[]{:S(2)}) collective-permute-start(bf16[32,1024]{1,0:T(8,128)(2,1)S(1)} %get-tuple-element.31), channel_id=1, source_target_pairs={{0,2},{1,3},{2,0},{3,1},{4,6},{5,7},{6,4},{7,5},{8,10},{9,11},{10,... | collective-permute-start | bytes 196616 | tf_op jit(solution)/shard_map/ppermute | solution.py:20
  19.3 4.3 %collective-permute-start.4 = (bf16[32,1024]{1,0:T(8,128)(2,1)S(1)}, bf16[32,1024]{1,0:T(8,128)(2,1)S(1)}, u32[]{:S(2)}, u32[]{:S(2)}) collective-permute-start(bf16[32,1024]{1,0:T(8,128)(2,1)S(1)} %fusion.6), channel_id=1, source_target_pairs={{0,4},{1,5},{2,6},{3,7},{4,0},{5,1},{6,2},{7,3},{8,12},{9,13},{10,... | collective-permute-start | bytes 196616 | tf_op jit(solution)/shard_map/ppermute | solution.py:20

commit v3 on v2

--- a/solution.py
+++ b/solution.py
@@ -29,9 +29,17 @@
     peers = lax.axis_size("ep")
     rank = lax.axis_index("ep")
     quarter = width_all // GROUP
-    halves = GROUP
-    block = hidden.reshape(tok_rows, GROUP, quarter).transpose(1, 0, 2)[:, None]
-    mask = 1
+    other = swapped(hidden, 1, True)
+    bit = (rank & 1) > 0
+
+    def kept(rows):
+        quarters = rows.reshape(tok_rows, GROUP // 2, 2, quarter)
+        return jnp.where(bit, quarters[:, :, 1], quarters[:, :, 0]).transpose(1, 0, 2)
+
+    own = lax.optimization_barrier(kept(hidden))
+    block = jnp.moveaxis(ordered(own, kept(other), bit), 0, 1)
+    halves = GROUP // 2
+    mask = 2
     while mask < peers:
         bit = (rank & mask) > 0
         if halves > 1:
@@ -41,7 +49,6 @@
             halves //= 2
         else:
             own = sent = block
-        own, sent = lax.optimization_barrier((own, sent))
         other = swapped(sent, mask, True)
         both = ordered(own, other, bit)
         block = jnp.moveaxis(both, 0, 1).reshape(own.shape[0], 2 * own.shape[1], tok_rows, quarter)
@@ -88,7 +95,7 @@
         outgoing = outgoing.reshape(peer_count, capacity, quarter)
         arrived = lax.all_to_all(outgoing, "ep", split_axis=0, concat_axis=0, tiled=True)
     row_block = arrived.reshape(peer_count * capacity, quarter)
-    weights_in = jnp.concatenate([w_gate[0], w_up[0]], axis=1)
+    weights_in = lax.optimization_barrier(jnp.concatenate([w_gate[0], w_up[0]], axis=1))
     parts = jnp.dot(row_block, weights_in, preferred_element_type=jnp.float32)
     for bit_index in range(group_bits):
         other = swapped(parts.astype(jnp.bfloat16), 2**bit_index, False)

time: 39.4 us -> 37.7 us (0.957)
  matrix products: 2.13 us -> 0.67 us
  waiting for transfers between devices: 8.65 us -> 7.8 us
  local copies, waits for them, and re-layouts: 0.11 us -> 0.94 us
  starting transfers between devices: 11.3 us -> 10.8 us
    concatenate x0 -> x1, other arithmetic: none -> 1.69 us  [local(): jnp.concatenate([w_gate[0], w_up[0]], axis=1)]
    dot_general x1, matrix products: 1.88 us -> 0.42 us  [local(): parts = jnp.dot(row_block, weights_in, preferred_element_type=jnp.float32)]
    ppermute x5, waiting for transfers between devices: 8.65 us -> 7.8 us  [swapped(): return lax.ppermute(value, ('ep', 'tp'), pairs)]
    reshape x0 -> x2, local copies, waits for them, and re-layouts: none -> 0.81 us  [kept(): quarters = rows.reshape(tok_rows, GROUP // 2, 2, quarter)]
    reduce_sum x1, other arithmetic: 0.7 us -> 0.02 us  [local(): jnp.sum(gate_scores, axis=1, keepdims=True)]
    select_n x2 -> x3, other arithmetic: 0.85 us -> 0.18 us  [the longest x2 0.11 us: kept(): jnp.where(bit, quarters[:, :, 1], quarters[:, :, 0]).transpose(1, 0, 2)]
    ppermute x5, starting transfers between devices: 11.3 us -> 10.8 us  [swapped(): return lax.ppermute(value, ('ep', 'tp'), pairs)]
  transfers between devices with their start and end apart: 5 -> 5, of which waited for: 5 -> 4; matrix products, arithmetic and copies ran while one was open for 2% -> 7% of each run, Pallas kernels for 0% -> 0%
where the time goes in v3:
time: 37.7 us; the launch traced here: 37.5 us
  blocking collectives  14.2 us (38%)
  starting transfers between devices  10.8 us (29%)
  waiting for transfers between devices  7.8 us (21%)
  other arithmetic  2.89 us (8%)
  local copies, waits for them, and re-layouts  0.94 us (2%)
  matrix products  0.67 us (2%)
    all_to_all x1, blocking collectives, local(): lax.all_to_all(leaving.reshape(peer_count * core_count, capacity, quarter...  14.2 us
    ppermute x5, starting transfers between devices, swapped(): return lax.ppermute(value, ('ep', 'tp'), pairs)  10.8 us
    ppermute x5, waiting for transfers between devices, swapped(): return lax.ppermute(value, ('ep', 'tp'), pairs)  7.8 us
    concatenate x1, other arithmetic, local(): jnp.concatenate([w_gate[0], w_up[0]], axis=1)  1.69 us
    reshape x2, local copies, waits for them, and re-layouts, kept(): quarters = rows.reshape(tok_rows, GROUP // 2, 2, quarter)  0.81 us
  transfers between devices with their start and end apart: 5, of which 4 were waited for; matrix products, arithmetic and copies ran while one was open for 7% of the time, Pallas kernels for 0%

profile of v3, /device:TPU:0, one launch (start us, length us, event | category | flops | bytes accessed | tf_op | source)
XLA Modules:
  0.0 37.5 jit_solution(14106203658368888483)
XLA Ops:
  0.0 0.0 copy-start
  0.0 2.4 %collective-permute-start = (bf16[4,3584]{1,0:T(4,128)(2,1)}, bf16[4,3584]{1,0:T(4,128)(2,1)S(1)}, u32[]{:S(2)}, u32[]{:S(2)}) collective-permute-start(bf16[4,3584]{1,0:T(4,128)(2,1)} %param.6), channel_id=1, source_target_pairs={{0,3},{1,2},{2,1},{3,0},{4,7},{5,6},{6,5},{7,4},{8,11},{9,10},{10,... | collective-permute-start | bytes 86024 | tf_op jit(solution)/shard_map/ppermute | solution.py:20
  2.4 0.8 %reshape.72 = bf16[4,2,2,896]{3,2,1,0:T(2,128)(2,1)S(1)} reshape(bf16[4,3584]{1,0:T(4,128)(2,1)} %param.6) | data formatting | bytes 57344 | tf_op jit(solution)/shard_map/reshape | solution.py:36
  3.2 0.1 broadcast_select_fusion
  3.3 1.0 %collective-permute-done = bf16[4,3584]{1,0:T(4,128)(2,1)S(1)} collective-permute-done((bf16[4,3584]{1,0:T(4,128)(2,1)}, bf16[4,3584]{1,0:T(4,128)(2,1)S(1)}, u32[]{:S(2)}, u32[]{:S(2)}) %collective-permute-start) | collective-permute-done | bytes 28704 | tf_op jit(solution)/shard_map/ppermute | solution.py:20
  4.3 0.1 broadcast_select_fusion.1
  4.5 0.1 broadcast_select_fusion.2
  4.6 2.3 %collective-permute-start.1 = (bf16[1,2,4,896]{3,2,1,0:T(4,128)(2,1)S(1)}, bf16[1,2,4,896]{3,2,1,0:T(4,128)(2,1)S(1)}, u32[]{:S(2)}, u32[]{:S(2)}) collective-permute-start(bf16[1,2,4,896]{3,2,1,0:T(4,128)(2,1)S(1)} %bitcast.58), channel_id=1, source_target_pairs={{0,5},{1,4},{2,7},{3,6},{4,1},{5,0},{6,3},{7,2},{8,13},{9,12},{10,... | collective-permute-start | bytes 43016 | tf_op jit(solution)/shard_map/ppermute | solution.py:20
  6.9 1.4 %collective-permute-done.1 = bf16[1,2,4,896]{3,2,1,0:T(4,128)(2,1)S(1)} collective-permute-done((bf16[1,2,4,896]{3,2,1,0:T(4,128)(2,1)S(1)}, bf16[1,2,4,896]{3,2,1,0:T(4,128)(2,1)S(1)}, u32[]{:S(2)}, u32[]{:S(2)}) %collective-permute-start.1) | collective-permute-done | bytes 14368 | tf_op jit(solution)/shard_map/ppermute | solution.py:20
  8.3 2.8 %collective-permute-start.2 = (bf16[1,4,4,896]{3,2,1,0:T(4,128)(2,1)S(1)}, bf16[1,4,4,896]{3,2,1,0:T(4,128)(2,1)S(1)}, u32[]{:S(2)}, u32[]{:S(2)}) collective-permute-start(bf16[1,4,4,896]{3,2,1,0:T(4,128)(2,1)S(1)} %bitcast.55), channel_id=1, source_target_pairs={{0,9},{1,8},{2,11},{3,10},{4,13},{5,12},{6,15},{7,14},{8,1},{9,0},... | collective-permute-start | bytes 86024 | tf_op jit(solution)/shard_map/ppermute | solution.py:20
  11.1 1.7 %pad_maximum_fusion = bf16[896,1024]{1,0:T(8,128)(2,1)S(1)} fusion(bf16[896,512]{1,0:T(8,128)(2,1)} %bitcast.51, bf16[896,512]{1,0:T(8,128)(2,1)} %bitcast.52), kind=kLoop, calls=%fused_computation | loop fusion | flops 3670016 | bytes 3670016 | tf_op jit(solution)/shard_map/concatenate | solution.py:98
  12.8 0.0 copy-start.2
  12.8 0.0 copy-done.1
  12.9 0.0 collective-permute-done.2
  13.0 0.4 %fusion.13 = (bf16[32,1024]{1,0:T(8,128)(2,1)S(1)}, f32[32,1024]{1,0:T(8,128)S(1)}) fusion(bf16[32,896]{1,0:T(8,128)(2,1)S(1)} %reshape_squeeze_reshape_transpose.3, bf16[896,1024]{1,0:T(8,128)(2,1)S(1)} %pad_maximum_fusion), kind=kOutput, calls=%fused_computation.35 | convolution fusion | flops 58753024 | bytes 2088960 | tf_op jit(solution)/shard_map/dot_general | solution.py:99
  13.4 1.7 %collective-permute-start.3 = (bf16[32,1024]{1,0:T(8,128)(2,1)S(1)}, bf16[32,1024]{1,0:T(8,128)(2,1)S(1)}, u32[]{:S(2)}, u32[]{:S(2)}) collective-permute-start(bf16[32,1024]{1,0:T(8,128)(2,1)S(1)} %get-tuple-element.17), channel_id=1, source_target_pairs={{0,2},{1,3},{2,0},{3,1},{4,6},{5,7},{6,4},{7,5},{8,10},{9,11},{10,... | collective-permute-start | bytes 196616 | tf_op jit(solution)/shard_map/ppermute | solution.py:20
  15.1 2.7 %collective-permute-done.3 = bf16[32,1024]{1,0:T(8,128)(2,1)S(1)} collective-permute-done((bf16[32,1024]{1,0:T(8,128)(2,1)S(1)}, bf16[32,1024]{1,0:T(8,128)(2,1)S(1)}, u32[]{:S(2)}, u32[]{:S(2)}) %collective-permute-start.3) | collective-permute-done | bytes 65568 | tf_op jit(solution)/shard_map/ppermute | solution.py:20
  17.9 1.7 %collective-permute-start.4 = (bf16[32,1024]{1,0:T(8,128)(2,1)S(1)}, bf16[32,1024]{1,0:T(8,128)(2,1)S(1)}, u32[]{:S(2)}, u32[]{:S(2)}) collective-permute-start(bf16[32,1024]{1,0:T(8,128)(2,1)S(1)} %fusion.2), channel_id=1, source_target_pairs={{0,4},{1,5},{2,6},{3,7},{4,0},{5,1},{6,2},{7,3},{8,12},{9,13},{10,... | collective-permute-start | bytes 196616 | tf_op jit(solution)/shard_map/ppermute | solution.py:20
  19.5 0.0 copy-done.2
  19.6 2.6 %collective-permute-done.4 = bf16[32,1024]{1,0:T(8,128)(2,1)S(1)} collective-permute-done((bf16[32,1024]{1,0:T(8,128)(2,1)S(1)}, bf16[32,1024]{1,0:T(8,128)(2,1)S(1)}, u32[]{:S(2)}, u32[]{:S(2)}) %collective-permute-start.4) | collective-permute-done | bytes 65568 | tf_op jit(solution)/shard_map/ppermute | solution.py:20
  22.2 0.0 copy-done
  22.2 0.2 convolution_convert_fusion
  22.6 14.2 %all_to_all.5 = bf16[16,4,896]{2,1,0:T(4,128)(2,1)S(1)} all-to-all(bf16[16,4,896]{2,1,0:T(4,128)(2,1)S(1)} %bitcast.54), channel_id=1, replica_groups=mesh['groups'=2,'ep'=8,'tp'=2] {'ep','tp'}, dimensions={0} | all-to-all | bytes 229376 | tf_op jit(solution)/shard_map/all_to_all | solution.py:120
  36.7 0.7 %fusion.1 = bf16[4,4,896]{2,1,0:T(4,128)(2,1)} fusion(bf16[2,4,2,4,896]{4,3,2,1,0:T(4,128)(2,1)S(1)} %bitcast.53, f32[2,4]{1,0:T(2,128)S(1)} %bitcast.59), kind=kLoop, calls=%fused_computation.4 | loop fusion | flops 157696 | bytes 143392 | tf_op jit(solution)/shard_map/reduce_sum | solution.py:129
  (18 shorter events, 0.4 us)
Async XLA Ops:
  0.0 22.2 %copy-start = (bf16[1,512,896]{2,1,0:T(8,128)(2,1)S(1)}, bf16[1,512,896]{2,1,0:T(8,128)(2,1)}, u32[]{:S(2)}) copy-start(bf16[1,512,896]{2,1,0:T(8,128)(2,1)} %param.11) | copy-start | bytes 2752516
  0.0 4.3 %collective-permute-start = (bf16[4,3584]{1,0:T(4,128)(2,1)}, bf16[4,3584]{1,0:T(4,128)(2,1)S(1)}, u32[]{:S(2)}, u32[]{:S(2)}) collective-permute-start(bf16[4,3584]{1,0:T(4,128)(2,1)} %param.6), channel_id=1, source_target_pairs={{0,3},{1,2},{2,1},{3,0},{4,7},{5,6},{6,5},{7,4},{8,11},{9,10},{10,... | collective-permute-start | bytes 86024 | tf_op jit(solution)/shard_map/ppermute | solution.py:20
  4.6 3.7 %collective-permute-start.1 = (bf16[1,2,4,896]{3,2,1,0:T(4,128)(2,1)S(1)}, bf16[1,2,4,896]{3,2,1,0:T(4,128)(2,1)S(1)}, u32[]{:S(2)}, u32[]{:S(2)}) collective-permute-start(bf16[1,2,4,896]{3,2,1,0:T(4,128)(2,1)S(1)} %bitcast.58), channel_id=1, source_target_pairs={{0,5},{1,4},{2,7},{3,6},{4,1},{5,0},{6,3},{7,2},{8,13},{9,12},{10,... | collective-permute-start | bytes 43016 | tf_op jit(solution)/shard_map/ppermute | solution.py:20
  8.3 4.5 %collective-permute-start.2 = (bf16[1,4,4,896]{3,2,1,0:T(4,128)(2,1)S(1)}, bf16[1,4,4,896]{3,2,1,0:T(4,128)(2,1)S(1)}, u32[]{:S(2)}, u32[]{:S(2)}) collective-permute-start(bf16[1,4,4,896]{3,2,1,0:T(4,128)(2,1)S(1)} %bitcast.55), channel_id=1, source_target_pairs={{0,9},{1,8},{2,11},{3,10},{4,13},{5,12},{6,15},{7,14},{8,1},{9,0},... | collective-permute-start | bytes 86024 | tf_op jit(solution)/shard_map/ppermute | solution.py:20
  11.1 1.7 %copy-start.1 = (f32[4,2]{0,1:T(2,128)S(1)}, f32[4,2]{0,1:T(2,128)}, u32[]{:S(2)}) copy-start(f32[4,2]{0,1:T(2,128)} %param.8) | copy-start | bytes 100
  12.8 6.7 %copy-start.2 = (s32[4,2]{0,1:T(2,128)S(1)}, s32[4,2]{0,1:T(2,128)}, u32[]{:S(2)}) copy-start(s32[4,2]{0,1:T(2,128)} %param.7) | copy-start | bytes 100
  13.4 4.4 %collective-permute-start.3 = (bf16[32,1024]{1,0:T(8,128)(2,1)S(1)}, bf16[32,1024]{1,0:T(8,128)(2,1)S(1)}, u32[]{:S(2)}, u32[]{:S(2)}) collective-permute-start(bf16[32,1024]{1,0:T(8,128)(2,1)S(1)} %get-tuple-element.17), channel_id=1, source_target_pairs={{0,2},{1,3},{2,0},{3,1},{4,6},{5,7},{6,4},{7,5},{8,10},{9,11},{10,... | collective-permute-start | bytes 196616 | tf_op jit(solution)/shard_map/ppermute | solution.py:20
  17.9 4.3 %collective-permute-start.4 = (bf16[32,1024]{1,0:T(8,128)(2,1)S(1)}, bf16[32,1024]{1,0:T(8,128)(2,1)S(1)}, u32[]{:S(2)}, u32[]{:S(2)}) collective-permute-start(bf16[32,1024]{1,0:T(8,128)(2,1)S(1)} %fusion.2), channel_id=1, source_target_pairs={{0,4},{1,5},{2,6},{3,7},{4,0},{5,1},{6,2},{7,3},{8,12},{9,13},{10,... | collective-permute-start | bytes 196616 | tf_op jit(solution)/shard_map/ppermute | solution.py:20

commit v4 on v0

v4 whole, which is shorter than its diff:
```python
import jax
import jax.numpy as jnp
from jax import lax
from jax.sharding import PartitionSpec as P

GROUP = 4


route_scale = 2.5


def swapped(value, mask, crossed):
    ranks = lax.axis_size("ep")
    cores = lax.axis_size("tp")
    pairs = []
    for source in range(ranks):
        for core in range(cores):
            target_core = (core + 1) % cores if crossed else core
            pairs.append((source * cores + core, (source ^ mask) * cores + target_core))
    return lax.ppermute(value, ("ep", "tp"), pairs)


def core_sum(value):
    cores = lax.axis_size("tp")
    total = value
    for step in range(1, cores):
        pairs = [(core, (core + step) % cores) for core in range(cores)]
        total = total + lax.ppermute(value, "tp", pairs)
    return total


def by_xor(blocks, rank):
    mask = 1
    while mask < len(blocks):
        bit = (rank & mask) > 0
        blocks = [
            jnp.where(bit, blocks[index ^ mask], blocks[index]) for index in range(len(blocks))
        ]
        mask *= 2
    return blocks


def quarters_of(rows):
    quarter = rows.shape[1] // GROUP
    return [rows[:, index * quarter : (index + 1) * quarter] for index in range(GROUP)]


def spread_tokens(hidden):
    rank = lax.axis_index("ep")
    whole = {mask: swapped(hidden, mask, True) for mask in range(1, GROUP)}
    own = lax.optimization_barrier(by_xor(quarters_of(hidden), rank)[0])
    arrived = [own] + [by_xor(quarters_of(whole[mask]), rank)[0] for mask in range(1, GROUP)]
    tokens = jnp.stack(by_xor(arrived, rank))
    mask = GROUP
    while mask < lax.axis_size("ep"):
        bit = (rank & mask) > 0
        other = swapped(tokens, mask, True)
        tokens = jnp.concatenate(
            [jnp.where(bit, other, tokens), jnp.where(bit, tokens, other)], axis=0
        )
        mask *= 2
    return tokens


def return_tokens(expert_out):
    rank = lax.axis_index("ep")
    peers, tokens, quarter = expert_out.shape
    held = expert_out[:, None]
    mask = peers // 2
    while mask >= GROUP:
        bit = (rank & mask) > 0
        kept = jnp.where(bit, held[mask:], held[:mask])
        other = swapped(jnp.where(bit, held[:mask], held[mask:]), mask, True)
        held = jnp.concatenate(
            [jnp.where(bit, other, kept), jnp.where(bit, kept, other)], axis=1
        )
        mask //= 2
    bits = held.shape[1].bit_length() - 1
    order = [int(format(index, "b").zfill(bits)[::-1], 2) if bits else 0 for index in range(2**bits)]
    leaving = by_xor([held[index] for index in range(GROUP)], rank)
    leaving = lax.optimization_barrier(leaving)
    arrived = [leaving[0]] + [swapped(leaving[mask], mask, True) for mask in (3, 1, 2)]
    arrived = [arrived[index] for index in (0, 2, 3, 1)]
    return [
        jnp.stack([block[order[index]] for index in range(len(order))])
        for block in by_xor(arrived, rank)
    ]


def route_tables(expert_ids, experts, capacity):
    tok_rows, route_count = expert_ids.shape
    flat_ids = expert_ids.reshape(-1)
    expert_hot = (flat_ids[:, None] == jnp.arange(experts, dtype=jnp.int32)[None, :]).astype(
        jnp.int32
    )
    ranking = jnp.sum((jnp.cumsum(expert_hot, axis=0) - expert_hot) * expert_hot, axis=1)
    slot_hot = (ranking[:, None] == jnp.arange(capacity, dtype=jnp.int32)[None, :]).astype(
        jnp.float32
    )
    expert_float = expert_hot.astype(jnp.float32).reshape(tok_rows, route_count, experts)
    return (expert_float, slot_hot.reshape(tok_rows, route_count, capacity))


def expert_rows(rows, w_gate, w_up, w_down):
    hidden_units = w_gate.shape[1]
    weights_in = lax.optimization_barrier(jnp.concatenate([w_gate, w_up], axis=1))
    parts = jnp.dot(rows, weights_in, preferred_element_type=jnp.float32)
    sent = parts.astype(jnp.bfloat16)
    others = [swapped(sent, mask, False) for mask in range(GROUP - 1, 0, -1)]
    for other in others:
        parts = parts + other.astype(jnp.float32)
    inner_rows = (jax.nn.silu(parts[:, :hidden_units]) * parts[:, hidden_units:]).astype(
        jnp.bfloat16
    )
    partial_out = jnp.dot(inner_rows, w_down, preferred_element_type=jnp.float32)
    return core_sum(partial_out).astype(jnp.bfloat16)


def local(hidden, expert_ids, gate_scores, w_gate, w_up, w_down):
    tok_rows, width_all = hidden.shape
    route_count = expert_ids.shape[1]
    peer_count = lax.axis_size("ep")
    experts = peer_count // GROUP
    quarter = width_all // GROUP
    routing = (gate_scores / jnp.sum(gate_scores, axis=1, keepdims=True) * route_scale).astype(
        jnp.bfloat16
    )
    routing = routing.astype(jnp.float32)
    if route_count == experts:
        named = expert_ids[:, :, None] == jnp.arange(experts, dtype=jnp.int32)
        share = jnp.sum(jnp.where(named, routing[:, :, None], 0.0), axis=1)
        rows = spread_tokens(hidden).reshape(peer_count * tok_rows, quarter)
        expert_out = expert_rows(rows, w_gate[0], w_up[0], w_down[0])
        returned = return_tokens(expert_out.reshape(peer_count, tok_rows, quarter))
        combined = jnp.concatenate(
            [
                sum(
                    block[index].astype(jnp.float32) * share[:, index : index + 1]
                    for index in range(experts)
                )
                for block in returned
            ],
            axis=1,
        )
        return combined.astype(jnp.bfloat16)
    capacity = min(tok_rows, 2 * tok_rows * route_count // experts)
    expert_hot, slot_hot = route_tables(expert_ids, experts, capacity)
    placing = jnp.einsum("tke,tkc->ect", expert_hot, slot_hot).astype(jnp.bfloat16)
    outgoing = jnp.einsum(
        "ect,tgd->egcd",
        placing,
        hidden.reshape(tok_rows, GROUP, quarter),
        preferred_element_type=jnp.float32,
    ).astype(jnp.bfloat16)
    outgoing = outgoing.reshape(peer_count, capacity, quarter)
    arrived = lax.all_to_all(outgoing, "ep", split_axis=0, concat_axis=0, tiled=True)
    rows = arrived.reshape(peer_count * capacity, quarter)
    expert_out = expert_rows(rows, w_gate[0], w_up[0], w_down[0])
    returned = lax.all_to_all(
        expert_out.reshape(peer_count, capacity, quarter),
        "ep",
        split_axis=0,
        concat_axis=0,
        tiled=True,
    ).reshape(experts, GROUP, capacity, quarter)
    combining = jnp.einsum("tk,tke,tkc->tec", routing, expert_hot, slot_hot).astype(jnp.bfloat16)
    combined = jnp.einsum(
        "tec,egcd->tgd", combining, returned, preferred_element_type=jnp.float32
    )
    return combined.reshape(tok_rows, width_all).astype(jnp.bfloat16)


def solution(mesh):
    return jax.shard_map(
        local,
        mesh=mesh,
        in_specs=(
            P(("groups", "ep"), None),
            P(("groups", "ep"), None),
            P(("groups", "ep"), None),
            P("ep", None, "tp"),
            P("ep", None, "tp"),
            P("ep", "tp", None),
        ),
        out_specs=P(("groups", "ep"), None),
        check_vma=False,
    )
```

time: 66.2 us -> 32.2 us (0.49)
  blocking collectives: 18 us -> 0 us
  between operations: 13.5 us -> 0.16 us
  starting transfers between devices: 9.63 us -> 16.1 us
  waiting for transfers between devices: 17.3 us -> 11.5 us
  matrix products: 4.15 us -> 0.67 us
  other arithmetic: 1.2 us -> 3.55 us
  local copies, waits for them, and re-layouts: 1.99 us -> 0.07 us
    all_to_all x1 -> x0, blocking collectives: 13.9 us -> none  [local(): lax.all_to_all(outgoing, 'ep', split_axis=0, concat_axis=0, tiled=True)]
    ppermute x4 -> x12, starting transfers between devices: 3.88 us -> 16.1 us  [the longest x11 16 us: swapped(): return lax.ppermute(value, ('ep', 'tp'), pairs)]
    ppermute x4 -> x12, waiting for transfers between devices: 5.15 us -> 11.5 us  [the longest x11 10.2 us: swapped(): return lax.ppermute(value, ('ep', 'tp'), pairs)]
    all_to_all x1 -> x0, waiting for transfers between devices: 6.35 us -> none  [local(): lax.all_to_all(expert_out, 'ep', split_axis=0, concat_axis=0, tiled=True)]
    reduce_scatter x1 -> x0, waiting for transfers between devices: 5.78 us -> none  [local(): lax.psum_scatter(partial_out, 'tp', scatter_dimension=1, tiled=True)]
    all_to_all x1 -> x0, starting transfers between devices: 5.75 us -> none  [local(): lax.all_to_all(expert_out, 'ep', split_axis=0, concat_axis=0, tiled=True)]
    psum x1 -> x0, blocking collectives: 4.12 us -> none  [local(): combined = lax.psum(combined.reshape(tok_rows, width_all), 'tp')]
    dot_general x7 -> x2, matrix products: 4.15 us -> 0.67 us  [the longest x1 0.42 us: expert_rows(): parts = jnp.dot(rows, weights_in, preferred_element_type=jnp.float32)]
  transfers between devices with their start and end apart: 6 -> 12, of which waited for: 6 -> 11; matrix products, arithmetic and copies ran while one was open for 1% -> 8% of each run, Pallas kernels for 0% -> 0%
where the time goes in v4:
time: 32.2 us; the launch traced here: 32 us
  starting transfers between devices  16.1 us (50%)
  waiting for transfers between devices  11.5 us (36%)
  other arithmetic  3.55 us (11%)
  matrix products  0.67 us (2%)
    ppermute x11, starting transfers between devices, swapped(): return lax.ppermute(value, ('ep', 'tp'), pairs)  16 us
    ppermute x11, waiting for transfers between devices, swapped(): return lax.ppermute(value, ('ep', 'tp'), pairs)  10.2 us
    concatenate x1, other arithmetic, expert_rows(): jnp.concatenate([w_gate, w_up], axis=1)  1.68 us
    ppermute x1, waiting for transfers between devices, core_sum(): total = total + lax.ppermute(value, 'tp', pairs)  1.3 us
    select_n x4, other arithmetic, by_xor(): jnp.where(bit, blocks[index ^ mask], blocks[index])  0.88 us
  transfers between devices with their start and end apart: 12, of which 11 were waited for; matrix products, arithmetic and copies ran while one was open for 8% of the time, Pallas kernels for 0%

profile of v4, /device:TPU:0, one launch (start us, length us, event | category | flops | bytes accessed | tf_op | source)
XLA Modules:
  0.0 32.0 jit_solution(17097198112715077655)
XLA Ops:
  0.0 3.4 %collective-permute-start = (bf16[4,3584]{1,0:T(4,128)(2,1)}, bf16[4,3584]{1,0:T(4,128)(2,1)S(1)}, u32[]{:S(2)}, u32[]{:S(2)}) collective-permute-start(bf16[4,3584]{1,0:T(4,128)(2,1)} %param.6), channel_id=1, source_target_pairs={{0,7},{1,6},{2,5},{3,4},{4,3},{5,2},{6,1},{7,0},{8,15},{9,14},{10,... | collective-permute-start | bytes 86024 | tf_op jit(solution)/shard_map/ppermute | solution.py:20
  3.4 0.7 %collective-permute-start.1 = (bf16[4,3584]{1,0:T(4,128)(2,1)}, bf16[4,3584]{1,0:T(4,128)(2,1)S(1)}, u32[]{:S(2)}, u32[]{:S(2)}) collective-permute-start(bf16[4,3584]{1,0:T(4,128)(2,1)} %param.6), channel_id=1, source_target_pairs={{0,5},{1,4},{2,7},{3,6},{4,1},{5,0},{6,3},{7,2},{8,13},{9,12},{10,... | collective-permute-start | bytes 86024 | tf_op jit(solution)/shard_map/ppermute | solution.py:20
  4.3 0.8 %select_select_fusion = bf16[4,896]{1,0:T(4,128)(2,1)S(1)} fusion(bf16[4,3584]{1,0:T(4,128)(2,1)} %param.6, pred[]{:T(512)S(6)} %gt.7, pred[]{:T(512)S(6)} %gt.6), kind=kLoop, calls=%fused_computation.80 | loop fusion | flops 10752 | bytes 35842 | tf_op jit(solution)/shard_map/jit(_where)/select_n | solution.py:37
  5.1 0.2 collective-permute-done
  5.3 1.6 %collective-permute-done.1 = bf16[4,3584]{1,0:T(4,128)(2,1)S(1)} collective-permute-done((bf16[4,3584]{1,0:T(4,128)(2,1)}, bf16[4,3584]{1,0:T(4,128)(2,1)S(1)}, u32[]{:S(2)}, u32[]{:S(2)}) %collective-permute-start.1) | collective-permute-done | bytes 28704 | tf_op jit(solution)/shard_map/ppermute | solution.py:20
  6.9 0.9 %collective-permute-done.2 = bf16[4,3584]{1,0:T(4,128)(2,1)S(1)} collective-permute-done((bf16[4,3584]{1,0:T(4,128)(2,1)}, bf16[4,3584]{1,0:T(4,128)(2,1)S(1)}, u32[]{:S(2)}, u32[]{:S(2)}) %collective-permute-start.2) | collective-permute-done | bytes 28704 | tf_op jit(solution)/shard_map/ppermute | solution.py:20
  7.9 2.4 %collective-permute-start.3 = (bf16[4,4,896]{2,1,0:T(4,128)(2,1)S(1)}, bf16[4,4,896]{2,1,0:T(4,128)(2,1)S(1)}, u32[]{:S(2)}, u32[]{:S(2)}) collective-permute-start(bf16[4,4,896]{2,1,0:T(4,128)(2,1)S(1)} %pad_maximum_fusion.2), channel_id=1, source_target_pairs={{0,9},{1,8},{2,11},{3,10},{4,13},{5,12},{6,15},{7,14},{8,1},{9,0},... | collective-permute-start | bytes 86024 | tf_op jit(solution)/shard_map/ppermute | solution.py:20
  10.3 1.7 %pad_maximum_fusion = bf16[896,1024]{1,0:T(8,128)(2,1)S(1)} fusion(bf16[896,512]{1,0:T(8,128)(2,1)} %bitcast.80, bf16[896,512]{1,0:T(8,128)(2,1)} %bitcast.81), kind=kLoop, calls=%fused_computation | loop fusion | flops 3670016 | bytes 3670016 | tf_op jit(solution)/shard_map/concatenate | solution.py:106
  12.0 0.2 collective-permute-done.3
  12.3 0.4 %fusion.25 = (bf16[32,1024]{1,0:T(8,128)(2,1)S(1)}, f32[32,1024]{1,0:T(8,128)S(1)}) fusion(bf16[32,896]{1,0:T(8,128)(2,1)S(1)} %reshape.84, bf16[896,1024]{1,0:T(8,128)(2,1)S(1)} %pad_maximum_fusion), kind=kOutput, calls=%fused_computation.92 | convolution fusion | flops 58753024 | bytes 2088960 | tf_op jit(solution)/shard_map/dot_general | solution.py:107
  12.7 1.6 %collective-permute-start.4 = (bf16[32,1024]{1,0:T(8,128)(2,1)S(1)}, bf16[32,1024]{1,0:T(8,128)(2,1)S(1)}, u32[]{:S(2)}, u32[]{:S(2)}) collective-permute-start(bf16[32,1024]{1,0:T(8,128)(2,1)S(1)} %get-tuple-element.41), channel_id=1, source_target_pairs={{0,6},{1,7},{2,4},{3,5},{4,2},{5,3},{6,0},{7,1},{8,14},{9,15},{10,... | collective-permute-start | bytes 196616 | tf_op jit(solution)/shard_map/ppermute | solution.py:20
  14.5 1.7 %collective-permute-start.6 = (bf16[32,1024]{1,0:T(8,128)(2,1)S(1)}, bf16[32,1024]{1,0:T(8,128)(2,1)S(1)}, u32[]{:S(2)}, u32[]{:S(2)}) collective-permute-start(bf16[32,1024]{1,0:T(8,128)(2,1)S(1)} %get-tuple-element.41), channel_id=1, source_target_pairs={{0,2},{1,3},{2,0},{3,1},{4,6},{5,7},{6,4},{7,5},{8,10},{9,11},{10,... | collective-permute-start | bytes 196616 | tf_op jit(solution)/shard_map/ppermute | solution.py:20
  16.3 1.7 %collective-permute-done.4 = bf16[32,1024]{1,0:T(8,128)(2,1)S(1)} collective-permute-done((bf16[32,1024]{1,0:T(8,128)(2,1)S(1)}, bf16[32,1024]{1,0:T(8,128)(2,1)S(1)}, u32[]{:S(2)}, u32[]{:S(2)}) %collective-permute-start.4) | collective-permute-done | bytes 65568 | tf_op jit(solution)/shard_map/ppermute | solution.py:20
  18.0 0.6 %collective-permute-done.5 = bf16[32,1024]{1,0:T(8,128)(2,1)S(1)} collective-permute-done((bf16[32,1024]{1,0:T(8,128)(2,1)S(1)}, bf16[32,1024]{1,0:T(8,128)(2,1)S(1)}, u32[]{:S(2)}, u32[]{:S(2)}) %collective-permute-start.5) | collective-permute-done | bytes 65568 | tf_op jit(solution)/shard_map/ppermute | solution.py:20
  18.6 0.7 %collective-permute-done.6 = bf16[32,1024]{1,0:T(8,128)(2,1)S(1)} collective-permute-done((bf16[32,1024]{1,0:T(8,128)(2,1)S(1)}, bf16[32,1024]{1,0:T(8,128)(2,1)S(1)}, u32[]{:S(2)}, u32[]{:S(2)}) %collective-permute-start.6) | collective-permute-done | bytes 65568 | tf_op jit(solution)/shard_map/ppermute | solution.py:20
  19.3 0.2 fusion
  19.6 1.3 %collective-permute-done.7 = f32[32,896]{1,0:T(8,128)S(1)} collective-permute-done((f32[32,896]{1,0:T(8,128)S(1)}, f32[32,896]{1,0:T(8,128)S(1)}, u32[]{:S(2)}, u32[]{:S(2)}) %collective-permute-start.7) | collective-permute-done | bytes 114720 | tf_op jit(solution)/shard_map/ppermute | solution.py:28
  21.0 2.6 %collective-permute-start.8 = (bf16[4,1,4,896]{3,2,1,0:T(4,128)(2,1)S(1)}, bf16[4,1,4,896]{3,2,1,0:T(4,128)(2,1)S(1)}, u32[]{:S(2)}, u32[]{:S(2)}) collective-permute-start(bf16[4,1,4,896]{3,2,1,0:T(4,128)(2,1)S(1)} %bitcast.87), channel_id=1, source_target_pairs={{0,9},{1,8},{2,11},{3,10},{4,13},{5,12},{6,15},{7,14},{8,1},{9,0},... | collective-permute-start | bytes 86024 | tf_op jit(solution)/shard_map/ppermute | solution.py:20
  23.6 1.6 %collective-permute-done.8 = bf16[4,1,4,896]{3,2,1,0:T(4,128)(2,1)S(1)} collective-permute-done((bf16[4,1,4,896]{3,2,1,0:T(4,128)(2,1)S(1)}, bf16[4,1,4,896]{3,2,1,0:T(4,128)(2,1)S(1)}, u32[]{:S(2)}, u32[]{:S(2)}) %collective-permute-start.8) | collective-permute-done | bytes 28704 | tf_op jit(solution)/shard_map/ppermute | solution.py:20
  25.4 2.8 %collective-permute-start.9 = (bf16[2,4,896]{2,1,0:T(4,128)(2,1)S(1)}, bf16[2,4,896]{2,1,0:T(4,128)(2,1)S(1)}, u32[]{:S(2)}, u32[]{:S(2)}) collective-permute-start(bf16[2,4,896]{2,1,0:T(4,128)(2,1)S(1)} %get-tuple-element.9), channel_id=1, source_target_pairs={{0,7},{1,6},{2,5},{3,4},{4,3},{5,2},{6,1},{7,0},{8,15},{9,14},{10,... | collective-permute-start | bytes 43016 | tf_op jit(solution)/shard_map/ppermute | solution.py:20
  28.2 0.5 %collective-permute-start.11 = (bf16[2,4,896]{2,1,0:T(4,128)(2,1)S(1)}, bf16[2,4,896]{2,1,0:T(4,128)(2,1)S(1)}, u32[]{:S(2)}, u32[]{:S(2)}) collective-permute-start(bf16[2,4,896]{2,1,0:T(4,128)(2,1)S(1)} %get-tuple-element.11), channel_id=1, source_target_pairs={{0,3},{1,2},{2,1},{3,0},{4,7},{5,6},{6,5},{7,4},{8,11},{9,10},{10,... | collective-permute-start | bytes 43016 | tf_op jit(solution)/shard_map/ppermute | solution.py:20
  28.6 1.0 %collective-permute-done.9 = bf16[2,4,896]{2,1,0:T(4,128)(2,1)S(1)} collective-permute-done((bf16[2,4,896]{2,1,0:T(4,128)(2,1)S(1)}, bf16[2,4,896]{2,1,0:T(4,128)(2,1)S(1)}, u32[]{:S(2)}, u32[]{:S(2)}) %collective-permute-start.9) | collective-permute-done | bytes 14368 | tf_op jit(solution)/shard_map/ppermute | solution.py:20
  29.6 1.7 %collective-permute-done.10 = bf16[2,4,896]{2,1,0:T(4,128)(2,1)S(1)} collective-permute-done((bf16[2,4,896]{2,1,0:T(4,128)(2,1)S(1)}, bf16[2,4,896]{2,1,0:T(4,128)(2,1)S(1)}, u32[]{:S(2)}, u32[]{:S(2)}) %collective-permute-start.10) | collective-permute-done | bytes 14368 | tf_op jit(solution)/shard_map/ppermute | solution.py:20
  31.4 0.6 %pad_maximum_fusion.3 = bf16[4,3584]{1,0:T(4,128)(2,1)} fusion(bf16[4,896]{1,0:T(4,128)(2,1)S(1)} %get-tuple-element.38, bf16[4,896]{1,0:T(4,128)(2,1)S(1)} %get-tuple-element.37, bf16[4,896]{1,0:T(4,128)(2,1)S(1)} %get-tuple-element.36, bf16[4,896]{1,0:T(4,128)(2,1)S(1)} %get-tuple-element.35), kind=kLoop, calls=%fused_computation.16 | loop fusion | flops 114688 | bytes 57344 | tf_op jit(solution)/shard_map/concatenate | solution.py:135
  (31 shorter events, 1.0 us)
Async XLA Ops:
  0.0 19.3 %copy-start = (bf16[1,512,896]{2,1,0:T(8,128)(2,1)S(1)}, bf16[1,512,896]{2,1,0:T(8,128)(2,1)}, u32[]{:S(2)}) copy-start(bf16[1,512,896]{2,1,0:T(8,128)(2,1)} %param.11) | copy-start | bytes 2752516
  0.0 5.3 %collective-permute-start = (bf16[4,3584]{1,0:T(4,128)(2,1)}, bf16[4,3584]{1,0:T(4,128)(2,1)S(1)}, u32[]{:S(2)}, u32[]{:S(2)}) collective-permute-start(bf16[4,3584]{1,0:T(4,128)(2,1)} %param.6), channel_id=1, source_target_pairs={{0,7},{1,6},{2,5},{3,4},{4,3},{5,2},{6,1},{7,0},{8,15},{9,14},{10,... | collective-permute-start | bytes 86024 | tf_op jit(solution)/shard_map/ppermute | solution.py:20
  3.4 3.5 %collective-permute-start.1 = (bf16[4,3584]{1,0:T(4,128)(2,1)}, bf16[4,3584]{1,0:T(4,128)(2,1)S(1)}, u32[]{:S(2)}, u32[]{:S(2)}) collective-permute-start(bf16[4,3584]{1,0:T(4,128)(2,1)} %param.6), channel_id=1, source_target_pairs={{0,5},{1,4},{2,7},{3,6},{4,1},{5,0},{6,3},{7,2},{8,13},{9,12},{10,... | collective-permute-start | bytes 86024 | tf_op jit(solution)/shard_map/ppermute | solution.py:20
  4.1 3.7 %collective-permute-start.2 = (bf16[4,3584]{1,0:T(4,128)(2,1)}, bf16[4,3584]{1,0:T(4,128)(2,1)S(1)}, u32[]{:S(2)}, u32[]{:S(2)}) collective-permute-start(bf16[4,3584]{1,0:T(4,128)(2,1)} %param.6), channel_id=1, source_target_pairs={{0,3},{1,2},{2,1},{3,0},{4,7},{5,6},{6,5},{7,4},{8,11},{9,10},{10,... | collective-permute-start | bytes 86024 | tf_op jit(solution)/shard_map/ppermute | solution.py:20
  7.9 4.3 %collective-permute-start.3 = (bf16[4,4,896]{2,1,0:T(4,128)(2,1)S(1)}, bf16[4,4,896]{2,1,0:T(4,128)(2,1)S(1)}, u32[]{:S(2)}, u32[]{:S(2)}) collective-permute-start(bf16[4,4,896]{2,1,0:T(4,128)(2,1)S(1)} %pad_maximum_fusion.2), channel_id=1, source_target_pairs={{0,9},{1,8},{2,11},{3,10},{4,13},{5,12},{6,15},{7,14},{8,1},{9,0},... | collective-permute-start | bytes 86024 | tf_op jit(solution)/shard_map/ppermute | solution.py:20
  12.0 4.3 %copy-start.1 = (f32[4,2]{0,1:T(2,128)S(1)}, f32[4,2]{0,1:T(2,128)}, u32[]{:S(2)}) copy-start(f32[4,2]{0,1:T(2,128)} %param.8) | copy-start | bytes 100
  12.3 11.3 %copy-start.2 = (s32[4,2]{0,1:T(2,128)S(1)}, s32[4,2]{0,1:T(2,128)}, u32[]{:S(2)}) copy-start(s32[4,2]{0,1:T(2,128)} %param.7) | copy-start | bytes 100
  12.7 5.3 %collective-permute-start.4 = (bf16[32,1024]{1,0:T(8,128)(2,1)S(1)}, bf16[32,1024]{1,0:T(8,128)(2,1)S(1)}, u32[]{:S(2)}, u32[]{:S(2)}) collective-permute-start(bf16[32,1024]{1,0:T(8,128)(2,1)S(1)} %get-tuple-element.41), channel_id=1, source_target_pairs={{0,6},{1,7},{2,4},{3,5},{4,2},{5,3},{6,0},{7,1},{8,14},{9,15},{10,... | collective-permute-start | bytes 196616 | tf_op jit(solution)/shard_map/ppermute | solution.py:20
  14.4 4.3 %collective-permute-start.5 = (bf16[32,1024]{1,0:T(8,128)(2,1)S(1)}, bf16[32,1024]{1,0:T(8,128)(2,1)S(1)}, u32[]{:S(2)}, u32[]{:S(2)}) collective-permute-start(bf16[32,1024]{1,0:T(8,128)(2,1)S(1)} %get-tuple-element.41), channel_id=1, source_target_pairs={{0,4},{1,5},{2,6},{3,7},{4,0},{5,1},{6,2},{7,3},{8,12},{9,13},{10,... | collective-permute-start | bytes 196616 | tf_op jit(solution)/shard_map/ppermute | solution.py:20
  14.5 4.7 %collective-permute-start.6 = (bf16[32,1024]{1,0:T(8,128)(2,1)S(1)}, bf16[32,1024]{1,0:T(8,128)(2,1)S(1)}, u32[]{:S(2)}, u32[]{:S(2)}) collective-permute-start(bf16[32,1024]{1,0:T(8,128)(2,1)S(1)} %get-tuple-element.41), channel_id=1, source_target_pairs={{0,2},{1,3},{2,0},{3,1},{4,6},{5,7},{6,4},{7,5},{8,10},{9,11},{10,... | collective-permute-start | bytes 196616 | tf_op jit(solution)/shard_map/ppermute | solution.py:20
  19.6 1.4 %collective-permute-start.7 = (f32[32,896]{1,0:T(8,128)S(1)}, f32[32,896]{1,0:T(8,128)S(1)}, u32[]{:S(2)}, u32[]{:S(2)}) collective-permute-start(f32[32,896]{1,0:T(8,128)S(1)} %fusion), channel_id=1, source_target_pairs={{0,1},{1,0},{2,3},{3,2},{4,5},{5,4},{6,7},{7,6},{8,9},{9,8},{10,11... | collective-permute-start | bytes 344072 | tf_op jit(solution)/shard_map/ppermute | solution.py:28
  21.0 4.3 %collective-permute-start.8 = (bf16[4,1,4,896]{3,2,1,0:T(4,128)(2,1)S(1)}, bf16[4,1,4,896]{3,2,1,0:T(4,128)(2,1)S(1)}, u32[]{:S(2)}, u32[]{:S(2)}) collective-permute-start(bf16[4,1,4,896]{3,2,1,0:T(4,128)(2,1)S(1)} %bitcast.87), channel_id=1, source_target_pairs={{0,9},{1,8},{2,11},{3,10},{4,13},{5,12},{6,15},{7,14},{8,1},{9,0},... | collective-permute-start | bytes 86024 | tf_op jit(solution)/shard_map/ppermute | solution.py:20
  25.4 4.2 %collective-permute-start.9 = (bf16[2,4,896]{2,1,0:T(4,128)(2,1)S(1)}, bf16[2,4,896]{2,1,0:T(4,128)(2,1)S(1)}, u32[]{:S(2)}, u32[]{:S(2)}) collective-permute-start(bf16[2,4,896]{2,1,0:T(4,128)(2,1)S(1)} %get-tuple-element.9), channel_id=1, source_target_pairs={{0,7},{1,6},{2,5},{3,4},{4,3},{5,2},{6,1},{7,0},{8,15},{9,14},{10,... | collective-permute-start | bytes 43016 | tf_op jit(solution)/shard_map/ppermute | solution.py:20
  28.2 3.1 %collective-permute-start.10 = (bf16[2,4,896]{2,1,0:T(4,128)(2,1)S(1)}, bf16[2,4,896]{2,1,0:T(4,128)(2,1)S(1)}, u32[]{:S(2)}, u32[]{:S(2)}) collective-permute-start(bf16[2,4,896]{2,1,0:T(4,128)(2,1)S(1)} %get-tuple-element.10), channel_id=1, source_target_pairs={{0,5},{1,4},{2,7},{3,6},{4,1},{5,0},{6,3},{7,2},{8,13},{9,12},{10,... | collective-permute-start | bytes 43016 | tf_op jit(solution)/shard_map/ppermute | solution.py:20
  28.2 3.1 %collective-permute-start.11 = (bf16[2,4,896]{2,1,0:T(4,128)(2,1)S(1)}, bf16[2,4,896]{2,1,0:T(4,128)(2,1)S(1)}, u32[]{:S(2)}, u32[]{:S(2)}) collective-permute-start(bf16[2,4,896]{2,1,0:T(4,128)(2,1)S(1)} %get-tuple-element.11), channel_id=1, source_target_pairs={{0,3},{1,2},{2,1},{3,0},{4,7},{5,6},{6,5},{7,4},{8,11},{9,10},{10,... | collective-permute-start | bytes 43016 | tf_op jit(solution)/shard_map/ppermute | solution.py:20

commit v5 on v4

--- a/solution.py
+++ b/solution.py
@@ -9,24 +9,23 @@
 route_scale = 2.5
 
 
-def swapped(value, mask, crossed):
+def swapped(value, masks, crossed):
     ranks = lax.axis_size("ep")
     cores = lax.axis_size("tp")
     pairs = []
     for source in range(ranks):
         for core in range(cores):
             target_core = (core + 1) % cores if crossed else core
-            pairs.append((source * cores + core, (source ^ mask) * cores + target_core))
+            pairs.append((source * cores + core, (source ^ masks[core]) * cores + target_core))
     return lax.ppermute(value, ("ep", "tp"), pairs)
 
 
-def core_sum(value):
-    cores = lax.axis_size("tp")
-    total = value
-    for step in range(1, cores):
-        pairs = [(core, (core + step) % cores) for core in range(cores)]
-        total = total + lax.ppermute(value, "tp", pairs)
-    return total
+def same_mask(mask):
+    return [mask] * lax.axis_size("tp")
+
+
+def other_core(value):
+    return lax.ppermute(value, "tp", [(0, 1), (1, 0)])
 
 
 def by_xor(blocks, rank):
@@ -45,16 +44,28 @@
     return [rows[:, index * quarter : (index + 1) * quarter] for index in range(GROUP)]
 
 
+def gathered(outgoing, near, arrive):
+    apart = arrive(swapped(outgoing, [2, 3], False))
+    close = arrive(swapped(near, same_mask(1), True))
+    swap = other_core(apart)
+    swap, apart, close = lax.optimization_barrier((swap, apart, close))
+    upper = lax.axis_index("tp") == 1
+    return [None, close, jnp.where(upper, swap, apart), jnp.where(upper, apart, swap)]
+
+
 def spread_tokens(hidden):
     rank = lax.axis_index("ep")
-    whole = {mask: swapped(hidden, mask, True) for mask in range(1, GROUP)}
-    own = lax.optimization_barrier(by_xor(quarters_of(hidden), rank)[0])
-    arrived = [own] + [by_xor(quarters_of(whole[mask]), rank)[0] for mask in range(1, GROUP)]
-    tokens = jnp.stack(by_xor(arrived, rank))
+
+    def own_quarter(rows):
+        return by_xor(quarters_of(rows), rank)[0]
+
+    blocks = gathered(hidden, hidden, own_quarter)
+    blocks[0] = lax.optimization_barrier(own_quarter(hidden))
+    tokens = jnp.stack(by_xor(blocks, rank))
     mask = GROUP
     while mask < lax.axis_size("ep"):
         bit = (rank & mask) > 0
-        other = swapped(tokens, mask, True)
+        other = swapped(tokens, same_mask(mask), True)
         tokens = jnp.concatenate(
             [jnp.where(bit, other, tokens), jnp.where(bit, tokens, other)], axis=0
         )
@@ -64,27 +75,26 @@
 
 def return_tokens(expert_out):
     rank = lax.axis_index("ep")
-    peers, tokens, quarter = expert_out.shape
     held = expert_out[:, None]
-    mask = peers // 2
-    while mask >= GROUP:
+    mask = GROUP
+    while mask < lax.axis_size("ep"):
         bit = (rank & mask) > 0
-        kept = jnp.where(bit, held[mask:], held[:mask])
-        other = swapped(jnp.where(bit, held[:mask], held[mask:]), mask, True)
+        pairs = held.reshape((-1, 2, GROUP) + held.shape[1:])
+        kept = jnp.where(bit, pairs[:, 1], pairs[:, 0]).reshape((-1,) + held.shape[1:])
+        sent = jnp.where(bit, pairs[:, 0], pairs[:, 1]).reshape((-1,) + held.shape[1:])
+        other = swapped(sent, same_mask(mask), True)
         held = jnp.concatenate(
             [jnp.where(bit, other, kept), jnp.where(bit, kept, other)], axis=1
         )
-        mask //= 2
-    bits = held.shape[1].bit_length() - 1
-    order = [int(format(index, "b").zfill(bits)[::-1], 2) if bits else 0 for index in range(2**bits)]
+        mask *= 2
     leaving = by_xor([held[index] for index in range(GROUP)], rank)
-    leaving = lax.optimization_barrier(leaving)
-    arrived = [leaving[0]] + [swapped(leaving[mask], mask, True) for mask in (3, 1, 2)]
-    arrived = [arrived[index] for index in (0, 2, 3, 1)]
-    return [
-        jnp.stack([block[order[index]] for index in range(len(order))])
-        for block in by_xor(arrived, rank)
-    ]
+    upper = lax.axis_index("tp") == 1
+    own, close, apart = lax.optimization_barrier(
+        (leaving[0], leaving[1], jnp.where(upper, leaving[3], leaving[2]))
+    )
+    blocks = gathered(apart, close, lambda block: block)
+    blocks[0] = own
+    return by_xor(blocks, rank)
 
 
 def route_tables(expert_ids, experts, capacity):
@@ -106,14 +116,14 @@
     weights_in = lax.optimization_barrier(jnp.concatenate([w_gate, w_up], axis=1))
     parts = jnp.dot(rows, weights_in, preferred_element_type=jnp.float32)
     sent = parts.astype(jnp.bfloat16)
-    others = [swapped(sent, mask, False) for mask in range(GROUP - 1, 0, -1)]
+    others = [swapped(sent, same_mask(mask), False) for mask in range(GROUP - 1, 0, -1)]
     for other in others:
         parts = parts + other.astype(jnp.float32)
     inner_rows = (jax.nn.silu(parts[:, :hidden_units]) * parts[:, hidden_units:]).astype(
         jnp.bfloat16
     )
     partial_out = jnp.dot(inner_rows, w_down, preferred_element_type=jnp.float32)
-    return core_sum(partial_out).astype(jnp.bfloat16)
+    return (partial_out + other_core(partial_out)).astype(jnp.bfloat16)
 
 
 def local(hidden, expert_ids, gate_scores, w_gate, w_up, w_down):

time: 32.2 us -> 31.4 us (0.975)
  waiting for transfers between devices: 11.5 us -> 10.2 us
  starting transfers between devices: 16.1 us -> 16.5 us
    ppermute x11 -> x9, waiting for transfers between devices: 10.2 us -> 8.87 us  [swapped(): return lax.ppermute(value, ('ep', 'tp'), pairs)]
    ppermute x1 -> x3, starting transfers between devices: 0.06 us -> 0.59 us  [other_core(): return lax.ppermute(value, 'tp', [(0, 1), (1, 0)])]
    ppermute x11 -> x9, starting transfers between devices: 16 us -> 15.9 us  [swapped(): return lax.ppermute(value, ('ep', 'tp'), pairs)]
    ppermute x1 -> x3, waiting for transfers between devices: 1.3 us -> 1.29 us  [other_core(): return lax.ppermute(value, 'tp', [(0, 1), (1, 0)])]
    select_n x4 -> x6, other arithmetic: 0.88 us -> 0.86 us  [by_xor(): jnp.where(bit, blocks[index ^ mask], blocks[index])]
  transfers between devices with their start and end apart: 12 -> 12, of which waited for: 11 -> 9; matrix products, arithmetic and copies ran while one was open for 8% -> 8% of each run, Pallas kernels for 0% -> 0%
where the time goes in v5:
time: 31.4 us; the launch traced here: 31.2 us
  starting transfers between devices  16.5 us (53%)
  waiting for transfers between devices  10.2 us (32%)
  other arithmetic  3.59 us (11%)
  matrix products  0.67 us (2%)
    ppermute x9, starting transfers between devices, swapped(): return lax.ppermute(value, ('ep', 'tp'), pairs)  15.9 us
    ppermute x9, waiting for transfers between devices, swapped(): return lax.ppermute(value, ('ep', 'tp'), pairs)  8.87 us
    concatenate x1, other arithmetic, expert_rows(): jnp.concatenate([w_gate, w_up], axis=1)  1.68 us
    ppermute x3, waiting for transfers between devices, other_core(): return lax.ppermute(value, 'tp', [(0, 1), (1, 0)])  1.29 us
    select_n x6, other arithmetic, by_xor(): jnp.where(bit, blocks[index ^ mask], blocks[index])  0.86 us
  transfers between devices with their start and end apart: 12, of which 9 were waited for; matrix products, arithmetic and copies ran while one was open for 8% of the time, Pallas kernels for 0%

profile of v5, /device:TPU:0, one launch (start us, length us, event | category | flops | bytes accessed | tf_op | source)
XLA Modules:
  0.0 31.2 jit_solution(14888638120588712285)
XLA Ops:
  0.0 3.0 %collective-permute-start = (bf16[4,3584]{1,0:T(4,128)(2,1)}, bf16[4,3584]{1,0:T(4,128)(2,1)S(1)}, u32[]{:S(2)}, u32[]{:S(2)}) collective-permute-start(bf16[4,3584]{1,0:T(4,128)(2,1)} %param.6), channel_id=1, source_target_pairs={{0,4},{1,7},{2,6},{3,5},{4,0},{5,3},{6,2},{7,1},{8,12},{9,15},{10,... | collective-permute-start | bytes 86024 | tf_op jit(solution)/shard_map/ppermute | solution.py:20
  3.0 0.6 %collective-permute-start.2 = (bf16[4,3584]{1,0:T(4,128)(2,1)}, bf16[4,3584]{1,0:T(4,128)(2,1)S(1)}, u32[]{:S(2)}, u32[]{:S(2)}) collective-permute-start(bf16[4,3584]{1,0:T(4,128)(2,1)} %param.6), channel_id=1, source_target_pairs={{0,3},{1,2},{2,1},{3,0},{4,7},{5,6},{6,5},{7,4},{8,11},{9,10},{10,... | collective-permute-start | bytes 86024 | tf_op jit(solution)/shard_map/ppermute | solution.py:20
  3.6 0.8 %select_select_fusion = bf16[4,896]{1,0:T(4,128)(2,1)S(1)} fusion(bf16[4,3584]{1,0:T(4,128)(2,1)} %param.6, pred[]{:T(512)S(6)} %gt.7, pred[]{:T(512)S(6)} %gt.6), kind=kLoop, calls=%fused_computation.78 | loop fusion | flops 10752 | bytes 35842 | tf_op jit(solution)/shard_map/jit(_where)/select_n | solution.py:36
  4.4 0.7 %collective-permute-done = bf16[4,3584]{1,0:T(4,128)(2,1)S(1)} collective-permute-done((bf16[4,3584]{1,0:T(4,128)(2,1)}, bf16[4,3584]{1,0:T(4,128)(2,1)S(1)}, u32[]{:S(2)}, u32[]{:S(2)}) %collective-permute-start) | collective-permute-done | bytes 28704 | tf_op jit(solution)/shard_map/ppermute | solution.py:20
  5.2 0.3 %collective-permute-start.1 = (bf16[4,896]{1,0:T(4,128)(2,1)S(1)}, bf16[4,896]{1,0:T(4,128)(2,1)S(1)}, u32[]{:S(2)}, u32[]{:S(2)}) collective-permute-start(bf16[4,896]{1,0:T(4,128)(2,1)S(1)} %fusion.17), channel_id=1, source_target_pairs={{0,1},{1,0},{2,3},{3,2},{4,5},{5,4},{6,7},{7,6},{8,9},{9,8},{10,11... | collective-permute-start | bytes 21512 | tf_op jit(solution)/shard_map/ppermute | solution.py:28
  5.5 1.0 %collective-permute-done.2 = bf16[4,3584]{1,0:T(4,128)(2,1)S(1)} collective-permute-done((bf16[4,3584]{1,0:T(4,128)(2,1)}, bf16[4,3584]{1,0:T(4,128)(2,1)S(1)}, u32[]{:S(2)}, u32[]{:S(2)}) %collective-permute-start.2) | collective-permute-done | bytes 28704 | tf_op jit(solution)/shard_map/ppermute | solution.py:20
  6.7 2.7 %collective-permute-start.3 = (bf16[4,4,896]{2,1,0:T(4,128)(2,1)S(1)}, bf16[4,4,896]{2,1,0:T(4,128)(2,1)S(1)}, u32[]{:S(2)}, u32[]{:S(2)}) collective-permute-start(bf16[4,4,896]{2,1,0:T(4,128)(2,1)S(1)} %pad_maximum_fusion.2), channel_id=1, source_target_pairs={{0,9},{1,8},{2,11},{3,10},{4,13},{5,12},{6,15},{7,14},{8,1},{9,0},... | collective-permute-start | bytes 86024 | tf_op jit(solution)/shard_map/ppermute | solution.py:20
  9.4 1.7 %pad_maximum_fusion = bf16[896,1024]{1,0:T(8,128)(2,1)S(1)} fusion(bf16[896,512]{1,0:T(8,128)(2,1)} %bitcast.88, bf16[896,512]{1,0:T(8,128)(2,1)} %bitcast.89), kind=kLoop, calls=%fused_computation | loop fusion | flops 3670016 | bytes 3670016 | tf_op jit(solution)/shard_map/concatenate | solution.py:116
  11.2 0.4 %fusion.21 = (bf16[32,1024]{1,0:T(8,128)(2,1)S(1)}, f32[32,1024]{1,0:T(8,128)S(1)}) fusion(bf16[32,896]{1,0:T(8,128)(2,1)S(1)} %reshape.90, bf16[896,1024]{1,0:T(8,128)(2,1)S(1)} %pad_maximum_fusion), kind=kOutput, calls=%fused_computation.92 | convolution fusion | flops 58753024 | bytes 2088960 | tf_op jit(solution)/shard_map/dot_general | solution.py:117
  11.7 2.6 %collective-permute-start.4 = (bf16[32,1024]{1,0:T(8,128)(2,1)S(1)}, bf16[32,1024]{1,0:T(8,128)(2,1)S(1)}, u32[]{:S(2)}, u32[]{:S(2)}) collective-permute-start(bf16[32,1024]{1,0:T(8,128)(2,1)S(1)} %get-tuple-element.49), channel_id=1, source_target_pairs={{0,6},{1,7},{2,4},{3,5},{4,2},{5,3},{6,0},{7,1},{8,14},{9,15},{10,... | collective-permute-start | bytes 196616 | tf_op jit(solution)/shard_map/ppermute | solution.py:20
  14.3 0.4 %collective-permute-start.5 = (bf16[32,1024]{1,0:T(8,128)(2,1)S(1)}, bf16[32,1024]{1,0:T(8,128)(2,1)S(1)}, u32[]{:S(2)}, u32[]{:S(2)}) collective-permute-start(bf16[32,1024]{1,0:T(8,128)(2,1)S(1)} %get-tuple-element.49), channel_id=1, source_target_pairs={{0,4},{1,5},{2,6},{3,7},{4,0},{5,1},{6,2},{7,3},{8,12},{9,13},{10,... | collective-permute-start | bytes 196616 | tf_op jit(solution)/shard_map/ppermute | solution.py:20
  14.7 0.5 %collective-permute-start.6 = (bf16[32,1024]{1,0:T(8,128)(2,1)S(1)}, bf16[32,1024]{1,0:T(8,128)(2,1)S(1)}, u32[]{:S(2)}, u32[]{:S(2)}) collective-permute-start(bf16[32,1024]{1,0:T(8,128)(2,1)S(1)} %get-tuple-element.49), channel_id=1, source_target_pairs={{0,2},{1,3},{2,0},{3,1},{4,6},{5,7},{6,4},{7,5},{8,10},{9,11},{10,... | collective-permute-start | bytes 196616 | tf_op jit(solution)/shard_map/ppermute | solution.py:20
  15.2 1.9 %collective-permute-done.4 = bf16[32,1024]{1,0:T(8,128)(2,1)S(1)} collective-permute-done((bf16[32,1024]{1,0:T(8,128)(2,1)S(1)}, bf16[32,1024]{1,0:T(8,128)(2,1)S(1)}, u32[]{:S(2)}, u32[]{:S(2)}) %collective-permute-start.4) | collective-permute-done | bytes 65568 | tf_op jit(solution)/shard_map/ppermute | solution.py:20
  17.1 1.4 %collective-permute-done.5 = bf16[32,1024]{1,0:T(8,128)(2,1)S(1)} collective-permute-done((bf16[32,1024]{1,0:T(8,128)(2,1)S(1)}, bf16[32,1024]{1,0:T(8,128)(2,1)S(1)}, u32[]{:S(2)}, u32[]{:S(2)}) %collective-permute-start.5) | collective-permute-done | bytes 65568 | tf_op jit(solution)/shard_map/ppermute | solution.py:20
  18.5 0.4 %collective-permute-done.6 = bf16[32,1024]{1,0:T(8,128)(2,1)S(1)} collective-permute-done((bf16[32,1024]{1,0:T(8,128)(2,1)S(1)}, bf16[32,1024]{1,0:T(8,128)(2,1)S(1)}, u32[]{:S(2)}, u32[]{:S(2)}) %collective-permute-start.6) | collective-permute-done | bytes 65568 | tf_op jit(solution)/shard_map/ppermute | solution.py:20
  19.0 0.2 fusion
  19.3 1.3 %collective-permute-done.7 = f32[32,896]{1,0:T(8,128)S(1)} collective-permute-done((f32[32,896]{1,0:T(8,128)S(1)}, f32[32,896]{1,0:T(8,128)S(1)}, u32[]{:S(2)}, u32[]{:S(2)}) %collective-permute-start.7) | collective-permute-done | bytes 114720 | tf_op jit(solution)/shard_map/ppermute | solution.py:28
  20.7 2.7 %collective-permute-start.8 = (bf16[4,1,4,896]{3,2,1,0:T(4,128)(2,1)S(1)}, bf16[4,1,4,896]{3,2,1,0:T(4,128)(2,1)S(1)}, u32[]{:S(2)}, u32[]{:S(2)}) collective-permute-start(bf16[4,1,4,896]{3,2,1,0:T(4,128)(2,1)S(1)} %select_bitcast_fusion), channel_id=1, source_target_pairs={{0,9},{1,8},{2,11},{3,10},{4,13},{5,12},{6,15},{7,14},{8,1},{9,0},... | collective-permute-start | bytes 86024 | tf_op jit(solution)/shard_map/ppermute | solution.py:20
  23.4 1.6 %collective-permute-done.8 = bf16[4,1,4,896]{3,2,1,0:T(4,128)(2,1)S(1)} collective-permute-done((bf16[4,1,4,896]{3,2,1,0:T(4,128)(2,1)S(1)}, bf16[4,1,4,896]{3,2,1,0:T(4,128)(2,1)S(1)}, u32[]{:S(2)}, u32[]{:S(2)}) %collective-permute-start.8) | collective-permute-done | bytes 28704 | tf_op jit(solution)/shard_map/ppermute | solution.py:20
  25.1 2.1 %collective-permute-start.9 = (bf16[2,4,896]{2,1,0:T(4,128)(2,1)S(1)}, bf16[2,4,896]{2,1,0:T(4,128)(2,1)S(1)}, u32[]{:S(2)}, u32[]{:S(2)}) collective-permute-start(bf16[2,4,896]{2,1,0:T(4,128)(2,1)S(1)} %get-tuple-element.17), channel_id=1, source_target_pairs={{0,4},{1,7},{2,6},{3,5},{4,0},{5,3},{6,2},{7,1},{8,12},{9,15},{10,... | collective-permute-start | bytes 43016 | tf_op jit(solution)/shard_map/ppermute | solution.py:20
  27.2 1.2 %collective-permute-start.11 = (bf16[2,4,896]{2,1,0:T(4,128)(2,1)S(1)}, bf16[2,4,896]{2,1,0:T(4,128)(2,1)S(1)}, u32[]{:S(2)}, u32[]{:S(2)}) collective-permute-start(bf16[2,4,896]{2,1,0:T(4,128)(2,1)S(1)} %get-tuple-element.18), channel_id=1, source_target_pairs={{0,3},{1,2},{2,1},{3,0},{4,7},{5,6},{6,5},{7,4},{8,11},{9,10},{10,... | collective-permute-start | bytes 43016 | tf_op jit(solution)/shard_map/ppermute | solution.py:20
  28.4 0.5 %collective-permute-done.9 = bf16[2,4,896]{2,1,0:T(4,128)(2,1)S(1)} collective-permute-done((bf16[2,4,896]{2,1,0:T(4,128)(2,1)S(1)}, bf16[2,4,896]{2,1,0:T(4,128)(2,1)S(1)}, u32[]{:S(2)}, u32[]{:S(2)}) %collective-permute-start.9) | collective-permute-done | bytes 14368 | tf_op jit(solution)/shard_map/ppermute | solution.py:20
  29.1 1.3 %collective-permute-done.11 = bf16[2,4,896]{2,1,0:T(4,128)(2,1)S(1)} collective-permute-done((bf16[2,4,896]{2,1,0:T(4,128)(2,1)S(1)}, bf16[2,4,896]{2,1,0:T(4,128)(2,1)S(1)}, u32[]{:S(2)}, u32[]{:S(2)}) %collective-permute-start.11) | collective-permute-done | bytes 14368 | tf_op jit(solution)/shard_map/ppermute | solution.py:20
  30.5 0.6 %pad_maximum_fusion.3 = bf16[4,3584]{1,0:T(4,128)(2,1)} fusion(bf16[4,896]{1,0:T(4,128)(2,1)S(1)} %get-tuple-element.46, bf16[4,896]{1,0:T(4,128)(2,1)S(1)} %get-tuple-element.45, bf16[4,896]{1,0:T(4,128)(2,1)S(1)} %get-tuple-element.44, bf16[4,896]{1,0:T(4,128)(2,1)S(1)} %get-tuple-element.43), kind=kLoop, calls=%fused_computation.16 | loop fusion | flops 114688 | bytes 57344 | tf_op jit(solution)/shard_map/concatenate | solution.py:145
  (33 shorter events, 0.8 us)
Async XLA Ops:
  0.0 19.0 %copy-start = (bf16[1,512,896]{2,1,0:T(8,128)(2,1)S(1)}, bf16[1,512,896]{2,1,0:T(8,128)(2,1)}, u32[]{:S(2)}) copy-start(bf16[1,512,896]{2,1,0:T(8,128)(2,1)} %param.11) | copy-start | bytes 2752516
  0.0 5.1 %collective-permute-start = (bf16[4,3584]{1,0:T(4,128)(2,1)}, bf16[4,3584]{1,0:T(4,128)(2,1)S(1)}, u32[]{:S(2)}, u32[]{:S(2)}) collective-permute-start(bf16[4,3584]{1,0:T(4,128)(2,1)} %param.6), channel_id=1, source_target_pairs={{0,4},{1,7},{2,6},{3,5},{4,0},{5,3},{6,2},{7,1},{8,12},{9,15},{10,... | collective-permute-start | bytes 86024 | tf_op jit(solution)/shard_map/ppermute | solution.py:20
  3.0 3.5 %collective-permute-start.2 = (bf16[4,3584]{1,0:T(4,128)(2,1)}, bf16[4,3584]{1,0:T(4,128)(2,1)S(1)}, u32[]{:S(2)}, u32[]{:S(2)}) collective-permute-start(bf16[4,3584]{1,0:T(4,128)(2,1)} %param.6), channel_id=1, source_target_pairs={{0,3},{1,2},{2,1},{3,0},{4,7},{5,6},{6,5},{7,4},{8,11},{9,10},{10,... | collective-permute-start | bytes 86024 | tf_op jit(solution)/shard_map/ppermute | solution.py:20
  5.2 1.4 %collective-permute-start.1 = (bf16[4,896]{1,0:T(4,128)(2,1)S(1)}, bf16[4,896]{1,0:T(4,128)(2,1)S(1)}, u32[]{:S(2)}, u32[]{:S(2)}) collective-permute-start(bf16[4,896]{1,0:T(4,128)(2,1)S(1)} %fusion.17), channel_id=1, source_target_pairs={{0,1},{1,0},{2,3},{3,2},{4,5},{5,4},{6,7},{7,6},{8,9},{9,8},{10,11... | collective-permute-start | bytes 21512 | tf_op jit(solution)/shard_map/ppermute | solution.py:28
  6.7 4.4 %collective-permute-start.3 = (bf16[4,4,896]{2,1,0:T(4,128)(2,1)S(1)}, bf16[4,4,896]{2,1,0:T(4,128)(2,1)S(1)}, u32[]{:S(2)}, u32[]{:S(2)}) collective-permute-start(bf16[4,4,896]{2,1,0:T(4,128)(2,1)S(1)} %pad_maximum_fusion.2), channel_id=1, source_target_pairs={{0,9},{1,8},{2,11},{3,10},{4,13},{5,12},{6,15},{7,14},{8,1},{9,0},... | collective-permute-start | bytes 86024 | tf_op jit(solution)/shard_map/ppermute | solution.py:20
  11.2 8.1 %copy-start.1 = (f32[4,2]{0,1:T(2,128)S(1)}, f32[4,2]{0,1:T(2,128)}, u32[]{:S(2)}) copy-start(f32[4,2]{0,1:T(2,128)} %param.8) | copy-start | bytes 100
  11.2 16.0 %copy-start.2 = (s32[4,2]{0,1:T(2,128)S(1)}, s32[4,2]{0,1:T(2,128)}, u32[]{:S(2)}) copy-start(s32[4,2]{0,1:T(2,128)} %param.7) | copy-start | bytes 100
  11.7 5.4 %collective-permute-start.4 = (bf16[32,1024]{1,0:T(8,128)(2,1)S(1)}, bf16[32,1024]{1,0:T(8,128)(2,1)S(1)}, u32[]{:S(2)}, u32[]{:S(2)}) collective-permute-start(bf16[32,1024]{1,0:T(8,128)(2,1)S(1)} %get-tuple-element.49), channel_id=1, source_target_pairs={{0,6},{1,7},{2,4},{3,5},{4,2},{5,3},{6,0},{7,1},{8,14},{9,15},{10,... | collective-permute-start | bytes 196616 | tf_op jit(solution)/shard_map/ppermute | solution.py:20
  14.3 4.3 %collective-permute-start.5 = (bf16[32,1024]{1,0:T(8,128)(2,1)S(1)}, bf16[32,1024]{1,0:T(8,128)(2,1)S(1)}, u32[]{:S(2)}, u32[]{:S(2)}) collective-permute-start(bf16[32,1024]{1,0:T(8,128)(2,1)S(1)} %get-tuple-element.49), channel_id=1, source_target_pairs={{0,4},{1,5},{2,6},{3,7},{4,0},{5,1},{6,2},{7,3},{8,12},{9,13},{10,... | collective-permute-start | bytes 196616 | tf_op jit(solution)/shard_map/ppermute | solution.py:20
  14.7 4.3 %collective-permute-start.6 = (bf16[32,1024]{1,0:T(8,128)(2,1)S(1)}, bf16[32,1024]{1,0:T(8,128)(2,1)S(1)}, u32[]{:S(2)}, u32[]{:S(2)}) collective-permute-start(bf16[32,1024]{1,0:T(8,128)(2,1)S(1)} %get-tuple-element.49), channel_id=1, source_target_pairs={{0,2},{1,3},{2,0},{3,1},{4,6},{5,7},{6,4},{7,5},{8,10},{9,11},{10,... | collective-permute-start | bytes 196616 | tf_op jit(solution)/shard_map/ppermute | solution.py:20
  19.2 1.4 %collective-permute-start.7 = (f32[32,896]{1,0:T(8,128)S(1)}, f32[32,896]{1,0:T(8,128)S(1)}, u32[]{:S(2)}, u32[]{:S(2)}) collective-permute-start(f32[32,896]{1,0:T(8,128)S(1)} %fusion), channel_id=1, source_target_pairs={{0,1},{1,0},{2,3},{3,2},{4,5},{5,4},{6,7},{7,6},{8,9},{9,8},{10,11... | collective-permute-start | bytes 344072 | tf_op jit(solution)/shard_map/ppermute | solution.py:28
  20.7 4.3 %collective-permute-start.8 = (bf16[4,1,4,896]{3,2,1,0:T(4,128)(2,1)S(1)}, bf16[4,1,4,896]{3,2,1,0:T(4,128)(2,1)S(1)}, u32[]{:S(2)}, u32[]{:S(2)}) collective-permute-start(bf16[4,1,4,896]{3,2,1,0:T(4,128)(2,1)S(1)} %select_bitcast_fusion), channel_id=1, source_target_pairs={{0,9},{1,8},{2,11},{3,10},{4,13},{5,12},{6,15},{7,14},{8,1},{9,0},... | collective-permute-start | bytes 86024 | tf_op jit(solution)/shard_map/ppermute | solution.py:20
  25.1 3.8 %collective-permute-start.9 = (bf16[2,4,896]{2,1,0:T(4,128)(2,1)S(1)}, bf16[2,4,896]{2,1,0:T(4,128)(2,1)S(1)}, u32[]{:S(2)}, u32[]{:S(2)}) collective-permute-start(bf16[2,4,896]{2,1,0:T(4,128)(2,1)S(1)} %get-tuple-element.17), channel_id=1, source_target_pairs={{0,4},{1,7},{2,6},{3,5},{4,0},{5,3},{6,2},{7,1},{8,12},{9,15},{10,... | collective-permute-start | bytes 43016 | tf_op jit(solution)/shard_map/ppermute | solution.py:20
  27.2 3.2 %collective-permute-start.11 = (bf16[2,4,896]{2,1,0:T(4,128)(2,1)S(1)}, bf16[2,4,896]{2,1,0:T(4,128)(2,1)S(1)}, u32[]{:S(2)}, u32[]{:S(2)}) collective-permute-start(bf16[2,4,896]{2,1,0:T(4,128)(2,1)S(1)} %get-tuple-element.18), channel_id=1, source_target_pairs={{0,3},{1,2},{2,1},{3,0},{4,7},{5,6},{6,5},{7,4},{8,11},{9,10},{10,... | collective-permute-start | bytes 43016 | tf_op jit(solution)/shard_map/ppermute | solution.py:20
  28.9 1.5 %collective-permute-start.10 = (bf16[2,4,896]{2,1,0:T(4,128)(2,1)S(1)}, bf16[2,4,896]{2,1,0:T(4,128)(2,1)S(1)}, u32[]{:S(2)}, u32[]{:S(2)}) collective-permute-start(bf16[2,4,896]{2,1,0:T(4,128)(2,1)S(1)} %collective-permute-done.9), channel_id=1, source_target_pairs={{0,1},{1,0},{2,3},{3,2},{4,5},{5,4},{6,7},{7,6},{8,9},{9,8},{10,11... | collective-permute-start | bytes 43016 | tf_op jit(solution)/shard_map/ppermute | solution.py:28

commit v6 on v5

--- a/solution.py
+++ b/solution.py
@@ -44,13 +44,19 @@
     return [rows[:, index * quarter : (index + 1) * quarter] for index in range(GROUP)]
 
 
-def gathered(outgoing, near, arrive):
-    apart = arrive(swapped(outgoing, [2, 3], False))
-    close = arrive(swapped(near, same_mask(1), True))
-    swap = other_core(apart)
-    swap, apart, close = lax.optimization_barrier((swap, apart, close))
+def gathered(split, masks, crossed, shared, shared_crossed, arrive):
+    third = masks[0] ^ masks[1]
+    got = arrive(swapped(split, masks, crossed))
+    both = arrive(swapped(shared, same_mask(third), shared_crossed))
+    swap = other_core(got)
+    swap, got, both = lax.optimization_barrier((swap, got, both))
     upper = lax.axis_index("tp") == 1
-    return [None, close, jnp.where(upper, swap, apart), jnp.where(upper, apart, swap)]
+    lower_mask, upper_mask = reversed(masks) if crossed else masks
+    return {
+        third: both,
+        lower_mask: jnp.where(upper, swap, got),
+        upper_mask: jnp.where(upper, got, swap),
+    }
 
 
 def spread_tokens(hidden):
@@ -59,9 +65,9 @@
     def own_quarter(rows):
         return by_xor(quarters_of(rows), rank)[0]
 
-    blocks = gathered(hidden, hidden, own_quarter)
+    blocks = gathered(hidden, [3, 2], True, hidden, True, own_quarter)
     blocks[0] = lax.optimization_barrier(own_quarter(hidden))
-    tokens = jnp.stack(by_xor(blocks, rank))
+    tokens = jnp.stack(by_xor([blocks[index] for index in range(GROUP)], rank))
     mask = GROUP
     while mask < lax.axis_size("ep"):
         bit = (rank & mask) > 0
@@ -89,12 +95,13 @@
         mask *= 2
     leaving = by_xor([held[index] for index in range(GROUP)], rank)
     upper = lax.axis_index("tp") == 1
-    own, close, apart = lax.optimization_barrier(
-        (leaving[0], leaving[1], jnp.where(upper, leaving[3], leaving[2]))
-    )
-    blocks = gathered(apart, close, lambda block: block)
+    masks = [1, 3]
+    own, shared, split = lax.optimization_barrier(
+        (leaving[0], leaving[2], jnp.where(upper, leaving[masks[1]], leaving[masks[0]]))
+    )
+    blocks = gathered(split, masks, False, shared, False, lambda block: block)
     blocks[0] = own
-    return by_xor(blocks, rank)
+    return by_xor([blocks[index] for index in range(GROUP)], rank)
 
 
 def route_tables(expert_ids, experts, capacity):

time: 31.4 us -> 30.9 us (0.984)
  waiting for transfers between devices: 10.2 us -> 9.67 us
    ppermute x9, waiting for transfers between devices: 8.87 us -> 8.34 us  [swapped(): return lax.ppermute(value, ('ep', 'tp'), pairs)]
    ppermute x3, starting transfers between devices: 0.59 us -> 0.98 us  [other_core(): return lax.ppermute(value, 'tp', [(0, 1), (1, 0)])]
    ppermute x9, starting transfers between devices: 15.9 us -> 15.5 us  [swapped(): return lax.ppermute(value, ('ep', 'tp'), pairs)]
  transfers between devices with their start and end apart: 12 -> 12, of which waited for: 9 -> 11; matrix products, arithmetic and copies ran while one was open for 8% -> 8% of each run, Pallas kernels for 0% -> 0%
where the time goes in v6:
time: 30.9 us; the launch traced here: 30.7 us
  starting transfers between devices  16.5 us (53%)
  waiting for transfers between devices  9.67 us (31%)
  other arithmetic  3.59 us (12%)
  matrix products  0.67 us (2%)
    ppermute x9, starting transfers between devices, swapped(): return lax.ppermute(value, ('ep', 'tp'), pairs)  15.5 us
    ppermute x9, waiting for transfers between devices, swapped(): return lax.ppermute(value, ('ep', 'tp'), pairs)  8.34 us
    concatenate x1, other arithmetic, expert_rows(): jnp.concatenate([w_gate, w_up], axis=1)  1.68 us
    ppermute x3, waiting for transfers between devices, other_core(): return lax.ppermute(value, 'tp', [(0, 1), (1, 0)])  1.34 us
    ppermute x3, starting transfers between devices, other_core(): return lax.ppermute(value, 'tp', [(0, 1), (1, 0)])  0.98 us
    select_n x6, other arithmetic, by_xor(): jnp.where(bit, blocks[index ^ mask], blocks[index])  0.86 us
    concatenate x1, other arithmetic, local(): jnp.concatenate([sum((block[index].astype(jnp.float32) * share[:, index:i...  0.63 us
  transfers between devices with their start and end apart: 12, of which 11 were waited for; matrix products, arithmetic and copies ran while one was open for 8% of the time, Pallas kernels for 0%

profile of v6, /device:TPU:0, one launch (start us, length us, event | category | flops | bytes accessed | tf_op | source)
XLA Modules:
  0.0 30.7 jit_solution(502059365460509056)
XLA Ops:
  0.0 3.4 %collective-permute-start = (bf16[4,3584]{1,0:T(4,128)(2,1)}, bf16[4,3584]{1,0:T(4,128)(2,1)S(1)}, u32[]{:S(2)}, u32[]{:S(2)}) collective-permute-start(bf16[4,3584]{1,0:T(4,128)(2,1)} %param.6), channel_id=1, source_target_pairs={{0,7},{1,4},{2,5},{3,6},{4,3},{5,0},{6,1},{7,2},{8,15},{9,12},{10,... | collective-permute-start | bytes 86024 | tf_op jit(solution)/shard_map/ppermute | solution.py:20
  3.4 0.8 %collective-permute-start.2 = (bf16[4,3584]{1,0:T(4,128)(2,1)}, bf16[4,3584]{1,0:T(4,128)(2,1)S(1)}, u32[]{:S(2)}, u32[]{:S(2)}) collective-permute-start(bf16[4,3584]{1,0:T(4,128)(2,1)} %param.6), channel_id=1, source_target_pairs={{0,3},{1,2},{2,1},{3,0},{4,7},{5,6},{6,5},{7,4},{8,11},{9,10},{10,... | collective-permute-start | bytes 86024 | tf_op jit(solution)/shard_map/ppermute | solution.py:20
  4.2 0.8 %select_select_fusion = bf16[4,896]{1,0:T(4,128)(2,1)S(1)} fusion(bf16[4,3584]{1,0:T(4,128)(2,1)} %param.6, pred[]{:T(512)S(6)} %gt.7, pred[]{:T(512)S(6)} %gt.6), kind=kLoop, calls=%fused_computation.76 | loop fusion | flops 10752 | bytes 35842 | tf_op jit(solution)/shard_map/jit(_where)/select_n | solution.py:36
  5.2 0.9 %collective-permute-start.1 = (bf16[4,896]{1,0:T(4,128)(2,1)S(1)}, bf16[4,896]{1,0:T(4,128)(2,1)S(1)}, u32[]{:S(2)}, u32[]{:S(2)}) collective-permute-start(bf16[4,896]{1,0:T(4,128)(2,1)S(1)} %fusion.17), channel_id=1, source_target_pairs={{0,1},{1,0},{2,3},{3,2},{4,5},{5,4},{6,7},{7,6},{8,9},{9,8},{10,11... | collective-permute-start | bytes 21512 | tf_op jit(solution)/shard_map/ppermute | solution.py:28
  6.1 1.0 %collective-permute-done.2 = bf16[4,3584]{1,0:T(4,128)(2,1)S(1)} collective-permute-done((bf16[4,3584]{1,0:T(4,128)(2,1)}, bf16[4,3584]{1,0:T(4,128)(2,1)S(1)}, u32[]{:S(2)}, u32[]{:S(2)}) %collective-permute-start.2) | collective-permute-done | bytes 28704 | tf_op jit(solution)/shard_map/ppermute | solution.py:20
  7.3 2.4 %collective-permute-start.3 = (bf16[4,4,896]{2,1,0:T(4,128)(2,1)S(1)}, bf16[4,4,896]{2,1,0:T(4,128)(2,1)S(1)}, u32[]{:S(2)}, u32[]{:S(2)}) collective-permute-start(bf16[4,4,896]{2,1,0:T(4,128)(2,1)S(1)} %pad_maximum_fusion.2), channel_id=1, source_target_pairs={{0,9},{1,8},{2,11},{3,10},{4,13},{5,12},{6,15},{7,14},{8,1},{9,0},... | collective-permute-start | bytes 86024 | tf_op jit(solution)/shard_map/ppermute | solution.py:20
  9.6 1.7 %pad_maximum_fusion = bf16[896,1024]{1,0:T(8,128)(2,1)S(1)} fusion(bf16[896,512]{1,0:T(8,128)(2,1)} %bitcast.88, bf16[896,512]{1,0:T(8,128)(2,1)} %bitcast.89), kind=kLoop, calls=%fused_computation | loop fusion | flops 3670016 | bytes 3670016 | tf_op jit(solution)/shard_map/concatenate | solution.py:123
  11.3 0.2 collective-permute-done.3
  11.7 0.4 %fusion.21 = (bf16[32,1024]{1,0:T(8,128)(2,1)S(1)}, f32[32,1024]{1,0:T(8,128)S(1)}) fusion(bf16[32,896]{1,0:T(8,128)(2,1)S(1)} %reshape.90, bf16[896,1024]{1,0:T(8,128)(2,1)S(1)} %pad_maximum_fusion), kind=kOutput, calls=%fused_computation.90 | convolution fusion | flops 58753024 | bytes 2088960 | tf_op jit(solution)/shard_map/dot_general | solution.py:124
  12.1 2.1 %collective-permute-start.4 = (bf16[32,1024]{1,0:T(8,128)(2,1)S(1)}, bf16[32,1024]{1,0:T(8,128)(2,1)S(1)}, u32[]{:S(2)}, u32[]{:S(2)}) collective-permute-start(bf16[32,1024]{1,0:T(8,128)(2,1)S(1)} %get-tuple-element.49), channel_id=1, source_target_pairs={{0,6},{1,7},{2,4},{3,5},{4,2},{5,3},{6,0},{7,1},{8,14},{9,15},{10,... | collective-permute-start | bytes 196616 | tf_op jit(solution)/shard_map/ppermute | solution.py:20
  14.2 0.4 %collective-permute-start.5 = (bf16[32,1024]{1,0:T(8,128)(2,1)S(1)}, bf16[32,1024]{1,0:T(8,128)(2,1)S(1)}, u32[]{:S(2)}, u32[]{:S(2)}) collective-permute-start(bf16[32,1024]{1,0:T(8,128)(2,1)S(1)} %get-tuple-element.49), channel_id=1, source_target_pairs={{0,4},{1,5},{2,6},{3,7},{4,0},{5,1},{6,2},{7,3},{8,12},{9,13},{10,... | collective-permute-start | bytes 196616 | tf_op jit(solution)/shard_map/ppermute | solution.py:20
  14.6 1.1 %collective-permute-start.6 = (bf16[32,1024]{1,0:T(8,128)(2,1)S(1)}, bf16[32,1024]{1,0:T(8,128)(2,1)S(1)}, u32[]{:S(2)}, u32[]{:S(2)}) collective-permute-start(bf16[32,1024]{1,0:T(8,128)(2,1)S(1)} %get-tuple-element.49), channel_id=1, source_target_pairs={{0,2},{1,3},{2,0},{3,1},{4,6},{5,7},{6,4},{7,5},{8,10},{9,11},{10,... | collective-permute-start | bytes 196616 | tf_op jit(solution)/shard_map/ppermute | solution.py:20
  15.6 2.1 %collective-permute-done.4 = bf16[32,1024]{1,0:T(8,128)(2,1)S(1)} collective-permute-done((bf16[32,1024]{1,0:T(8,128)(2,1)S(1)}, bf16[32,1024]{1,0:T(8,128)(2,1)S(1)}, u32[]{:S(2)}, u32[]{:S(2)}) %collective-permute-start.4) | collective-permute-done | bytes 65568 | tf_op jit(solution)/shard_map/ppermute | solution.py:20
  17.7 0.7 %collective-permute-done.5 = bf16[32,1024]{1,0:T(8,128)(2,1)S(1)} collective-permute-done((bf16[32,1024]{1,0:T(8,128)(2,1)S(1)}, bf16[32,1024]{1,0:T(8,128)(2,1)S(1)}, u32[]{:S(2)}, u32[]{:S(2)}) %collective-permute-start.5) | collective-permute-done | bytes 65568 | tf_op jit(solution)/shard_map/ppermute | solution.py:20
  18.5 0.4 %collective-permute-done.6 = bf16[32,1024]{1,0:T(8,128)(2,1)S(1)} collective-permute-done((bf16[32,1024]{1,0:T(8,128)(2,1)S(1)}, bf16[32,1024]{1,0:T(8,128)(2,1)S(1)}, u32[]{:S(2)}, u32[]{:S(2)}) %collective-permute-start.6) | collective-permute-done | bytes 65568 | tf_op jit(solution)/shard_map/ppermute | solution.py:20
  18.9 0.2 fusion
  19.2 1.3 %collective-permute-done.7 = f32[32,896]{1,0:T(8,128)S(1)} collective-permute-done((f32[32,896]{1,0:T(8,128)S(1)}, f32[32,896]{1,0:T(8,128)S(1)}, u32[]{:S(2)}, u32[]{:S(2)}) %collective-permute-start.7) | collective-permute-done | bytes 114720 | tf_op jit(solution)/shard_map/ppermute | solution.py:28
  20.6 2.5 %collective-permute-start.8 = (bf16[4,1,4,896]{3,2,1,0:T(4,128)(2,1)S(1)}, bf16[4,1,4,896]{3,2,1,0:T(4,128)(2,1)S(1)}, u32[]{:S(2)}, u32[]{:S(2)}) collective-permute-start(bf16[4,1,4,896]{3,2,1,0:T(4,128)(2,1)S(1)} %select_bitcast_fusion), channel_id=1, source_target_pairs={{0,9},{1,8},{2,11},{3,10},{4,13},{5,12},{6,15},{7,14},{8,1},{9,0},... | collective-permute-start | bytes 86024 | tf_op jit(solution)/shard_map/ppermute | solution.py:20
  23.1 1.8 %collective-permute-done.8 = bf16[4,1,4,896]{3,2,1,0:T(4,128)(2,1)S(1)} collective-permute-done((bf16[4,1,4,896]{3,2,1,0:T(4,128)(2,1)S(1)}, bf16[4,1,4,896]{3,2,1,0:T(4,128)(2,1)S(1)}, u32[]{:S(2)}, u32[]{:S(2)}) %collective-permute-start.8) | collective-permute-done | bytes 28704 | tf_op jit(solution)/shard_map/ppermute | solution.py:20
  25.0 1.1 %collective-permute-start.9 = (bf16[2,4,896]{2,1,0:T(4,128)(2,1)S(1)}, bf16[2,4,896]{2,1,0:T(4,128)(2,1)S(1)}, u32[]{:S(2)}, u32[]{:S(2)}) collective-permute-start(bf16[2,4,896]{2,1,0:T(4,128)(2,1)S(1)} %get-tuple-element.17), channel_id=1, source_target_pairs={{0,2},{1,7},{2,0},{3,5},{4,6},{5,3},{6,4},{7,1},{8,10},{9,15},{10,... | collective-permute-start | bytes 43016 | tf_op jit(solution)/shard_map/ppermute | solution.py:20
  26.1 1.8 %collective-permute-start.11 = (bf16[2,4,896]{2,1,0:T(4,128)(2,1)S(1)}, bf16[2,4,896]{2,1,0:T(4,128)(2,1)S(1)}, u32[]{:S(2)}, u32[]{:S(2)}) collective-permute-start(bf16[2,4,896]{2,1,0:T(4,128)(2,1)S(1)} %get-tuple-element.18), channel_id=1, source_target_pairs={{0,4},{1,5},{2,6},{3,7},{4,0},{5,1},{6,2},{7,3},{8,12},{9,13},{10,... | collective-permute-start | bytes 43016 | tf_op jit(solution)/shard_map/ppermute | solution.py:20
  27.9 0.8 %collective-permute-done.9 = bf16[2,4,896]{2,1,0:T(4,128)(2,1)S(1)} collective-permute-done((bf16[2,4,896]{2,1,0:T(4,128)(2,1)S(1)}, bf16[2,4,896]{2,1,0:T(4,128)(2,1)S(1)}, u32[]{:S(2)}, u32[]{:S(2)}) %collective-permute-start.9) | collective-permute-done | bytes 14368 | tf_op jit(solution)/shard_map/ppermute | solution.py:20
  28.8 1.1 %collective-permute-done.11 = bf16[2,4,896]{2,1,0:T(4,128)(2,1)S(1)} collective-permute-done((bf16[2,4,896]{2,1,0:T(4,128)(2,1)S(1)}, bf16[2,4,896]{2,1,0:T(4,128)(2,1)S(1)}, u32[]{:S(2)}, u32[]{:S(2)}) %collective-permute-start.11) | collective-permute-done | bytes 14368 | tf_op jit(solution)/shard_map/ppermute | solution.py:20
  30.1 0.6 %pad_maximum_fusion.3 = bf16[4,3584]{1,0:T(4,128)(2,1)} fusion(bf16[4,896]{1,0:T(4,128)(2,1)S(1)} %get-tuple-element.46, bf16[4,896]{1,0:T(4,128)(2,1)S(1)} %get-tuple-element.45, bf16[4,896]{1,0:T(4,128)(2,1)S(1)} %get-tuple-element.44, bf16[4,896]{1,0:T(4,128)(2,1)S(1)} %get-tuple-element.43), kind=kLoop, calls=%fused_computation.16 | loop fusion | flops 114688 | bytes 57344 | tf_op jit(solution)/shard_map/concatenate | solution.py:152
  (33 shorter events, 0.8 us)
Async XLA Ops:
  0.0 18.9 %copy-start = (bf16[1,512,896]{2,1,0:T(8,128)(2,1)S(1)}, bf16[1,512,896]{2,1,0:T(8,128)(2,1)}, u32[]{:S(2)}) copy-start(bf16[1,512,896]{2,1,0:T(8,128)(2,1)} %param.11) | copy-start | bytes 2752516
  0.0 5.2 %collective-permute-start = (bf16[4,3584]{1,0:T(4,128)(2,1)}, bf16[4,3584]{1,0:T(4,128)(2,1)S(1)}, u32[]{:S(2)}, u32[]{:S(2)}) collective-permute-start(bf16[4,3584]{1,0:T(4,128)(2,1)} %param.6), channel_id=1, source_target_pairs={{0,7},{1,4},{2,5},{3,6},{4,3},{5,0},{6,1},{7,2},{8,15},{9,12},{10,... | collective-permute-start | bytes 86024 | tf_op jit(solution)/shard_map/ppermute | solution.py:20
  3.4 3.7 %collective-permute-start.2 = (bf16[4,3584]{1,0:T(4,128)(2,1)}, bf16[4,3584]{1,0:T(4,128)(2,1)S(1)}, u32[]{:S(2)}, u32[]{:S(2)}) collective-permute-start(bf16[4,3584]{1,0:T(4,128)(2,1)} %param.6), channel_id=1, source_target_pairs={{0,3},{1,2},{2,1},{3,0},{4,7},{5,6},{6,5},{7,4},{8,11},{9,10},{10,... | collective-permute-start | bytes 86024 | tf_op jit(solution)/shard_map/ppermute | solution.py:20
  5.2 2.0 %collective-permute-start.1 = (bf16[4,896]{1,0:T(4,128)(2,1)S(1)}, bf16[4,896]{1,0:T(4,128)(2,1)S(1)}, u32[]{:S(2)}, u32[]{:S(2)}) collective-permute-start(bf16[4,896]{1,0:T(4,128)(2,1)S(1)} %fusion.17), channel_id=1, source_target_pairs={{0,1},{1,0},{2,3},{3,2},{4,5},{5,4},{6,7},{7,6},{8,9},{9,8},{10,11... | collective-permute-start | bytes 21512 | tf_op jit(solution)/shard_map/ppermute | solution.py:28
  7.3 4.3 %collective-permute-start.3 = (bf16[4,4,896]{2,1,0:T(4,128)(2,1)S(1)}, bf16[4,4,896]{2,1,0:T(4,128)(2,1)S(1)}, u32[]{:S(2)}, u32[]{:S(2)}) collective-permute-start(bf16[4,4,896]{2,1,0:T(4,128)(2,1)S(1)} %pad_maximum_fusion.2), channel_id=1, source_target_pairs={{0,9},{1,8},{2,11},{3,10},{4,13},{5,12},{6,15},{7,14},{8,1},{9,0},... | collective-permute-start | bytes 86024 | tf_op jit(solution)/shard_map/ppermute | solution.py:20
  11.7 7.5 %copy-start.1 = (f32[4,2]{0,1:T(2,128)S(1)}, f32[4,2]{0,1:T(2,128)}, u32[]{:S(2)}) copy-start(f32[4,2]{0,1:T(2,128)} %param.8) | copy-start | bytes 100
  11.7 14.4 %copy-start.2 = (s32[4,2]{0,1:T(2,128)S(1)}, s32[4,2]{0,1:T(2,128)}, u32[]{:S(2)}) copy-start(s32[4,2]{0,1:T(2,128)} %param.7) | copy-start | bytes 100
  12.1 5.6 %collective-permute-start.4 = (bf16[32,1024]{1,0:T(8,128)(2,1)S(1)}, bf16[32,1024]{1,0:T(8,128)(2,1)S(1)}, u32[]{:S(2)}, u32[]{:S(2)}) collective-permute-start(bf16[32,1024]{1,0:T(8,128)(2,1)S(1)} %get-tuple-element.49), channel_id=1, source_target_pairs={{0,6},{1,7},{2,4},{3,5},{4,2},{5,3},{6,0},{7,1},{8,14},{9,15},{10,... | collective-permute-start | bytes 196616 | tf_op jit(solution)/shard_map/ppermute | solution.py:20
  14.2 4.3 %collective-permute-start.5 = (bf16[32,1024]{1,0:T(8,128)(2,1)S(1)}, bf16[32,1024]{1,0:T(8,128)(2,1)S(1)}, u32[]{:S(2)}, u32[]{:S(2)}) collective-permute-start(bf16[32,1024]{1,0:T(8,128)(2,1)S(1)} %get-tuple-element.49), channel_id=1, source_target_pairs={{0,4},{1,5},{2,6},{3,7},{4,0},{5,1},{6,2},{7,3},{8,12},{9,13},{10,... | collective-permute-start | bytes 196616 | tf_op jit(solution)/shard_map/ppermute | solution.py:20
  14.6 4.3 %collective-permute-start.6 = (bf16[32,1024]{1,0:T(8,128)(2,1)S(1)}, bf16[32,1024]{1,0:T(8,128)(2,1)S(1)}, u32[]{:S(2)}, u32[]{:S(2)}) collective-permute-start(bf16[32,1024]{1,0:T(8,128)(2,1)S(1)} %get-tuple-element.49), channel_id=1, source_target_pairs={{0,2},{1,3},{2,0},{3,1},{4,6},{5,7},{6,4},{7,5},{8,10},{9,11},{10,... | collective-permute-start | bytes 196616 | tf_op jit(solution)/shard_map/ppermute | solution.py:20
  19.1 1.4 %collective-permute-start.7 = (f32[32,896]{1,0:T(8,128)S(1)}, f32[32,896]{1,0:T(8,128)S(1)}, u32[]{:S(2)}, u32[]{:S(2)}) collective-permute-start(f32[32,896]{1,0:T(8,128)S(1)} %fusion), channel_id=1, source_target_pairs={{0,1},{1,0},{2,3},{3,2},{4,5},{5,4},{6,7},{7,6},{8,9},{9,8},{10,11... | collective-permute-start | bytes 344072 | tf_op jit(solution)/shard_map/ppermute | solution.py:28
  20.6 4.3 %collective-permute-start.8 = (bf16[4,1,4,896]{3,2,1,0:T(4,128)(2,1)S(1)}, bf16[4,1,4,896]{3,2,1,0:T(4,128)(2,1)S(1)}, u32[]{:S(2)}, u32[]{:S(2)}) collective-permute-start(bf16[4,1,4,896]{3,2,1,0:T(4,128)(2,1)S(1)} %select_bitcast_fusion), channel_id=1, source_target_pairs={{0,9},{1,8},{2,11},{3,10},{4,13},{5,12},{6,15},{7,14},{8,1},{9,0},... | collective-permute-start | bytes 86024 | tf_op jit(solution)/shard_map/ppermute | solution.py:20
  25.0 3.8 %collective-permute-start.9 = (bf16[2,4,896]{2,1,0:T(4,128)(2,1)S(1)}, bf16[2,4,896]{2,1,0:T(4,128)(2,1)S(1)}, u32[]{:S(2)}, u32[]{:S(2)}) collective-permute-start(bf16[2,4,896]{2,1,0:T(4,128)(2,1)S(1)} %get-tuple-element.17), channel_id=1, source_target_pairs={{0,2},{1,7},{2,0},{3,5},{4,6},{5,3},{6,4},{7,1},{8,10},{9,15},{10,... | collective-permute-start | bytes 43016 | tf_op jit(solution)/shard_map/ppermute | solution.py:20
  26.1 3.8 %collective-permute-start.11 = (bf16[2,4,896]{2,1,0:T(4,128)(2,1)S(1)}, bf16[2,4,896]{2,1,0:T(4,128)(2,1)S(1)}, u32[]{:S(2)}, u32[]{:S(2)}) collective-permute-start(bf16[2,4,896]{2,1,0:T(4,128)(2,1)S(1)} %get-tuple-element.18), channel_id=1, source_target_pairs={{0,4},{1,5},{2,6},{3,7},{4,0},{5,1},{6,2},{7,3},{8,12},{9,13},{10,... | collective-permute-start | bytes 43016 | tf_op jit(solution)/shard_map/ppermute | solution.py:20
  28.8 1.2 %collective-permute-start.10 = (bf16[2,4,896]{2,1,0:T(4,128)(2,1)S(1)}, bf16[2,4,896]{2,1,0:T(4,128)(2,1)S(1)}, u32[]{:S(2)}, u32[]{:S(2)}) collective-permute-start(bf16[2,4,896]{2,1,0:T(4,128)(2,1)S(1)} %collective-permute-done.9), channel_id=1, source_target_pairs={{0,1},{1,0},{2,3},{3,2},{4,5},{5,4},{6,7},{7,6},{8,9},{9,8},{10,11... | collective-permute-start | bytes 43016 | tf_op jit(solution)/shard_map/ppermute | solution.py:28

commit v7 on v6

--- a/solution.py
+++ b/solution.py
@@ -70,11 +70,7 @@
     tokens = jnp.stack(by_xor([blocks[index] for index in range(GROUP)], rank))
     mask = GROUP
     while mask < lax.axis_size("ep"):
-        bit = (rank & mask) > 0
-        other = swapped(tokens, same_mask(mask), True)
-        tokens = jnp.concatenate(
-            [jnp.where(bit, other, tokens), jnp.where(bit, tokens, other)], axis=0
-        )
+        tokens = jnp.concatenate([tokens, swapped(tokens, same_mask(mask), True)], axis=0)
         mask *= 2
     return tokens
 
@@ -84,14 +80,10 @@
     held = expert_out[:, None]
     mask = GROUP
     while mask < lax.axis_size("ep"):
-        bit = (rank & mask) > 0
         pairs = held.reshape((-1, 2, GROUP) + held.shape[1:])
-        kept = jnp.where(bit, pairs[:, 1], pairs[:, 0]).reshape((-1,) + held.shape[1:])
-        sent = jnp.where(bit, pairs[:, 0], pairs[:, 1]).reshape((-1,) + held.shape[1:])
-        other = swapped(sent, same_mask(mask), True)
-        held = jnp.concatenate(
-            [jnp.where(bit, other, kept), jnp.where(bit, kept, other)], axis=1
-        )
+        kept = pairs[:, 0].reshape((-1,) + held.shape[1:])
+        sent = pairs[:, 1].reshape((-1,) + held.shape[1:])
+        held = jnp.concatenate([kept, swapped(sent, same_mask(mask), True)], axis=1)
         mask *= 2
     leaving = by_xor([held[index] for index in range(GROUP)], rank)
     upper = lax.axis_index("tp") == 1
@@ -149,15 +141,12 @@
         rows = spread_tokens(hidden).reshape(peer_count * tok_rows, quarter)
         expert_out = expert_rows(rows, w_gate[0], w_up[0], w_down[0])
         returned = return_tokens(expert_out.reshape(peer_count, tok_rows, quarter))
-        combined = jnp.concatenate(
-            [
-                sum(
-                    block[index].astype(jnp.float32) * share[:, index : index + 1]
-                    for index in range(experts)
-                )
-                for block in returned
-            ],
-            axis=1,
+        shares = [share[:, index : index + 1] for index in range(experts)]
+        shares = by_xor(shares, lax.axis_index("ep") // GROUP)
+        combined = sum(
+            jnp.concatenate([block[index] for block in returned], axis=1).astype(jnp.float32)
+            * shares[index]
+            for index in range(experts)
         )
         return combined.astype(jnp.bfloat16)
     capacity = min(tok_rows, 2 * tok_rows * route_count // experts)

time: 30.9 us -> 30.8 us (level)
    convert_element_type x0 -> x1, other arithmetic: none -> 0.7 us  [local(): return combined.astype(jnp.bfloat16)]
    concatenate x2 -> x0, other arithmetic: 0.67 us -> none  [the longest x1 0.63 us: local(): jnp.concatenate([sum((block[index].astype(jnp.float32) * share[:, index:i...]
  transfers between devices with their start and end apart: 12 -> 12, of which waited for: 11 -> 10; matrix products, arithmetic and copies ran while one was open for 8% -> 8% of each run, Pallas kernels for 0% -> 0%
where the time goes in v7:
time: 30.8 us; the launch traced here: 30.6 us
  starting transfers between devices  16.5 us (54%)
  waiting for transfers between devices  9.64 us (31%)
  other arithmetic  3.48 us (11%)
  matrix products  0.67 us (2%)
    ppermute x9, starting transfers between devices, swapped(): return lax.ppermute(value, ('ep', 'tp'), pairs)  15.6 us
    ppermute x9, waiting for transfers between devices, swapped(): return lax.ppermute(value, ('ep', 'tp'), pairs)  8.33 us
    concatenate x1, other arithmetic, expert_rows(): jnp.concatenate([w_gate, w_up], axis=1)  1.68 us
    ppermute x3, waiting for transfers between devices, other_core(): return lax.ppermute(value, 'tp', [(0, 1), (1, 0)])  1.31 us
    ppermute x3, starting transfers between devices, other_core(): return lax.ppermute(value, 'tp', [(0, 1), (1, 0)])  0.98 us
    select_n x6, other arithmetic, by_xor(): jnp.where(bit, blocks[index ^ mask], blocks[index])  0.86 us
    convert_element_type x1, other arithmetic, local(): return combined.astype(jnp.bfloat16)  0.7 us
  transfers between devices with their start and end apart: 12, of which 10 were waited for; matrix products, arithmetic and copies ran while one was open for 8% of the time, Pallas kernels for 0%

profile of v7, /device:TPU:0, one launch (start us, length us, event | category | flops | bytes accessed | tf_op | source)
XLA Modules:
  0.0 30.6 jit_solution(16806240553678330410)
XLA Ops:
  0.0 3.4 %collective-permute-start = (bf16[4,3584]{1,0:T(4,128)(2,1)}, bf16[4,3584]{1,0:T(4,128)(2,1)S(1)}, u32[]{:S(2)}, u32[]{:S(2)}) collective-permute-start(bf16[4,3584]{1,0:T(4,128)(2,1)} %param.6), channel_id=1, source_target_pairs={{0,7},{1,4},{2,5},{3,6},{4,3},{5,0},{6,1},{7,2},{8,15},{9,12},{10,... | collective-permute-start | bytes 86024 | tf_op jit(solution)/shard_map/ppermute | solution.py:20
  3.4 0.8 %collective-permute-start.2 = (bf16[4,3584]{1,0:T(4,128)(2,1)}, bf16[4,3584]{1,0:T(4,128)(2,1)S(1)}, u32[]{:S(2)}, u32[]{:S(2)}) collective-permute-start(bf16[4,3584]{1,0:T(4,128)(2,1)} %param.6), channel_id=1, source_target_pairs={{0,3},{1,2},{2,1},{3,0},{4,7},{5,6},{6,5},{7,4},{8,11},{9,10},{10,... | collective-permute-start | bytes 86024 | tf_op jit(solution)/shard_map/ppermute | solution.py:20
  4.2 0.8 %select_select_fusion = bf16[4,896]{1,0:T(4,128)(2,1)S(1)} fusion(bf16[4,3584]{1,0:T(4,128)(2,1)} %param.6, pred[]{:T(512)S(6)} %gt.7, pred[]{:T(512)S(6)} %gt.6), kind=kLoop, calls=%fused_computation.60 | loop fusion | flops 10752 | bytes 35842 | tf_op jit(solution)/shard_map/jit(_where)/select_n | solution.py:36
  5.2 0.9 %collective-permute-start.1 = (bf16[4,896]{1,0:T(4,128)(2,1)S(1)}, bf16[4,896]{1,0:T(4,128)(2,1)S(1)}, u32[]{:S(2)}, u32[]{:S(2)}) collective-permute-start(bf16[4,896]{1,0:T(4,128)(2,1)S(1)} %fusion.9), channel_id=1, source_target_pairs={{0,1},{1,0},{2,3},{3,2},{4,5},{5,4},{6,7},{7,6},{8,9},{9,8},{10,11... | collective-permute-start | bytes 21512 | tf_op jit(solution)/shard_map/ppermute | solution.py:28
  6.1 1.0 %collective-permute-done.2 = bf16[4,3584]{1,0:T(4,128)(2,1)S(1)} collective-permute-done((bf16[4,3584]{1,0:T(4,128)(2,1)}, bf16[4,3584]{1,0:T(4,128)(2,1)S(1)}, u32[]{:S(2)}, u32[]{:S(2)}) %collective-permute-start.2) | collective-permute-done | bytes 28704 | tf_op jit(solution)/shard_map/ppermute | solution.py:20
  7.3 2.4 %collective-permute-start.3 = (bf16[4,4,896]{2,1,0:T(4,128)(2,1)S(1)}, bf16[4,4,896]{2,1,0:T(4,128)(2,1)S(1)}, u32[]{:S(2)}, u32[]{:S(2)}) collective-permute-start(bf16[4,4,896]{2,1,0:T(4,128)(2,1)S(1)} %pad_maximum_fusion.1), channel_id=1, source_target_pairs={{0,9},{1,8},{2,11},{3,10},{4,13},{5,12},{6,15},{7,14},{8,1},{9,0},... | collective-permute-start | bytes 86024 | tf_op jit(solution)/shard_map/ppermute | solution.py:20
  9.7 1.7 %pad_maximum_fusion = bf16[896,1024]{1,0:T(8,128)(2,1)S(1)} fusion(bf16[896,512]{1,0:T(8,128)(2,1)} %bitcast.65, bf16[896,512]{1,0:T(8,128)(2,1)} %bitcast.66), kind=kLoop, calls=%fused_computation | loop fusion | flops 3670016 | bytes 3670016 | tf_op jit(solution)/shard_map/concatenate | solution.py:115
  11.3 0.2 collective-permute-done.3
  11.7 0.4 %fusion.15 = (bf16[32,1024]{1,0:T(8,128)(2,1)S(1)}, f32[32,1024]{1,0:T(8,128)S(1)}) fusion(bf16[32,896]{1,0:T(8,128)(2,1)S(1)} %reshape.24, bf16[896,1024]{1,0:T(8,128)(2,1)S(1)} %pad_maximum_fusion), kind=kOutput, calls=%fused_computation.76 | convolution fusion | flops 58753024 | bytes 2088960 | tf_op jit(solution)/shard_map/dot_general | solution.py:116
  12.1 2.1 %collective-permute-start.4 = (bf16[32,1024]{1,0:T(8,128)(2,1)S(1)}, bf16[32,1024]{1,0:T(8,128)(2,1)S(1)}, u32[]{:S(2)}, u32[]{:S(2)}) collective-permute-start(bf16[32,1024]{1,0:T(8,128)(2,1)S(1)} %get-tuple-element.55), channel_id=1, source_target_pairs={{0,6},{1,7},{2,4},{3,5},{4,2},{5,3},{6,0},{7,1},{8,14},{9,15},{10,... | collective-permute-start | bytes 196616 | tf_op jit(solution)/shard_map/ppermute | solution.py:20
  14.2 0.4 %collective-permute-start.5 = (bf16[32,1024]{1,0:T(8,128)(2,1)S(1)}, bf16[32,1024]{1,0:T(8,128)(2,1)S(1)}, u32[]{:S(2)}, u32[]{:S(2)}) collective-permute-start(bf16[32,1024]{1,0:T(8,128)(2,1)S(1)} %get-tuple-element.55), channel_id=1, source_target_pairs={{0,4},{1,5},{2,6},{3,7},{4,0},{5,1},{6,2},{7,3},{8,12},{9,13},{10,... | collective-permute-start | bytes 196616 | tf_op jit(solution)/shard_map/ppermute | solution.py:20
  14.5 1.1 %collective-permute-start.6 = (bf16[32,1024]{1,0:T(8,128)(2,1)S(1)}, bf16[32,1024]{1,0:T(8,128)(2,1)S(1)}, u32[]{:S(2)}, u32[]{:S(2)}) collective-permute-start(bf16[32,1024]{1,0:T(8,128)(2,1)S(1)} %get-tuple-element.55), channel_id=1, source_target_pairs={{0,2},{1,3},{2,0},{3,1},{4,6},{5,7},{6,4},{7,5},{8,10},{9,11},{10,... | collective-permute-start | bytes 196616 | tf_op jit(solution)/shard_map/ppermute | solution.py:20
  15.6 2.1 %collective-permute-done.4 = bf16[32,1024]{1,0:T(8,128)(2,1)S(1)} collective-permute-done((bf16[32,1024]{1,0:T(8,128)(2,1)S(1)}, bf16[32,1024]{1,0:T(8,128)(2,1)S(1)}, u32[]{:S(2)}, u32[]{:S(2)}) %collective-permute-start.4) | collective-permute-done | bytes 65568 | tf_op jit(solution)/shard_map/ppermute | solution.py:20
  17.7 0.7 %collective-permute-done.5 = bf16[32,1024]{1,0:T(8,128)(2,1)S(1)} collective-permute-done((bf16[32,1024]{1,0:T(8,128)(2,1)S(1)}, bf16[32,1024]{1,0:T(8,128)(2,1)S(1)}, u32[]{:S(2)}, u32[]{:S(2)}) %collective-permute-start.5) | collective-permute-done | bytes 65568 | tf_op jit(solution)/shard_map/ppermute | solution.py:20
  18.4 0.4 %collective-permute-done.6 = bf16[32,1024]{1,0:T(8,128)(2,1)S(1)} collective-permute-done((bf16[32,1024]{1,0:T(8,128)(2,1)S(1)}, bf16[32,1024]{1,0:T(8,128)(2,1)S(1)}, u32[]{:S(2)}, u32[]{:S(2)}) %collective-permute-start.6) | collective-permute-done | bytes 65568 | tf_op jit(solution)/shard_map/ppermute | solution.py:20
  18.8 0.2 fusion
  19.2 1.3 %collective-permute-done.7 = f32[32,896]{1,0:T(8,128)S(1)} collective-permute-done((f32[32,896]{1,0:T(8,128)S(1)}, f32[32,896]{1,0:T(8,128)S(1)}, u32[]{:S(2)}, u32[]{:S(2)}) %collective-permute-start.7) | collective-permute-done | bytes 114720 | tf_op jit(solution)/shard_map/ppermute | solution.py:28
  20.5 2.5 %collective-permute-start.8 = (bf16[4,1,4,896]{3,2,1,0:T(4,128)(2,1)S(1)}, bf16[4,1,4,896]{3,2,1,0:T(4,128)(2,1)S(1)}, u32[]{:S(2)}, u32[]{:S(2)}) collective-permute-start(bf16[4,1,4,896]{3,2,1,0:T(4,128)(2,1)S(1)} %get-tuple-element.44), channel_id=1, source_target_pairs={{0,9},{1,8},{2,11},{3,10},{4,13},{5,12},{6,15},{7,14},{8,1},{9,0},... | collective-permute-start | bytes 86024 | tf_op jit(solution)/shard_map/ppermute | solution.py:20
  23.1 1.7 %collective-permute-done.8 = bf16[4,1,4,896]{3,2,1,0:T(4,128)(2,1)S(1)} collective-permute-done((bf16[4,1,4,896]{3,2,1,0:T(4,128)(2,1)S(1)}, bf16[4,1,4,896]{3,2,1,0:T(4,128)(2,1)S(1)}, u32[]{:S(2)}, u32[]{:S(2)}) %collective-permute-start.8) | collective-permute-done | bytes 28704 | tf_op jit(solution)/shard_map/ppermute | solution.py:20
  24.9 1.1 %collective-permute-start.9 = (bf16[2,4,896]{2,1,0:T(4,128)(2,1)S(1)}, bf16[2,4,896]{2,1,0:T(4,128)(2,1)S(1)}, u32[]{:S(2)}, u32[]{:S(2)}) collective-permute-start(bf16[2,4,896]{2,1,0:T(4,128)(2,1)S(1)} %get-tuple-element.17), channel_id=1, source_target_pairs={{0,2},{1,7},{2,0},{3,5},{4,6},{5,3},{6,4},{7,1},{8,10},{9,15},{10,... | collective-permute-start | bytes 43016 | tf_op jit(solution)/shard_map/ppermute | solution.py:20
  26.1 1.8 %collective-permute-start.11 = (bf16[2,4,896]{2,1,0:T(4,128)(2,1)S(1)}, bf16[2,4,896]{2,1,0:T(4,128)(2,1)S(1)}, u32[]{:S(2)}, u32[]{:S(2)}) collective-permute-start(bf16[2,4,896]{2,1,0:T(4,128)(2,1)S(1)} %get-tuple-element.18), channel_id=1, source_target_pairs={{0,4},{1,5},{2,6},{3,7},{4,0},{5,1},{6,2},{7,3},{8,12},{9,13},{10,... | collective-permute-start | bytes 43016 | tf_op jit(solution)/shard_map/ppermute | solution.py:20
  27.9 0.8 %collective-permute-done.9 = bf16[2,4,896]{2,1,0:T(4,128)(2,1)S(1)} collective-permute-done((bf16[2,4,896]{2,1,0:T(4,128)(2,1)S(1)}, bf16[2,4,896]{2,1,0:T(4,128)(2,1)S(1)}, u32[]{:S(2)}, u32[]{:S(2)}) %collective-permute-start.9) | collective-permute-done | bytes 14368 | tf_op jit(solution)/shard_map/ppermute | solution.py:20
  28.7 1.1 %collective-permute-done.11 = bf16[2,4,896]{2,1,0:T(4,128)(2,1)S(1)} collective-permute-done((bf16[2,4,896]{2,1,0:T(4,128)(2,1)S(1)}, bf16[2,4,896]{2,1,0:T(4,128)(2,1)S(1)}, u32[]{:S(2)}, u32[]{:S(2)}) %collective-permute-start.11) | collective-permute-done | bytes 14368 | tf_op jit(solution)/shard_map/ppermute | solution.py:20
  29.9 0.7 %add_convert_fusion.1 = bf16[4,3584]{1,0:T(4,128)(2,1)} fusion(bf16[4,896]{1,0:T(4,128)(2,1)S(1)} %get-tuple-element.52, bf16[4,896]{1,0:T(4,128)(2,1)S(1)} %get-tuple-element.57, bf16[4,896]{1,0:T(4,128)(2,1)S(1)} %get-tuple-element.48, bf16[4,896]{1,0:T(4,128)(2,1)S(1)} %get-tuple-element.59, bf16[4,896]{1,0:T(4,128)(2,1)S(1)} %get-tuple-element.51, ...), kind=kLoop, calls=%fused_computation.13 | loop fusion | flops 286720 | bytes 86048 | tf_op jit(solution)/shard_map/convert_element_type | solution.py:151
  (34 shorter events, 0.7 us)
Async XLA Ops:
  0.0 18.8 %copy-start = (bf16[1,512,896]{2,1,0:T(8,128)(2,1)S(1)}, bf16[1,512,896]{2,1,0:T(8,128)(2,1)}, u32[]{:S(2)}) copy-start(bf16[1,512,896]{2,1,0:T(8,128)(2,1)} %param.11) | copy-start | bytes 2752516
  0.0 5.2 %collective-permute-start = (bf16[4,3584]{1,0:T(4,128)(2,1)}, bf16[4,3584]{1,0:T(4,128)(2,1)S(1)}, u32[]{:S(2)}, u32[]{:S(2)}) collective-permute-start(bf16[4,3584]{1,0:T(4,128)(2,1)} %param.6), channel_id=1, source_target_pairs={{0,7},{1,4},{2,5},{3,6},{4,3},{5,0},{6,1},{7,2},{8,15},{9,12},{10,... | collective-permute-start | bytes 86024 | tf_op jit(solution)/shard_map/ppermute | solution.py:20
  3.4 3.7 %collective-permute-start.2 = (bf16[4,3584]{1,0:T(4,128)(2,1)}, bf16[4,3584]{1,0:T(4,128)(2,1)S(1)}, u32[]{:S(2)}, u32[]{:S(2)}) collective-permute-start(bf16[4,3584]{1,0:T(4,128)(2,1)} %param.6), channel_id=1, source_target_pairs={{0,3},{1,2},{2,1},{3,0},{4,7},{5,6},{6,5},{7,4},{8,11},{9,10},{10,... | collective-permute-start | bytes 86024 | tf_op jit(solution)/shard_map/ppermute | solution.py:20
  5.2 2.0 %collective-permute-start.1 = (bf16[4,896]{1,0:T(4,128)(2,1)S(1)}, bf16[4,896]{1,0:T(4,128)(2,1)S(1)}, u32[]{:S(2)}, u32[]{:S(2)}) collective-permute-start(bf16[4,896]{1,0:T(4,128)(2,1)S(1)} %fusion.9), channel_id=1, source_target_pairs={{0,1},{1,0},{2,3},{3,2},{4,5},{5,4},{6,7},{7,6},{8,9},{9,8},{10,11... | collective-permute-start | bytes 21512 | tf_op jit(solution)/shard_map/ppermute | solution.py:28
  7.3 4.3 %collective-permute-start.3 = (bf16[4,4,896]{2,1,0:T(4,128)(2,1)S(1)}, bf16[4,4,896]{2,1,0:T(4,128)(2,1)S(1)}, u32[]{:S(2)}, u32[]{:S(2)}) collective-permute-start(bf16[4,4,896]{2,1,0:T(4,128)(2,1)S(1)} %pad_maximum_fusion.1), channel_id=1, source_target_pairs={{0,9},{1,8},{2,11},{3,10},{4,13},{5,12},{6,15},{7,14},{8,1},{9,0},... | collective-permute-start | bytes 86024 | tf_op jit(solution)/shard_map/ppermute | solution.py:20
  11.6 7.5 %copy-start.1 = (f32[4,2]{0,1:T(2,128)S(1)}, f32[4,2]{0,1:T(2,128)}, u32[]{:S(2)}) copy-start(f32[4,2]{0,1:T(2,128)} %param.8) | copy-start | bytes 100
  11.6 14.4 %copy-start.2 = (s32[4,2]{0,1:T(2,128)S(1)}, s32[4,2]{0,1:T(2,128)}, u32[]{:S(2)}) copy-start(s32[4,2]{0,1:T(2,128)} %param.7) | copy-start | bytes 100
  12.1 5.6 %collective-permute-start.4 = (bf16[32,1024]{1,0:T(8,128)(2,1)S(1)}, bf16[32,1024]{1,0:T(8,128)(2,1)S(1)}, u32[]{:S(2)}, u32[]{:S(2)}) collective-permute-start(bf16[32,1024]{1,0:T(8,128)(2,1)S(1)} %get-tuple-element.55), channel_id=1, source_target_pairs={{0,6},{1,7},{2,4},{3,5},{4,2},{5,3},{6,0},{7,1},{8,14},{9,15},{10,... | collective-permute-start | bytes 196616 | tf_op jit(solution)/shard_map/ppermute | solution.py:20
  14.2 4.3 %collective-permute-start.5 = (bf16[32,1024]{1,0:T(8,128)(2,1)S(1)}, bf16[32,1024]{1,0:T(8,128)(2,1)S(1)}, u32[]{:S(2)}, u32[]{:S(2)}) collective-permute-start(bf16[32,1024]{1,0:T(8,128)(2,1)S(1)} %get-tuple-element.55), channel_id=1, source_target_pairs={{0,4},{1,5},{2,6},{3,7},{4,0},{5,1},{6,2},{7,3},{8,12},{9,13},{10,... | collective-permute-start | bytes 196616 | tf_op jit(solution)/shard_map/ppermute | solution.py:20
  14.5 4.3 %collective-permute-start.6 = (bf16[32,1024]{1,0:T(8,128)(2,1)S(1)}, bf16[32,1024]{1,0:T(8,128)(2,1)S(1)}, u32[]{:S(2)}, u32[]{:S(2)}) collective-permute-start(bf16[32,1024]{1,0:T(8,128)(2,1)S(1)} %get-tuple-element.55), channel_id=1, source_target_pairs={{0,2},{1,3},{2,0},{3,1},{4,6},{5,7},{6,4},{7,5},{8,10},{9,11},{10,... | collective-permute-start | bytes 196616 | tf_op jit(solution)/shard_map/ppermute | solution.py:20
  19.1 1.4 %collective-permute-start.7 = (f32[32,896]{1,0:T(8,128)S(1)}, f32[32,896]{1,0:T(8,128)S(1)}, u32[]{:S(2)}, u32[]{:S(2)}) collective-permute-start(f32[32,896]{1,0:T(8,128)S(1)} %fusion), channel_id=1, source_target_pairs={{0,1},{1,0},{2,3},{3,2},{4,5},{5,4},{6,7},{7,6},{8,9},{9,8},{10,11... | collective-permute-start | bytes 344072 | tf_op jit(solution)/shard_map/ppermute | solution.py:28
  20.5 4.3 %collective-permute-start.8 = (bf16[4,1,4,896]{3,2,1,0:T(4,128)(2,1)S(1)}, bf16[4,1,4,896]{3,2,1,0:T(4,128)(2,1)S(1)}, u32[]{:S(2)}, u32[]{:S(2)}) collective-permute-start(bf16[4,1,4,896]{3,2,1,0:T(4,128)(2,1)S(1)} %get-tuple-element.44), channel_id=1, source_target_pairs={{0,9},{1,8},{2,11},{3,10},{4,13},{5,12},{6,15},{7,14},{8,1},{9,0},... | collective-permute-start | bytes 86024 | tf_op jit(solution)/shard_map/ppermute | solution.py:20
  24.9 3.8 %collective-permute-start.9 = (bf16[2,4,896]{2,1,0:T(4,128)(2,1)S(1)}, bf16[2,4,896]{2,1,0:T(4,128)(2,1)S(1)}, u32[]{:S(2)}, u32[]{:S(2)}) collective-permute-start(bf16[2,4,896]{2,1,0:T(4,128)(2,1)S(1)} %get-tuple-element.17), channel_id=1, source_target_pairs={{0,2},{1,7},{2,0},{3,5},{4,6},{5,3},{6,4},{7,1},{8,10},{9,15},{10,... | collective-permute-start | bytes 43016 | tf_op jit(solution)/shard_map/ppermute | solution.py:20
  26.1 3.8 %collective-permute-start.11 = (bf16[2,4,896]{2,1,0:T(4,128)(2,1)S(1)}, bf16[2,4,896]{2,1,0:T(4,128)(2,1)S(1)}, u32[]{:S(2)}, u32[]{:S(2)}) collective-permute-start(bf16[2,4,896]{2,1,0:T(4,128)(2,1)S(1)} %get-tuple-element.18), channel_id=1, source_target_pairs={{0,4},{1,5},{2,6},{3,7},{4,0},{5,1},{6,2},{7,3},{8,12},{9,13},{10,... | collective-permute-start | bytes 43016 | tf_op jit(solution)/shard_map/ppermute | solution.py:20
  28.7 1.2 %collective-permute-start.10 = (bf16[2,4,896]{2,1,0:T(4,128)(2,1)S(1)}, bf16[2,4,896]{2,1,0:T(4,128)(2,1)S(1)}, u32[]{:S(2)}, u32[]{:S(2)}) collective-permute-start(bf16[2,4,896]{2,1,0:T(4,128)(2,1)S(1)} %collective-permute-done.9), channel_id=1, source_target_pairs={{0,1},{1,0},{2,3},{3,2},{4,5},{5,4},{6,7},{7,6},{8,9},{9,8},{10,11... | collective-permute-start | bytes 43016 | tf_op jit(solution)/shard_map/ppermute | solution.py:28

commit v8 on v7

--- a/solution.py
+++ b/solution.py
@@ -75,10 +75,17 @@
     return tokens
 
 
-def return_tokens(expert_out):
+def return_tokens(near, far):
     rank = lax.axis_index("ep")
-    held = expert_out[:, None]
+    held = near[:, None]
     mask = GROUP
+    if mask * 2 == lax.axis_size("ep"):
+        other = swapped(far[:, None], same_mask(mask), True)
+        other, held = lax.optimization_barrier((other, held))
+        held = jnp.concatenate([held, other], axis=1)
+        mask *= 2
+    else:
+        held = jnp.concatenate([near, far])[:, None]
     while mask < lax.axis_size("ep"):
         pairs = held.reshape((-1, 2, GROUP) + held.shape[1:])
         kept = pairs[:, 0].reshape((-1,) + held.shape[1:])
@@ -110,7 +117,7 @@
     return (expert_float, slot_hot.reshape(tok_rows, route_count, capacity))
 
 
-def expert_rows(rows, w_gate, w_up, w_down):
+def expert_rows(rows, w_gate, w_up, w_down, groups=0):
     hidden_units = w_gate.shape[1]
     weights_in = lax.optimization_barrier(jnp.concatenate([w_gate, w_up], axis=1))
     parts = jnp.dot(rows, weights_in, preferred_element_type=jnp.float32)
@@ -122,7 +129,14 @@
         jnp.bfloat16
     )
     partial_out = jnp.dot(inner_rows, w_down, preferred_element_type=jnp.float32)
-    return (partial_out + other_core(partial_out)).astype(jnp.bfloat16)
+    if not groups:
+        return (partial_out + other_core(partial_out)).astype(jnp.bfloat16)
+    own_rows = partial_out.shape[0] // groups
+    near, far = partial_out[:own_rows], partial_out[own_rows:]
+    near, far = lax.optimization_barrier((near, far))
+    far_sum = (far + other_core(far)).astype(jnp.bfloat16)
+    near_sum = (near + other_core(near)).astype(jnp.bfloat16)
+    return near_sum, far_sum
 
 
 def local(hidden, expert_ids, gate_scores, w_gate, w_up, w_down):
@@ -139,8 +153,10 @@
         named = expert_ids[:, :, None] == jnp.arange(experts, dtype=jnp.int32)
         share = jnp.sum(jnp.where(named, routing[:, :, None], 0.0), axis=1)
         rows = spread_tokens(hidden).reshape(peer_count * tok_rows, quarter)
-        expert_out = expert_rows(rows, w_gate[0], w_up[0], w_down[0])
-        returned = return_tokens(expert_out.reshape(peer_count, tok_rows, quarter))
+        near, far = expert_rows(rows, w_gate[0], w_up[0], w_down[0], experts)
+        returned = return_tokens(
+            near.reshape(-1, tok_rows, quarter), far.reshape(-1, tok_rows, quarter)
+        )
         shares = [share[:, index : index + 1] for index in range(experts)]
         shares = by_xor(shares, lax.axis_index("ep") // GROUP)
         combined = sum(

time: 30.8 us -> 30.8 us (level)
  waiting for transfers between devices: 9.64 us -> 9.04 us
  starting transfers between devices: 16.5 us -> 17 us
    ppermute x3 -> x4, waiting for transfers between devices: 1.31 us -> 0.77 us  [other_core(): return lax.ppermute(value, 'tp', [(0, 1), (1, 0)])]
    ppermute x3 -> x4, starting transfers between devices: 0.98 us -> 1.48 us  [other_core(): return lax.ppermute(value, 'tp', [(0, 1), (1, 0)])]
  transfers between devices with their start and end apart: 12 -> 13, of which waited for: 10 -> 10; matrix products, arithmetic and copies ran while one was open for 8% -> 8% of each run, Pallas kernels for 0% -> 0%
where the time goes in v8:
time: 30.8 us; the launch traced here: 30.6 us
  starting transfers between devices  17 us (55%)
  waiting for transfers between devices  9.04 us (29%)
  other arithmetic  3.48 us (11%)
  matrix products  0.67 us (2%)
    ppermute x9, starting transfers between devices, swapped(): return lax.ppermute(value, ('ep', 'tp'), pairs)  15.6 us
    ppermute x9, waiting for transfers between devices, swapped(): return lax.ppermute(value, ('ep', 'tp'), pairs)  8.27 us
    concatenate x1, other arithmetic, expert_rows(): jnp.concatenate([w_gate, w_up], axis=1)  1.68 us
    ppermute x4, starting transfers between devices, other_core(): return lax.ppermute(value, 'tp', [(0, 1), (1, 0)])  1.48 us
    select_n x6, other arithmetic, by_xor(): jnp.where(bit, blocks[index ^ mask], blocks[index])  0.86 us
    ppermute x4, waiting for transfers between devices, other_core(): return lax.ppermute(value, 'tp', [(0, 1), (1, 0)])  0.77 us
    convert_element_type x1, other arithmetic, local(): return combined.astype(jnp.bfloat16)  0.7 us
  transfers between devices with their start and end apart: 13, of which 10 were waited for; matrix products, arithmetic and copies ran while one was open for 8% of the time, Pallas kernels for 0%

profile of v8, /device:TPU:0, one launch (start us, length us, event | category | flops | bytes accessed | tf_op | source)
XLA Modules:
  0.0 30.6 jit_solution(10124651200234692265)
XLA Ops:
  0.0 3.4 %collective-permute-start = (bf16[4,3584]{1,0:T(4,128)(2,1)}, bf16[4,3584]{1,0:T(4,128)(2,1)S(1)}, u32[]{:S(2)}, u32[]{:S(2)}) collective-permute-start(bf16[4,3584]{1,0:T(4,128)(2,1)} %param.6), channel_id=1, source_target_pairs={{0,7},{1,4},{2,5},{3,6},{4,3},{5,0},{6,1},{7,2},{8,15},{9,12},{10,... | collective-permute-start | bytes 86024 | tf_op jit(solution)/shard_map/ppermute | solution.py:20
  3.4 0.8 %collective-permute-start.2 = (bf16[4,3584]{1,0:T(4,128)(2,1)}, bf16[4,3584]{1,0:T(4,128)(2,1)S(1)}, u32[]{:S(2)}, u32[]{:S(2)}) collective-permute-start(bf16[4,3584]{1,0:T(4,128)(2,1)} %param.6), channel_id=1, source_target_pairs={{0,3},{1,2},{2,1},{3,0},{4,7},{5,6},{6,5},{7,4},{8,11},{9,10},{10,... | collective-permute-start | bytes 86024 | tf_op jit(solution)/shard_map/ppermute | solution.py:20
  4.2 0.8 %select_select_fusion = bf16[4,896]{1,0:T(4,128)(2,1)S(1)} fusion(bf16[4,3584]{1,0:T(4,128)(2,1)} %param.6, pred[]{:T(512)S(6)} %gt.7, pred[]{:T(512)S(6)} %gt.6), kind=kLoop, calls=%fused_computation.59 | loop fusion | flops 10752 | bytes 35842 | tf_op jit(solution)/shard_map/jit(_where)/select_n | solution.py:36
  5.2 0.9 %collective-permute-start.1 = (bf16[4,896]{1,0:T(4,128)(2,1)S(1)}, bf16[4,896]{1,0:T(4,128)(2,1)S(1)}, u32[]{:S(2)}, u32[]{:S(2)}) collective-permute-start(bf16[4,896]{1,0:T(4,128)(2,1)S(1)} %fusion.9), channel_id=1, source_target_pairs={{0,1},{1,0},{2,3},{3,2},{4,5},{5,4},{6,7},{7,6},{8,9},{9,8},{10,11... | collective-permute-start | bytes 21512 | tf_op jit(solution)/shard_map/ppermute | solution.py:28
  6.1 1.0 %collective-permute-done.2 = bf16[4,3584]{1,0:T(4,128)(2,1)S(1)} collective-permute-done((bf16[4,3584]{1,0:T(4,128)(2,1)}, bf16[4,3584]{1,0:T(4,128)(2,1)S(1)}, u32[]{:S(2)}, u32[]{:S(2)}) %collective-permute-start.2) | collective-permute-done | bytes 28704 | tf_op jit(solution)/shard_map/ppermute | solution.py:20
  7.3 2.4 %collective-permute-start.3 = (bf16[4,4,896]{2,1,0:T(4,128)(2,1)S(1)}, bf16[4,4,896]{2,1,0:T(4,128)(2,1)S(1)}, u32[]{:S(2)}, u32[]{:S(2)}) collective-permute-start(bf16[4,4,896]{2,1,0:T(4,128)(2,1)S(1)} %pad_maximum_fusion.1), channel_id=1, source_target_pairs={{0,9},{1,8},{2,11},{3,10},{4,13},{5,12},{6,15},{7,14},{8,1},{9,0},... | collective-permute-start | bytes 86024 | tf_op jit(solution)/shard_map/ppermute | solution.py:20
  9.7 1.7 %pad_maximum_fusion = bf16[896,1024]{1,0:T(8,128)(2,1)S(1)} fusion(bf16[896,512]{1,0:T(8,128)(2,1)} %bitcast.61, bf16[896,512]{1,0:T(8,128)(2,1)} %bitcast.62), kind=kLoop, calls=%fused_computation | loop fusion | flops 3670016 | bytes 3670016 | tf_op jit(solution)/shard_map/concatenate | solution.py:122
  11.6 0.4 %fusion.16 = (bf16[32,1024]{1,0:T(8,128)(2,1)S(1)}, f32[32,1024]{1,0:T(8,128)S(1)}) fusion(bf16[32,896]{1,0:T(8,128)(2,1)S(1)} %reshape.24, bf16[896,1024]{1,0:T(8,128)(2,1)S(1)} %pad_maximum_fusion), kind=kOutput, calls=%fused_computation.76 | convolution fusion | flops 58753024 | bytes 2088960 | tf_op jit(solution)/shard_map/dot_general | solution.py:123
  12.1 2.1 %collective-permute-start.4 = (bf16[32,1024]{1,0:T(8,128)(2,1)S(1)}, bf16[32,1024]{1,0:T(8,128)(2,1)S(1)}, u32[]{:S(2)}, u32[]{:S(2)}) collective-permute-start(bf16[32,1024]{1,0:T(8,128)(2,1)S(1)} %get-tuple-element.63), channel_id=1, source_target_pairs={{0,6},{1,7},{2,4},{3,5},{4,2},{5,3},{6,0},{7,1},{8,14},{9,15},{10,... | collective-permute-start | bytes 196616 | tf_op jit(solution)/shard_map/ppermute | solution.py:20
  14.2 0.4 %collective-permute-start.5 = (bf16[32,1024]{1,0:T(8,128)(2,1)S(1)}, bf16[32,1024]{1,0:T(8,128)(2,1)S(1)}, u32[]{:S(2)}, u32[]{:S(2)}) collective-permute-start(bf16[32,1024]{1,0:T(8,128)(2,1)S(1)} %get-tuple-element.63), channel_id=1, source_target_pairs={{0,4},{1,5},{2,6},{3,7},{4,0},{5,1},{6,2},{7,3},{8,12},{9,13},{10,... | collective-permute-start | bytes 196616 | tf_op jit(solution)/shard_map/ppermute | solution.py:20
  14.5 1.1 %collective-permute-start.6 = (bf16[32,1024]{1,0:T(8,128)(2,1)S(1)}, bf16[32,1024]{1,0:T(8,128)(2,1)S(1)}, u32[]{:S(2)}, u32[]{:S(2)}) collective-permute-start(bf16[32,1024]{1,0:T(8,128)(2,1)S(1)} %get-tuple-element.63), channel_id=1, source_target_pairs={{0,2},{1,3},{2,0},{3,1},{4,6},{5,7},{6,4},{7,5},{8,10},{9,11},{10,... | collective-permute-start | bytes 196616 | tf_op jit(solution)/shard_map/ppermute | solution.py:20
  15.6 2.1 %collective-permute-done.4 = bf16[32,1024]{1,0:T(8,128)(2,1)S(1)} collective-permute-done((bf16[32,1024]{1,0:T(8,128)(2,1)S(1)}, bf16[32,1024]{1,0:T(8,128)(2,1)S(1)}, u32[]{:S(2)}, u32[]{:S(2)}) %collective-permute-start.4) | collective-permute-done | bytes 65568 | tf_op jit(solution)/shard_map/ppermute | solution.py:20
  17.7 0.7 %collective-permute-done.5 = bf16[32,1024]{1,0:T(8,128)(2,1)S(1)} collective-permute-done((bf16[32,1024]{1,0:T(8,128)(2,1)S(1)}, bf16[32,1024]{1,0:T(8,128)(2,1)S(1)}, u32[]{:S(2)}, u32[]{:S(2)}) %collective-permute-start.5) | collective-permute-done | bytes 65568 | tf_op jit(solution)/shard_map/ppermute | solution.py:20
  18.4 0.4 %collective-permute-done.6 = bf16[32,1024]{1,0:T(8,128)(2,1)S(1)} collective-permute-done((bf16[32,1024]{1,0:T(8,128)(2,1)S(1)}, bf16[32,1024]{1,0:T(8,128)(2,1)S(1)}, u32[]{:S(2)}, u32[]{:S(2)}) %collective-permute-start.6) | collective-permute-done | bytes 65568 | tf_op jit(solution)/shard_map/ppermute | solution.py:20
  18.8 0.2 fusion
  19.2 0.5 %collective-permute-start.9 = (f32[16,896]{1,0:T(8,128)S(1)}, f32[16,896]{1,0:T(8,128)S(1)}, u32[]{:S(2)}, u32[]{:S(2)}) collective-permute-start(f32[16,896]{1,0:T(8,128)S(1)} %get-tuple-element.22), channel_id=1, source_target_pairs={{0,1},{1,0},{2,3},{3,2},{4,5},{5,4},{6,7},{7,6},{8,9},{9,8},{10,11... | collective-permute-start | bytes 172040 | tf_op jit(solution)/shard_map/ppermute | solution.py:28
  19.7 0.7 %collective-permute-done.7 = f32[16,896]{1,0:T(8,128)S(1)} collective-permute-done((f32[16,896]{1,0:T(8,128)S(1)}, f32[16,896]{1,0:T(8,128)S(1)}, u32[]{:S(2)}, u32[]{:S(2)}) %collective-permute-start.7) | collective-permute-done | bytes 57376 | tf_op jit(solution)/shard_map/ppermute | solution.py:28
  20.5 2.5 %collective-permute-start.8 = (bf16[4,1,4,896]{3,2,1,0:T(4,128)(2,1)S(1)}, bf16[4,1,4,896]{3,2,1,0:T(4,128)(2,1)S(1)}, u32[]{:S(2)}, u32[]{:S(2)}) collective-permute-start(bf16[4,1,4,896]{3,2,1,0:T(4,128)(2,1)S(1)} %bitcast.73), channel_id=1, source_target_pairs={{0,9},{1,8},{2,11},{3,10},{4,13},{5,12},{6,15},{7,14},{8,1},{9,0},... | collective-permute-start | bytes 86024 | tf_op jit(solution)/shard_map/ppermute | solution.py:20
  23.0 1.7 %collective-permute-done.8 = bf16[4,1,4,896]{3,2,1,0:T(4,128)(2,1)S(1)} collective-permute-done((bf16[4,1,4,896]{3,2,1,0:T(4,128)(2,1)S(1)}, bf16[4,1,4,896]{3,2,1,0:T(4,128)(2,1)S(1)}, u32[]{:S(2)}, u32[]{:S(2)}) %collective-permute-start.8) | collective-permute-done | bytes 28704 | tf_op jit(solution)/shard_map/ppermute | solution.py:20
  24.8 1.1 %collective-permute-start.10 = (bf16[2,4,896]{2,1,0:T(4,128)(2,1)S(1)}, bf16[2,4,896]{2,1,0:T(4,128)(2,1)S(1)}, u32[]{:S(2)}, u32[]{:S(2)}) collective-permute-start(bf16[2,4,896]{2,1,0:T(4,128)(2,1)S(1)} %get-tuple-element.25), channel_id=1, source_target_pairs={{0,2},{1,7},{2,0},{3,5},{4,6},{5,3},{6,4},{7,1},{8,10},{9,15},{10,... | collective-permute-start | bytes 43016 | tf_op jit(solution)/shard_map/ppermute | solution.py:20
  26.0 1.8 %collective-permute-start.12 = (bf16[2,4,896]{2,1,0:T(4,128)(2,1)S(1)}, bf16[2,4,896]{2,1,0:T(4,128)(2,1)S(1)}, u32[]{:S(2)}, u32[]{:S(2)}) collective-permute-start(bf16[2,4,896]{2,1,0:T(4,128)(2,1)S(1)} %get-tuple-element.26), channel_id=1, source_target_pairs={{0,4},{1,5},{2,6},{3,7},{4,0},{5,1},{6,2},{7,3},{8,12},{9,13},{10,... | collective-permute-start | bytes 43016 | tf_op jit(solution)/shard_map/ppermute | solution.py:20
  27.8 0.8 %collective-permute-done.10 = bf16[2,4,896]{2,1,0:T(4,128)(2,1)S(1)} collective-permute-done((bf16[2,4,896]{2,1,0:T(4,128)(2,1)S(1)}, bf16[2,4,896]{2,1,0:T(4,128)(2,1)S(1)}, u32[]{:S(2)}, u32[]{:S(2)}) %collective-permute-start.10) | collective-permute-done | bytes 14368 | tf_op jit(solution)/shard_map/ppermute | solution.py:20
  28.6 1.1 %collective-permute-done.12 = bf16[2,4,896]{2,1,0:T(4,128)(2,1)S(1)} collective-permute-done((bf16[2,4,896]{2,1,0:T(4,128)(2,1)S(1)}, bf16[2,4,896]{2,1,0:T(4,128)(2,1)S(1)}, u32[]{:S(2)}, u32[]{:S(2)}) %collective-permute-start.12) | collective-permute-done | bytes 14368 | tf_op jit(solution)/shard_map/ppermute | solution.py:20
  29.9 0.7 %add_convert_fusion = bf16[4,3584]{1,0:T(4,128)(2,1)} fusion(bf16[4,896]{1,0:T(4,128)(2,1)S(1)} %get-tuple-element.60, bf16[4,896]{1,0:T(4,128)(2,1)S(1)} %get-tuple-element.65, bf16[4,896]{1,0:T(4,128)(2,1)S(1)} %get-tuple-element.56, bf16[4,896]{1,0:T(4,128)(2,1)S(1)} %get-tuple-element.67, bf16[4,896]{1,0:T(4,128)(2,1)S(1)} %get-tuple-element.59, ...), kind=kLoop, calls=%fused_computation.12 | loop fusion | flops 286720 | bytes 86048 | tf_op jit(solution)/shard_map/convert_element_type | solution.py:167
  (38 shorter events, 1.0 us)
Async XLA Ops:
  0.0 18.8 %copy-start = (bf16[1,512,896]{2,1,0:T(8,128)(2,1)S(1)}, bf16[1,512,896]{2,1,0:T(8,128)(2,1)}, u32[]{:S(2)}) copy-start(bf16[1,512,896]{2,1,0:T(8,128)(2,1)} %param.11) | copy-start | bytes 2752516
  0.0 5.2 %collective-permute-start = (bf16[4,3584]{1,0:T(4,128)(2,1)}, bf16[4,3584]{1,0:T(4,128)(2,1)S(1)}, u32[]{:S(2)}, u32[]{:S(2)}) collective-permute-start(bf16[4,3584]{1,0:T(4,128)(2,1)} %param.6), channel_id=1, source_target_pairs={{0,7},{1,4},{2,5},{3,6},{4,3},{5,0},{6,1},{7,2},{8,15},{9,12},{10,... | collective-permute-start | bytes 86024 | tf_op jit(solution)/shard_map/ppermute | solution.py:20
  3.4 3.7 %collective-permute-start.2 = (bf16[4,3584]{1,0:T(4,128)(2,1)}, bf16[4,3584]{1,0:T(4,128)(2,1)S(1)}, u32[]{:S(2)}, u32[]{:S(2)}) collective-permute-start(bf16[4,3584]{1,0:T(4,128)(2,1)} %param.6), channel_id=1, source_target_pairs={{0,3},{1,2},{2,1},{3,0},{4,7},{5,6},{6,5},{7,4},{8,11},{9,10},{10,... | collective-permute-start | bytes 86024 | tf_op jit(solution)/shard_map/ppermute | solution.py:20
  5.2 2.0 %collective-permute-start.1 = (bf16[4,896]{1,0:T(4,128)(2,1)S(1)}, bf16[4,896]{1,0:T(4,128)(2,1)S(1)}, u32[]{:S(2)}, u32[]{:S(2)}) collective-permute-start(bf16[4,896]{1,0:T(4,128)(2,1)S(1)} %fusion.9), channel_id=1, source_target_pairs={{0,1},{1,0},{2,3},{3,2},{4,5},{5,4},{6,7},{7,6},{8,9},{9,8},{10,11... | collective-permute-start | bytes 21512 | tf_op jit(solution)/shard_map/ppermute | solution.py:28
  7.3 4.3 %collective-permute-start.3 = (bf16[4,4,896]{2,1,0:T(4,128)(2,1)S(1)}, bf16[4,4,896]{2,1,0:T(4,128)(2,1)S(1)}, u32[]{:S(2)}, u32[]{:S(2)}) collective-permute-start(bf16[4,4,896]{2,1,0:T(4,128)(2,1)S(1)} %pad_maximum_fusion.1), channel_id=1, source_target_pairs={{0,9},{1,8},{2,11},{3,10},{4,13},{5,12},{6,15},{7,14},{8,1},{9,0},... | collective-permute-start | bytes 86024 | tf_op jit(solution)/shard_map/ppermute | solution.py:20
  11.3 4.2 %copy-start.1 = (f32[4,2]{0,1:T(2,128)S(1)}, f32[4,2]{0,1:T(2,128)}, u32[]{:S(2)}) copy-start(f32[4,2]{0,1:T(2,128)} %param.8) | copy-start | bytes 100
  11.6 14.3 %copy-start.2 = (s32[4,2]{0,1:T(2,128)S(1)}, s32[4,2]{0,1:T(2,128)}, u32[]{:S(2)}) copy-start(s32[4,2]{0,1:T(2,128)} %param.7) | copy-start | bytes 100
  12.1 5.6 %collective-permute-start.4 = (bf16[32,1024]{1,0:T(8,128)(2,1)S(1)}, bf16[32,1024]{1,0:T(8,128)(2,1)S(1)}, u32[]{:S(2)}, u32[]{:S(2)}) collective-permute-start(bf16[32,1024]{1,0:T(8,128)(2,1)S(1)} %get-tuple-element.63), channel_id=1, source_target_pairs={{0,6},{1,7},{2,4},{3,5},{4,2},{5,3},{6,0},{7,1},{8,14},{9,15},{10,... | collective-permute-start | bytes 196616 | tf_op jit(solution)/shard_map/ppermute | solution.py:20
  14.2 4.3 %collective-permute-start.5 = (bf16[32,1024]{1,0:T(8,128)(2,1)S(1)}, bf16[32,1024]{1,0:T(8,128)(2,1)S(1)}, u32[]{:S(2)}, u32[]{:S(2)}) collective-permute-start(bf16[32,1024]{1,0:T(8,128)(2,1)S(1)} %get-tuple-element.63), channel_id=1, source_target_pairs={{0,4},{1,5},{2,6},{3,7},{4,0},{5,1},{6,2},{7,3},{8,12},{9,13},{10,... | collective-permute-start | bytes 196616 | tf_op jit(solution)/shard_map/ppermute | solution.py:20
  14.5 4.3 %collective-permute-start.6 = (bf16[32,1024]{1,0:T(8,128)(2,1)S(1)}, bf16[32,1024]{1,0:T(8,128)(2,1)S(1)}, u32[]{:S(2)}, u32[]{:S(2)}) collective-permute-start(bf16[32,1024]{1,0:T(8,128)(2,1)S(1)} %get-tuple-element.63), channel_id=1, source_target_pairs={{0,2},{1,3},{2,0},{3,1},{4,6},{5,7},{6,4},{7,5},{8,10},{9,11},{10,... | collective-permute-start | bytes 196616 | tf_op jit(solution)/shard_map/ppermute | solution.py:20
  19.1 1.3 %collective-permute-start.7 = (f32[16,896]{1,0:T(8,128)S(1)}, f32[16,896]{1,0:T(8,128)S(1)}, u32[]{:S(2)}, u32[]{:S(2)}) collective-permute-start(f32[16,896]{1,0:T(8,128)S(1)} %get-tuple-element.21), channel_id=1, source_target_pairs={{0,1},{1,0},{2,3},{3,2},{4,5},{5,4},{6,7},{7,6},{8,9},{9,8},{10,11... | collective-permute-start | bytes 172040 | tf_op jit(solution)/shard_map/ppermute | solution.py:28
  19.2 3.8 %collective-permute-start.9 = (f32[16,896]{1,0:T(8,128)S(1)}, f32[16,896]{1,0:T(8,128)S(1)}, u32[]{:S(2)}, u32[]{:S(2)}) collective-permute-start(f32[16,896]{1,0:T(8,128)S(1)} %get-tuple-element.22), channel_id=1, source_target_pairs={{0,1},{1,0},{2,3},{3,2},{4,5},{5,4},{6,7},{7,6},{8,9},{9,8},{10,11... | collective-permute-start | bytes 172040 | tf_op jit(solution)/shard_map/ppermute | solution.py:28
  20.5 4.3 %collective-permute-start.8 = (bf16[4,1,4,896]{3,2,1,0:T(4,128)(2,1)S(1)}, bf16[4,1,4,896]{3,2,1,0:T(4,128)(2,1)S(1)}, u32[]{:S(2)}, u32[]{:S(2)}) collective-permute-start(bf16[4,1,4,896]{3,2,1,0:T(4,128)(2,1)S(1)} %bitcast.73), channel_id=1, source_target_pairs={{0,9},{1,8},{2,11},{3,10},{4,13},{5,12},{6,15},{7,14},{8,1},{9,0},... | collective-permute-start | bytes 86024 | tf_op jit(solution)/shard_map/ppermute | solution.py:20
  24.8 3.8 %collective-permute-start.10 = (bf16[2,4,896]{2,1,0:T(4,128)(2,1)S(1)}, bf16[2,4,896]{2,1,0:T(4,128)(2,1)S(1)}, u32[]{:S(2)}, u32[]{:S(2)}) collective-permute-start(bf16[2,4,896]{2,1,0:T(4,128)(2,1)S(1)} %get-tuple-element.25), channel_id=1, source_target_pairs={{0,2},{1,7},{2,0},{3,5},{4,6},{5,3},{6,4},{7,1},{8,10},{9,15},{10,... | collective-permute-start | bytes 43016 | tf_op jit(solution)/shard_map/ppermute | solution.py:20
  26.0 3.8 %collective-permute-start.12 = (bf16[2,4,896]{2,1,0:T(4,128)(2,1)S(1)}, bf16[2,4,896]{2,1,0:T(4,128)(2,1)S(1)}, u32[]{:S(2)}, u32[]{:S(2)}) collective-permute-start(bf16[2,4,896]{2,1,0:T(4,128)(2,1)S(1)} %get-tuple-element.26), channel_id=1, source_target_pairs={{0,4},{1,5},{2,6},{3,7},{4,0},{5,1},{6,2},{7,3},{8,12},{9,13},{10,... | collective-permute-start | bytes 43016 | tf_op jit(solution)/shard_map/ppermute | solution.py:20
  28.6 1.2 %collective-permute-start.11 = (bf16[2,4,896]{2,1,0:T(4,128)(2,1)S(1)}, bf16[2,4,896]{2,1,0:T(4,128)(2,1)S(1)}, u32[]{:S(2)}, u32[]{:S(2)}) collective-permute-start(bf16[2,4,896]{2,1,0:T(4,128)(2,1)S(1)} %collective-permute-done.10), channel_id=1, source_target_pairs={{0,1},{1,0},{2,3},{3,2},{4,5},{5,4},{6,7},{7,6},{8,9},{9,8},{10,11... | collective-permute-start | bytes 43016 | tf_op jit(solution)/shard_map/ppermute | solution.py:28

commit v9 on v8

--- a/solution.py
+++ b/solution.py
@@ -65,7 +65,7 @@
     def own_quarter(rows):
         return by_xor(quarters_of(rows), rank)[0]
 
-    blocks = gathered(hidden, [3, 2], True, hidden, True, own_quarter)
+    blocks = gathered(hidden, [3, 1], True, hidden, True, own_quarter)
     blocks[0] = lax.optimization_barrier(own_quarter(hidden))
     tokens = jnp.stack(by_xor([blocks[index] for index in range(GROUP)], rank))
     mask = GROUP

time: 30.8 us -> 30.7 us (level)
  waiting for transfers between devices: 9.04 us -> 9.38 us
    ppermute x9, waiting for transfers between devices: 8.27 us -> 8.58 us  [swapped(): return lax.ppermute(value, ('ep', 'tp'), pairs)]
  transfers between devices with their start and end apart: 13 -> 13, of which waited for: 10 -> 11; matrix products, arithmetic and copies ran while one was open for 8% -> 8% of each run, Pallas kernels for 0% -> 0%
where the time goes in v9:
time: 30.7 us; the launch traced here: 30.5 us
  starting transfers between devices  16.7 us (54%)
  waiting for transfers between devices  9.38 us (31%)
  other arithmetic  3.48 us (11%)
  matrix products  0.67 us (2%)
    ppermute x9, starting transfers between devices, swapped(): return lax.ppermute(value, ('ep', 'tp'), pairs)  15.4 us
    ppermute x9, waiting for transfers between devices, swapped(): return lax.ppermute(value, ('ep', 'tp'), pairs)  8.58 us
    concatenate x1, other arithmetic, expert_rows(): jnp.concatenate([w_gate, w_up], axis=1)  1.68 us
    ppermute x4, starting transfers between devices, other_core(): return lax.ppermute(value, 'tp', [(0, 1), (1, 0)])  1.29 us
    select_n x6, other arithmetic, by_xor(): jnp.where(bit, blocks[index ^ mask], blocks[index])  0.86 us
    ppermute x4, waiting for transfers between devices, other_core(): return lax.ppermute(value, 'tp', [(0, 1), (1, 0)])  0.8 us
    convert_element_type x1, other arithmetic, local(): return combined.astype(jnp.bfloat16)  0.7 us
  transfers between devices with their start and end apart: 13, of which 11 were waited for; matrix products, arithmetic and copies ran while one was open for 8% of the time, Pallas kernels for 0%

profile of v9, /device:TPU:0, one launch (start us, length us, event | category | flops | bytes accessed | tf_op | source)
XLA Modules:
  0.0 30.5 jit_solution(4920942156454325742)
XLA Ops:
  0.0 3.4 %collective-permute-start = (bf16[4,3584]{1,0:T(4,128)(2,1)}, bf16[4,3584]{1,0:T(4,128)(2,1)S(1)}, u32[]{:S(2)}, u32[]{:S(2)}) collective-permute-start(bf16[4,3584]{1,0:T(4,128)(2,1)} %param.6), channel_id=1, source_target_pairs={{0,7},{1,2},{2,5},{3,0},{4,3},{5,6},{6,1},{7,4},{8,15},{9,10},{10,... | collective-permute-start | bytes 86024 | tf_op jit(solution)/shard_map/ppermute | solution.py:20
  3.4 0.8 %collective-permute-start.2 = (bf16[4,3584]{1,0:T(4,128)(2,1)}, bf16[4,3584]{1,0:T(4,128)(2,1)S(1)}, u32[]{:S(2)}, u32[]{:S(2)}) collective-permute-start(bf16[4,3584]{1,0:T(4,128)(2,1)} %param.6), channel_id=1, source_target_pairs={{0,5},{1,4},{2,7},{3,6},{4,1},{5,0},{6,3},{7,2},{8,13},{9,12},{10,... | collective-permute-start | bytes 86024 | tf_op jit(solution)/shard_map/ppermute | solution.py:20
  4.2 0.8 %select_select_fusion = bf16[4,896]{1,0:T(4,128)(2,1)S(1)} fusion(bf16[4,3584]{1,0:T(4,128)(2,1)} %param.6, pred[]{:T(512)S(6)} %gt.7, pred[]{:T(512)S(6)} %gt.6), kind=kLoop, calls=%fused_computation.59 | loop fusion | flops 10752 | bytes 35842 | tf_op jit(solution)/shard_map/jit(_where)/select_n | solution.py:36
  5.2 0.7 %collective-permute-start.1 = (bf16[4,896]{1,0:T(4,128)(2,1)S(1)}, bf16[4,896]{1,0:T(4,128)(2,1)S(1)}, u32[]{:S(2)}, u32[]{:S(2)}) collective-permute-start(bf16[4,896]{1,0:T(4,128)(2,1)S(1)} %fusion.9), channel_id=1, source_target_pairs={{0,1},{1,0},{2,3},{3,2},{4,5},{5,4},{6,7},{7,6},{8,9},{9,8},{10,11... | collective-permute-start | bytes 21512 | tf_op jit(solution)/shard_map/ppermute | solution.py:28
  5.9 1.1 %collective-permute-done.2 = bf16[4,3584]{1,0:T(4,128)(2,1)S(1)} collective-permute-done((bf16[4,3584]{1,0:T(4,128)(2,1)}, bf16[4,3584]{1,0:T(4,128)(2,1)S(1)}, u32[]{:S(2)}, u32[]{:S(2)}) %collective-permute-start.2) | collective-permute-done | bytes 28704 | tf_op jit(solution)/shard_map/ppermute | solution.py:20
  7.2 2.3 %collective-permute-start.3 = (bf16[4,4,896]{2,1,0:T(4,128)(2,1)S(1)}, bf16[4,4,896]{2,1,0:T(4,128)(2,1)S(1)}, u32[]{:S(2)}, u32[]{:S(2)}) collective-permute-start(bf16[4,4,896]{2,1,0:T(4,128)(2,1)S(1)} %pad_maximum_fusion.1), channel_id=1, source_target_pairs={{0,9},{1,8},{2,11},{3,10},{4,13},{5,12},{6,15},{7,14},{8,1},{9,0},... | collective-permute-start | bytes 86024 | tf_op jit(solution)/shard_map/ppermute | solution.py:20
  9.5 1.7 %pad_maximum_fusion = bf16[896,1024]{1,0:T(8,128)(2,1)S(1)} fusion(bf16[896,512]{1,0:T(8,128)(2,1)} %bitcast.61, bf16[896,512]{1,0:T(8,128)(2,1)} %bitcast.62), kind=kLoop, calls=%fused_computation | loop fusion | flops 3670016 | bytes 3670016 | tf_op jit(solution)/shard_map/concatenate | solution.py:122
  11.2 0.4 %collective-permute-done.3 = bf16[4,4,896]{2,1,0:T(4,128)(2,1)S(1)} collective-permute-done((bf16[4,4,896]{2,1,0:T(4,128)(2,1)S(1)}, bf16[4,4,896]{2,1,0:T(4,128)(2,1)S(1)}, u32[]{:S(2)}, u32[]{:S(2)}) %collective-permute-start.3) | collective-permute-done | bytes 28704 | tf_op jit(solution)/shard_map/ppermute | solution.py:20
  11.6 0.4 %fusion.16 = (bf16[32,1024]{1,0:T(8,128)(2,1)S(1)}, f32[32,1024]{1,0:T(8,128)S(1)}) fusion(bf16[32,896]{1,0:T(8,128)(2,1)S(1)} %reshape.24, bf16[896,1024]{1,0:T(8,128)(2,1)S(1)} %pad_maximum_fusion), kind=kOutput, calls=%fused_computation.76 | convolution fusion | flops 58753024 | bytes 2088960 | tf_op jit(solution)/shard_map/dot_general | solution.py:123
  12.0 2.2 %collective-permute-start.4 = (bf16[32,1024]{1,0:T(8,128)(2,1)S(1)}, bf16[32,1024]{1,0:T(8,128)(2,1)S(1)}, u32[]{:S(2)}, u32[]{:S(2)}) collective-permute-start(bf16[32,1024]{1,0:T(8,128)(2,1)S(1)} %get-tuple-element.63), channel_id=1, source_target_pairs={{0,6},{1,7},{2,4},{3,5},{4,2},{5,3},{6,0},{7,1},{8,14},{9,15},{10,... | collective-permute-start | bytes 196616 | tf_op jit(solution)/shard_map/ppermute | solution.py:20
  14.2 0.3 collective-permute-start.5
  14.5 1.0 %collective-permute-start.6 = (bf16[32,1024]{1,0:T(8,128)(2,1)S(1)}, bf16[32,1024]{1,0:T(8,128)(2,1)S(1)}, u32[]{:S(2)}, u32[]{:S(2)}) collective-permute-start(bf16[32,1024]{1,0:T(8,128)(2,1)S(1)} %get-tuple-element.63), channel_id=1, source_target_pairs={{0,2},{1,3},{2,0},{3,1},{4,6},{5,7},{6,4},{7,5},{8,10},{9,11},{10,... | collective-permute-start | bytes 196616 | tf_op jit(solution)/shard_map/ppermute | solution.py:20
  15.5 2.1 %collective-permute-done.4 = bf16[32,1024]{1,0:T(8,128)(2,1)S(1)} collective-permute-done((bf16[32,1024]{1,0:T(8,128)(2,1)S(1)}, bf16[32,1024]{1,0:T(8,128)(2,1)S(1)}, u32[]{:S(2)}, u32[]{:S(2)}) %collective-permute-start.4) | collective-permute-done | bytes 65568 | tf_op jit(solution)/shard_map/ppermute | solution.py:20
  17.6 0.9 %collective-permute-done.5 = bf16[32,1024]{1,0:T(8,128)(2,1)S(1)} collective-permute-done((bf16[32,1024]{1,0:T(8,128)(2,1)S(1)}, bf16[32,1024]{1,0:T(8,128)(2,1)S(1)}, u32[]{:S(2)}, u32[]{:S(2)}) %collective-permute-start.5) | collective-permute-done | bytes 65568 | tf_op jit(solution)/shard_map/ppermute | solution.py:20
  18.5 0.3 collective-permute-done.6
  19.2 0.5 %collective-permute-start.9 = (f32[16,896]{1,0:T(8,128)S(1)}, f32[16,896]{1,0:T(8,128)S(1)}, u32[]{:S(2)}, u32[]{:S(2)}) collective-permute-start(f32[16,896]{1,0:T(8,128)S(1)} %get-tuple-element.22), channel_id=1, source_target_pairs={{0,1},{1,0},{2,3},{3,2},{4,5},{5,4},{6,7},{7,6},{8,9},{9,8},{10,11... | collective-permute-start | bytes 172040 | tf_op jit(solution)/shard_map/ppermute | solution.py:28
  19.7 0.7 %collective-permute-done.7 = f32[16,896]{1,0:T(8,128)S(1)} collective-permute-done((f32[16,896]{1,0:T(8,128)S(1)}, f32[16,896]{1,0:T(8,128)S(1)}, u32[]{:S(2)}, u32[]{:S(2)}) %collective-permute-start.7) | collective-permute-done | bytes 57376 | tf_op jit(solution)/shard_map/ppermute | solution.py:28
  20.4 2.4 %collective-permute-start.8 = (bf16[4,1,4,896]{3,2,1,0:T(4,128)(2,1)S(1)}, bf16[4,1,4,896]{3,2,1,0:T(4,128)(2,1)S(1)}, u32[]{:S(2)}, u32[]{:S(2)}) collective-permute-start(bf16[4,1,4,896]{3,2,1,0:T(4,128)(2,1)S(1)} %bitcast.73), channel_id=1, source_target_pairs={{0,9},{1,8},{2,11},{3,10},{4,13},{5,12},{6,15},{7,14},{8,1},{9,0},... | collective-permute-start | bytes 86024 | tf_op jit(solution)/shard_map/ppermute | solution.py:20
  22.9 1.8 %collective-permute-done.8 = bf16[4,1,4,896]{3,2,1,0:T(4,128)(2,1)S(1)} collective-permute-done((bf16[4,1,4,896]{3,2,1,0:T(4,128)(2,1)S(1)}, bf16[4,1,4,896]{3,2,1,0:T(4,128)(2,1)S(1)}, u32[]{:S(2)}, u32[]{:S(2)}) %collective-permute-start.8) | collective-permute-done | bytes 28704 | tf_op jit(solution)/shard_map/ppermute | solution.py:20
  24.8 1.1 %collective-permute-start.10 = (bf16[2,4,896]{2,1,0:T(4,128)(2,1)S(1)}, bf16[2,4,896]{2,1,0:T(4,128)(2,1)S(1)}, u32[]{:S(2)}, u32[]{:S(2)}) collective-permute-start(bf16[2,4,896]{2,1,0:T(4,128)(2,1)S(1)} %get-tuple-element.25), channel_id=1, source_target_pairs={{0,2},{1,7},{2,0},{3,5},{4,6},{5,3},{6,4},{7,1},{8,10},{9,15},{10,... | collective-permute-start | bytes 43016 | tf_op jit(solution)/shard_map/ppermute | solution.py:20
  25.9 1.9 %collective-permute-start.12 = (bf16[2,4,896]{2,1,0:T(4,128)(2,1)S(1)}, bf16[2,4,896]{2,1,0:T(4,128)(2,1)S(1)}, u32[]{:S(2)}, u32[]{:S(2)}) collective-permute-start(bf16[2,4,896]{2,1,0:T(4,128)(2,1)S(1)} %get-tuple-element.26), channel_id=1, source_target_pairs={{0,4},{1,5},{2,6},{3,7},{4,0},{5,1},{6,2},{7,3},{8,12},{9,13},{10,... | collective-permute-start | bytes 43016 | tf_op jit(solution)/shard_map/ppermute | solution.py:20
  27.8 0.8 %collective-permute-done.10 = bf16[2,4,896]{2,1,0:T(4,128)(2,1)S(1)} collective-permute-done((bf16[2,4,896]{2,1,0:T(4,128)(2,1)S(1)}, bf16[2,4,896]{2,1,0:T(4,128)(2,1)S(1)}, u32[]{:S(2)}, u32[]{:S(2)}) %collective-permute-start.10) | collective-permute-done | bytes 14368 | tf_op jit(solution)/shard_map/ppermute | solution.py:20
  28.6 1.1 %collective-permute-done.12 = bf16[2,4,896]{2,1,0:T(4,128)(2,1)S(1)} collective-permute-done((bf16[2,4,896]{2,1,0:T(4,128)(2,1)S(1)}, bf16[2,4,896]{2,1,0:T(4,128)(2,1)S(1)}, u32[]{:S(2)}, u32[]{:S(2)}) %collective-permute-start.12) | collective-permute-done | bytes 14368 | tf_op jit(solution)/shard_map/ppermute | solution.py:20
  29.8 0.7 %add_convert_fusion = bf16[4,3584]{1,0:T(4,128)(2,1)} fusion(bf16[4,896]{1,0:T(4,128)(2,1)S(1)} %get-tuple-element.60, bf16[4,896]{1,0:T(4,128)(2,1)S(1)} %get-tuple-element.65, bf16[4,896]{1,0:T(4,128)(2,1)S(1)} %get-tuple-element.56, bf16[4,896]{1,0:T(4,128)(2,1)S(1)} %get-tuple-element.67, bf16[4,896]{1,0:T(4,128)(2,1)S(1)} %get-tuple-element.59, ...), kind=kLoop, calls=%fused_computation.12 | loop fusion | flops 286720 | bytes 86048 | tf_op jit(solution)/shard_map/convert_element_type | solution.py:167
  (38 shorter events, 1.0 us)
Async XLA Ops:
  0.0 18.8 %copy-start = (bf16[1,512,896]{2,1,0:T(8,128)(2,1)S(1)}, bf16[1,512,896]{2,1,0:T(8,128)(2,1)}, u32[]{:S(2)}) copy-start(bf16[1,512,896]{2,1,0:T(8,128)(2,1)} %param.11) | copy-start | bytes 2752516
  0.0 5.2 %collective-permute-start = (bf16[4,3584]{1,0:T(4,128)(2,1)}, bf16[4,3584]{1,0:T(4,128)(2,1)S(1)}, u32[]{:S(2)}, u32[]{:S(2)}) collective-permute-start(bf16[4,3584]{1,0:T(4,128)(2,1)} %param.6), channel_id=1, source_target_pairs={{0,7},{1,2},{2,5},{3,0},{4,3},{5,6},{6,1},{7,4},{8,15},{9,10},{10,... | collective-permute-start | bytes 86024 | tf_op jit(solution)/shard_map/ppermute | solution.py:20
  3.4 3.7 %collective-permute-start.2 = (bf16[4,3584]{1,0:T(4,128)(2,1)}, bf16[4,3584]{1,0:T(4,128)(2,1)S(1)}, u32[]{:S(2)}, u32[]{:S(2)}) collective-permute-start(bf16[4,3584]{1,0:T(4,128)(2,1)} %param.6), channel_id=1, source_target_pairs={{0,5},{1,4},{2,7},{3,6},{4,1},{5,0},{6,3},{7,2},{8,13},{9,12},{10,... | collective-permute-start | bytes 86024 | tf_op jit(solution)/shard_map/ppermute | solution.py:20
  5.2 1.9 %collective-permute-start.1 = (bf16[4,896]{1,0:T(4,128)(2,1)S(1)}, bf16[4,896]{1,0:T(4,128)(2,1)S(1)}, u32[]{:S(2)}, u32[]{:S(2)}) collective-permute-start(bf16[4,896]{1,0:T(4,128)(2,1)S(1)} %fusion.9), channel_id=1, source_target_pairs={{0,1},{1,0},{2,3},{3,2},{4,5},{5,4},{6,7},{7,6},{8,9},{9,8},{10,11... | collective-permute-start | bytes 21512 | tf_op jit(solution)/shard_map/ppermute | solution.py:28
  7.2 4.3 %collective-permute-start.3 = (bf16[4,4,896]{2,1,0:T(4,128)(2,1)S(1)}, bf16[4,4,896]{2,1,0:T(4,128)(2,1)S(1)}, u32[]{:S(2)}, u32[]{:S(2)}) collective-permute-start(bf16[4,4,896]{2,1,0:T(4,128)(2,1)S(1)} %pad_maximum_fusion.1), channel_id=1, source_target_pairs={{0,9},{1,8},{2,11},{3,10},{4,13},{5,12},{6,15},{7,14},{8,1},{9,0},... | collective-permute-start | bytes 86024 | tf_op jit(solution)/shard_map/ppermute | solution.py:20
  11.2 4.4 %copy-start.1 = (f32[4,2]{0,1:T(2,128)S(1)}, f32[4,2]{0,1:T(2,128)}, u32[]{:S(2)}) copy-start(f32[4,2]{0,1:T(2,128)} %param.8) | copy-start | bytes 100
  11.6 14.3 %copy-start.2 = (s32[4,2]{0,1:T(2,128)S(1)}, s32[4,2]{0,1:T(2,128)}, u32[]{:S(2)}) copy-start(s32[4,2]{0,1:T(2,128)} %param.7) | copy-start | bytes 100
  12.0 5.6 %collective-permute-start.4 = (bf16[32,1024]{1,0:T(8,128)(2,1)S(1)}, bf16[32,1024]{1,0:T(8,128)(2,1)S(1)}, u32[]{:S(2)}, u32[]{:S(2)}) collective-permute-start(bf16[32,1024]{1,0:T(8,128)(2,1)S(1)} %get-tuple-element.63), channel_id=1, source_target_pairs={{0,6},{1,7},{2,4},{3,5},{4,2},{5,3},{6,0},{7,1},{8,14},{9,15},{10,... | collective-permute-start | bytes 196616 | tf_op jit(solution)/shard_map/ppermute | solution.py:20
  14.2 4.3 %collective-permute-start.5 = (bf16[32,1024]{1,0:T(8,128)(2,1)S(1)}, bf16[32,1024]{1,0:T(8,128)(2,1)S(1)}, u32[]{:S(2)}, u32[]{:S(2)}) collective-permute-start(bf16[32,1024]{1,0:T(8,128)(2,1)S(1)} %get-tuple-element.63), channel_id=1, source_target_pairs={{0,4},{1,5},{2,6},{3,7},{4,0},{5,1},{6,2},{7,3},{8,12},{9,13},{10,... | collective-permute-start | bytes 196616 | tf_op jit(solution)/shard_map/ppermute | solution.py:20
  14.5 4.3 %collective-permute-start.6 = (bf16[32,1024]{1,0:T(8,128)(2,1)S(1)}, bf16[32,1024]{1,0:T(8,128)(2,1)S(1)}, u32[]{:S(2)}, u32[]{:S(2)}) collective-permute-start(bf16[32,1024]{1,0:T(8,128)(2,1)S(1)} %get-tuple-element.63), channel_id=1, source_target_pairs={{0,2},{1,3},{2,0},{3,1},{4,6},{5,7},{6,4},{7,5},{8,10},{9,11},{10,... | collective-permute-start | bytes 196616 | tf_op jit(solution)/shard_map/ppermute | solution.py:20
  19.1 1.3 %collective-permute-start.7 = (f32[16,896]{1,0:T(8,128)S(1)}, f32[16,896]{1,0:T(8,128)S(1)}, u32[]{:S(2)}, u32[]{:S(2)}) collective-permute-start(f32[16,896]{1,0:T(8,128)S(1)} %get-tuple-element.21), channel_id=1, source_target_pairs={{0,1},{1,0},{2,3},{3,2},{4,5},{5,4},{6,7},{7,6},{8,9},{9,8},{10,11... | collective-permute-start | bytes 172040 | tf_op jit(solution)/shard_map/ppermute | solution.py:28
  19.2 3.7 %collective-permute-start.9 = (f32[16,896]{1,0:T(8,128)S(1)}, f32[16,896]{1,0:T(8,128)S(1)}, u32[]{:S(2)}, u32[]{:S(2)}) collective-permute-start(f32[16,896]{1,0:T(8,128)S(1)} %get-tuple-element.22), channel_id=1, source_target_pairs={{0,1},{1,0},{2,3},{3,2},{4,5},{5,4},{6,7},{7,6},{8,9},{9,8},{10,11... | collective-permute-start | bytes 172040 | tf_op jit(solution)/shard_map/ppermute | solution.py:28
  20.4 4.3 %collective-permute-start.8 = (bf16[4,1,4,896]{3,2,1,0:T(4,128)(2,1)S(1)}, bf16[4,1,4,896]{3,2,1,0:T(4,128)(2,1)S(1)}, u32[]{:S(2)}, u32[]{:S(2)}) collective-permute-start(bf16[4,1,4,896]{3,2,1,0:T(4,128)(2,1)S(1)} %bitcast.73), channel_id=1, source_target_pairs={{0,9},{1,8},{2,11},{3,10},{4,13},{5,12},{6,15},{7,14},{8,1},{9,0},... | collective-permute-start | bytes 86024 | tf_op jit(solution)/shard_map/ppermute | solution.py:20
  24.8 3.8 %collective-permute-start.10 = (bf16[2,4,896]{2,1,0:T(4,128)(2,1)S(1)}, bf16[2,4,896]{2,1,0:T(4,128)(2,1)S(1)}, u32[]{:S(2)}, u32[]{:S(2)}) collective-permute-start(bf16[2,4,896]{2,1,0:T(4,128)(2,1)S(1)} %get-tuple-element.25), channel_id=1, source_target_pairs={{0,2},{1,7},{2,0},{3,5},{4,6},{5,3},{6,4},{7,1},{8,10},{9,15},{10,... | collective-permute-start | bytes 43016 | tf_op jit(solution)/shard_map/ppermute | solution.py:20
  25.9 3.8 %collective-permute-start.12 = (bf16[2,4,896]{2,1,0:T(4,128)(2,1)S(1)}, bf16[2,4,896]{2,1,0:T(4,128)(2,1)S(1)}, u32[]{:S(2)}, u32[]{:S(2)}) collective-permute-start(bf16[2,4,896]{2,1,0:T(4,128)(2,1)S(1)} %get-tuple-element.26), channel_id=1, source_target_pairs={{0,4},{1,5},{2,6},{3,7},{4,0},{5,1},{6,2},{7,3},{8,12},{9,13},{10,... | collective-permute-start | bytes 43016 | tf_op jit(solution)/shard_map/ppermute | solution.py:20
  28.6 1.2 %collective-permute-start.11 = (bf16[2,4,896]{2,1,0:T(4,128)(2,1)S(1)}, bf16[2,4,896]{2,1,0:T(4,128)(2,1)S(1)}, u32[]{:S(2)}, u32[]{:S(2)}) collective-permute-start(bf16[2,4,896]{2,1,0:T(4,128)(2,1)S(1)} %collective-permute-done.10), channel_id=1, source_target_pairs={{0,1},{1,0},{2,3},{3,2},{4,5},{5,4},{6,7},{7,6},{8,9},{9,8},{10,11... | collective-permute-start | bytes 43016 | tf_op jit(solution)/shard_map/ppermute | solution.py:28

commit v10 on v9

--- a/solution.py
+++ b/solution.py
@@ -75,7 +75,7 @@
     return tokens
 
 
-def return_tokens(near, far):
+def return_tokens(near, far, weighted):
     rank = lax.axis_index("ep")
     held = near[:, None]
     mask = GROUP
@@ -100,6 +100,7 @@
     )
     blocks = gathered(split, masks, False, shared, False, lambda block: block)
     blocks[0] = own
+    blocks = {mask: weighted(block) for mask, block in blocks.items()}
     return by_xor([blocks[index] for index in range(GROUP)], rank)
 
 
@@ -154,17 +155,17 @@
         share = jnp.sum(jnp.where(named, routing[:, :, None], 0.0), axis=1)
         rows = spread_tokens(hidden).reshape(peer_count * tok_rows, quarter)
         near, far = expert_rows(rows, w_gate[0], w_up[0], w_down[0], experts)
-        returned = return_tokens(
-            near.reshape(-1, tok_rows, quarter), far.reshape(-1, tok_rows, quarter)
-        )
         shares = [share[:, index : index + 1] for index in range(experts)]
         shares = by_xor(shares, lax.axis_index("ep") // GROUP)
-        combined = sum(
-            jnp.concatenate([block[index] for block in returned], axis=1).astype(jnp.float32)
-            * shares[index]
-            for index in range(experts)
+
+        def weighted(block):
+            total = sum(block[index].astype(jnp.float32) * shares[index] for index in range(experts))
+            return total.astype(jnp.bfloat16)
+
+        finished = return_tokens(
+            near.reshape(-1, tok_rows, quarter), far.reshape(-1, tok_rows, quarter), weighted
         )
-        return combined.astype(jnp.bfloat16)
+        return jnp.concatenate(finished, axis=1)
     capacity = min(tok_rows, 2 * tok_rows * route_count // experts)
     expert_hot, slot_hot = route_tables(expert_ids, experts, capacity)
     placing = jnp.einsum("tke,tkc->ect", expert_hot, slot_hot).astype(jnp.bfloat16)

time: 30.7 us -> 30.7 us (level)
    convert_element_type x1 -> x0, other arithmetic: 0.7 us -> none  [local(): return combined.astype(jnp.bfloat16)]
    concatenate x0 -> x1, other arithmetic: none -> 0.63 us  [local(): return jnp.concatenate(finished, axis=1)]
where the time goes in v10:
time: 30.7 us; the launch traced here: 30.5 us
  starting transfers between devices  16.7 us (54%)
  waiting for transfers between devices  9.38 us (31%)
  other arithmetic  3.51 us (11%)
  matrix products  0.67 us (2%)
    ppermute x9, starting transfers between devices, swapped(): return lax.ppermute(value, ('ep', 'tp'), pairs)  15.4 us
    ppermute x9, waiting for transfers between devices, swapped(): return lax.ppermute(value, ('ep', 'tp'), pairs)  8.58 us
    concatenate x1, other arithmetic, expert_rows(): jnp.concatenate([w_gate, w_up], axis=1)  1.68 us
    ppermute x4, starting transfers between devices, other_core(): return lax.ppermute(value, 'tp', [(0, 1), (1, 0)])  1.29 us
    select_n x6, other arithmetic, by_xor(): jnp.where(bit, blocks[index ^ mask], blocks[index])  0.95 us
    ppermute x4, waiting for transfers between devices, other_core(): return lax.ppermute(value, 'tp', [(0, 1), (1, 0)])  0.8 us
    concatenate x1, other arithmetic, local(): return jnp.concatenate(finished, axis=1)  0.63 us
  transfers between devices with their start and end apart: 13, of which 11 were waited for; matrix products, arithmetic and copies ran while one was open for 8% of the time, Pallas kernels for 0%

profile of v10, /device:TPU:0, one launch (start us, length us, event | category | flops | bytes accessed | tf_op | source)
XLA Modules:
  0.0 30.5 jit_solution(4101288495405680710)
XLA Ops:
  0.0 3.4 %collective-permute-start = (bf16[4,3584]{1,0:T(4,128)(2,1)}, bf16[4,3584]{1,0:T(4,128)(2,1)S(1)}, u32[]{:S(2)}, u32[]{:S(2)}) collective-permute-start(bf16[4,3584]{1,0:T(4,128)(2,1)} %param.6), channel_id=1, source_target_pairs={{0,7},{1,2},{2,5},{3,0},{4,3},{5,6},{6,1},{7,4},{8,15},{9,10},{10,... | collective-permute-start | bytes 86024 | tf_op jit(solution)/shard_map/ppermute | solution.py:20
  3.4 0.8 %collective-permute-start.2 = (bf16[4,3584]{1,0:T(4,128)(2,1)}, bf16[4,3584]{1,0:T(4,128)(2,1)S(1)}, u32[]{:S(2)}, u32[]{:S(2)}) collective-permute-start(bf16[4,3584]{1,0:T(4,128)(2,1)} %param.6), channel_id=1, source_target_pairs={{0,5},{1,4},{2,7},{3,6},{4,1},{5,0},{6,3},{7,2},{8,13},{9,12},{10,... | collective-permute-start | bytes 86024 | tf_op jit(solution)/shard_map/ppermute | solution.py:20
  4.2 0.8 %select_select_fusion = bf16[4,896]{1,0:T(4,128)(2,1)S(1)} fusion(bf16[4,3584]{1,0:T(4,128)(2,1)} %param.6, pred[]{:T(512)S(6)} %gt.7, pred[]{:T(512)S(6)} %gt.6), kind=kLoop, calls=%fused_computation.63 | loop fusion | flops 10752 | bytes 35842 | tf_op jit(solution)/shard_map/jit(_where)/select_n | solution.py:36
  5.2 0.7 %collective-permute-start.1 = (bf16[4,896]{1,0:T(4,128)(2,1)S(1)}, bf16[4,896]{1,0:T(4,128)(2,1)S(1)}, u32[]{:S(2)}, u32[]{:S(2)}) collective-permute-start(bf16[4,896]{1,0:T(4,128)(2,1)S(1)} %fusion.17), channel_id=1, source_target_pairs={{0,1},{1,0},{2,3},{3,2},{4,5},{5,4},{6,7},{7,6},{8,9},{9,8},{10,11... | collective-permute-start | bytes 21512 | tf_op jit(solution)/shard_map/ppermute | solution.py:28
  5.9 1.1 %collective-permute-done.2 = bf16[4,3584]{1,0:T(4,128)(2,1)S(1)} collective-permute-done((bf16[4,3584]{1,0:T(4,128)(2,1)}, bf16[4,3584]{1,0:T(4,128)(2,1)S(1)}, u32[]{:S(2)}, u32[]{:S(2)}) %collective-permute-start.2) | collective-permute-done | bytes 28704 | tf_op jit(solution)/shard_map/ppermute | solution.py:20
  7.2 2.3 %collective-permute-start.3 = (bf16[4,4,896]{2,1,0:T(4,128)(2,1)S(1)}, bf16[4,4,896]{2,1,0:T(4,128)(2,1)S(1)}, u32[]{:S(2)}, u32[]{:S(2)}) collective-permute-start(bf16[4,4,896]{2,1,0:T(4,128)(2,1)S(1)} %pad_maximum_fusion.1), channel_id=1, source_target_pairs={{0,9},{1,8},{2,11},{3,10},{4,13},{5,12},{6,15},{7,14},{8,1},{9,0},... | collective-permute-start | bytes 86024 | tf_op jit(solution)/shard_map/ppermute | solution.py:20
  9.5 1.7 %pad_maximum_fusion = bf16[896,1024]{1,0:T(8,128)(2,1)S(1)} fusion(bf16[896,512]{1,0:T(8,128)(2,1)} %bitcast.75, bf16[896,512]{1,0:T(8,128)(2,1)} %bitcast.76), kind=kLoop, calls=%fused_computation | loop fusion | flops 3670016 | bytes 3670016 | tf_op jit(solution)/shard_map/concatenate | solution.py:123
  11.2 0.4 %collective-permute-done.3 = bf16[4,4,896]{2,1,0:T(4,128)(2,1)S(1)} collective-permute-done((bf16[4,4,896]{2,1,0:T(4,128)(2,1)S(1)}, bf16[4,4,896]{2,1,0:T(4,128)(2,1)S(1)}, u32[]{:S(2)}, u32[]{:S(2)}) %collective-permute-start.3) | collective-permute-done | bytes 28704 | tf_op jit(solution)/shard_map/ppermute | solution.py:20
  11.6 0.4 %fusion.28 = (bf16[32,1024]{1,0:T(8,128)(2,1)S(1)}, f32[32,1024]{1,0:T(8,128)S(1)}) fusion(bf16[32,896]{1,0:T(8,128)(2,1)S(1)} %reshape.40, bf16[896,1024]{1,0:T(8,128)(2,1)S(1)} %pad_maximum_fusion), kind=kOutput, calls=%fused_computation.88 | convolution fusion | flops 58753024 | bytes 2088960 | tf_op jit(solution)/shard_map/dot_general | solution.py:124
  12.0 2.2 %collective-permute-start.4 = (bf16[32,1024]{1,0:T(8,128)(2,1)S(1)}, bf16[32,1024]{1,0:T(8,128)(2,1)S(1)}, u32[]{:S(2)}, u32[]{:S(2)}) collective-permute-start(bf16[32,1024]{1,0:T(8,128)(2,1)S(1)} %get-tuple-element.59), channel_id=1, source_target_pairs={{0,6},{1,7},{2,4},{3,5},{4,2},{5,3},{6,0},{7,1},{8,14},{9,15},{10,... | collective-permute-start | bytes 196616 | tf_op jit(solution)/shard_map/ppermute | solution.py:20
  14.2 0.3 collective-permute-start.5
  14.5 1.0 %collective-permute-start.6 = (bf16[32,1024]{1,0:T(8,128)(2,1)S(1)}, bf16[32,1024]{1,0:T(8,128)(2,1)S(1)}, u32[]{:S(2)}, u32[]{:S(2)}) collective-permute-start(bf16[32,1024]{1,0:T(8,128)(2,1)S(1)} %get-tuple-element.59), channel_id=1, source_target_pairs={{0,2},{1,3},{2,0},{3,1},{4,6},{5,7},{6,4},{7,5},{8,10},{9,11},{10,... | collective-permute-start | bytes 196616 | tf_op jit(solution)/shard_map/ppermute | solution.py:20
  15.5 2.1 %collective-permute-done.4 = bf16[32,1024]{1,0:T(8,128)(2,1)S(1)} collective-permute-done((bf16[32,1024]{1,0:T(8,128)(2,1)S(1)}, bf16[32,1024]{1,0:T(8,128)(2,1)S(1)}, u32[]{:S(2)}, u32[]{:S(2)}) %collective-permute-start.4) | collective-permute-done | bytes 65568 | tf_op jit(solution)/shard_map/ppermute | solution.py:20
  17.6 0.9 %collective-permute-done.5 = bf16[32,1024]{1,0:T(8,128)(2,1)S(1)} collective-permute-done((bf16[32,1024]{1,0:T(8,128)(2,1)S(1)}, bf16[32,1024]{1,0:T(8,128)(2,1)S(1)}, u32[]{:S(2)}, u32[]{:S(2)}) %collective-permute-start.5) | collective-permute-done | bytes 65568 | tf_op jit(solution)/shard_map/ppermute | solution.py:20
  18.5 0.3 collective-permute-done.6
  19.2 0.5 %collective-permute-start.9 = (f32[16,896]{1,0:T(8,128)S(1)}, f32[16,896]{1,0:T(8,128)S(1)}, u32[]{:S(2)}, u32[]{:S(2)}) collective-permute-start(f32[16,896]{1,0:T(8,128)S(1)} %get-tuple-element.22), channel_id=1, source_target_pairs={{0,1},{1,0},{2,3},{3,2},{4,5},{5,4},{6,7},{7,6},{8,9},{9,8},{10,11... | collective-permute-start | bytes 172040 | tf_op jit(solution)/shard_map/ppermute | solution.py:28
  19.7 0.7 %collective-permute-done.7 = f32[16,896]{1,0:T(8,128)S(1)} collective-permute-done((f32[16,896]{1,0:T(8,128)S(1)}, f32[16,896]{1,0:T(8,128)S(1)}, u32[]{:S(2)}, u32[]{:S(2)}) %collective-permute-start.7) | collective-permute-done | bytes 57376 | tf_op jit(solution)/shard_map/ppermute | solution.py:28
  20.4 2.4 %collective-permute-start.8 = (bf16[4,1,4,896]{3,2,1,0:T(4,128)(2,1)S(1)}, bf16[4,1,4,896]{3,2,1,0:T(4,128)(2,1)S(1)}, u32[]{:S(2)}, u32[]{:S(2)}) collective-permute-start(bf16[4,1,4,896]{3,2,1,0:T(4,128)(2,1)S(1)} %bitcast.81), channel_id=1, source_target_pairs={{0,9},{1,8},{2,11},{3,10},{4,13},{5,12},{6,15},{7,14},{8,1},{9,0},... | collective-permute-start | bytes 86024 | tf_op jit(solution)/shard_map/ppermute | solution.py:20
  22.9 1.8 %collective-permute-done.8 = bf16[4,1,4,896]{3,2,1,0:T(4,128)(2,1)S(1)} collective-permute-done((bf16[4,1,4,896]{3,2,1,0:T(4,128)(2,1)S(1)}, bf16[4,1,4,896]{3,2,1,0:T(4,128)(2,1)S(1)}, u32[]{:S(2)}, u32[]{:S(2)}) %collective-permute-start.8) | collective-permute-done | bytes 28704 | tf_op jit(solution)/shard_map/ppermute | solution.py:20
  24.8 1.1 %collective-permute-start.10 = (bf16[2,4,896]{2,1,0:T(4,128)(2,1)S(1)}, bf16[2,4,896]{2,1,0:T(4,128)(2,1)S(1)}, u32[]{:S(2)}, u32[]{:S(2)}) collective-permute-start(bf16[2,4,896]{2,1,0:T(4,128)(2,1)S(1)} %get-tuple-element.25), channel_id=1, source_target_pairs={{0,2},{1,7},{2,0},{3,5},{4,6},{5,3},{6,4},{7,1},{8,10},{9,15},{10,... | collective-permute-start | bytes 43016 | tf_op jit(solution)/shard_map/ppermute | solution.py:20
  25.9 1.9 %collective-permute-start.12 = (bf16[2,4,896]{2,1,0:T(4,128)(2,1)S(1)}, bf16[2,4,896]{2,1,0:T(4,128)(2,1)S(1)}, u32[]{:S(2)}, u32[]{:S(2)}) collective-permute-start(bf16[2,4,896]{2,1,0:T(4,128)(2,1)S(1)} %get-tuple-element.26), channel_id=1, source_target_pairs={{0,4},{1,5},{2,6},{3,7},{4,0},{5,1},{6,2},{7,3},{8,12},{9,13},{10,... | collective-permute-start | bytes 43016 | tf_op jit(solution)/shard_map/ppermute | solution.py:20
  27.8 0.8 %collective-permute-done.10 = bf16[2,4,896]{2,1,0:T(4,128)(2,1)S(1)} collective-permute-done((bf16[2,4,896]{2,1,0:T(4,128)(2,1)S(1)}, bf16[2,4,896]{2,1,0:T(4,128)(2,1)S(1)}, u32[]{:S(2)}, u32[]{:S(2)}) %collective-permute-start.10) | collective-permute-done | bytes 14368 | tf_op jit(solution)/shard_map/ppermute | solution.py:20
  28.6 1.1 %collective-permute-done.12 = bf16[2,4,896]{2,1,0:T(4,128)(2,1)S(1)} collective-permute-done((bf16[2,4,896]{2,1,0:T(4,128)(2,1)S(1)}, bf16[2,4,896]{2,1,0:T(4,128)(2,1)S(1)}, u32[]{:S(2)}, u32[]{:S(2)}) %collective-permute-start.12) | collective-permute-done | bytes 14368 | tf_op jit(solution)/shard_map/ppermute | solution.py:20
  29.9 0.6 %pad_maximum_fusion.2 = bf16[4,3584]{1,0:T(4,128)(2,1)} fusion(bf16[4,896]{1,0:T(4,128)(2,1)S(1)} %get-tuple-element.54, bf16[4,896]{1,0:T(4,128)(2,1)S(1)} %get-tuple-element.53, bf16[4,896]{1,0:T(4,128)(2,1)S(1)} %get-tuple-element.52, bf16[4,896]{1,0:T(4,128)(2,1)S(1)} %get-tuple-element.31), kind=kLoop, calls=%fused_computation.16 | loop fusion | flops 114688 | bytes 57344 | tf_op jit(solution)/shard_map/concatenate | solution.py:168
  (37 shorter events, 1.1 us)
Async XLA Ops:
  0.0 18.8 %copy-start = (bf16[1,512,896]{2,1,0:T(8,128)(2,1)S(1)}, bf16[1,512,896]{2,1,0:T(8,128)(2,1)}, u32[]{:S(2)}) copy-start(bf16[1,512,896]{2,1,0:T(8,128)(2,1)} %param.11) | copy-start | bytes 2752516
  0.0 5.2 %collective-permute-start = (bf16[4,3584]{1,0:T(4,128)(2,1)}, bf16[4,3584]{1,0:T(4,128)(2,1)S(1)}, u32[]{:S(2)}, u32[]{:S(2)}) collective-permute-start(bf16[4,3584]{1,0:T(4,128)(2,1)} %param.6), channel_id=1, source_target_pairs={{0,7},{1,2},{2,5},{3,0},{4,3},{5,6},{6,1},{7,4},{8,15},{9,10},{10,... | collective-permute-start | bytes 86024 | tf_op jit(solution)/shard_map/ppermute | solution.py:20
  3.4 3.7 %collective-permute-start.2 = (bf16[4,3584]{1,0:T(4,128)(2,1)}, bf16[4,3584]{1,0:T(4,128)(2,1)S(1)}, u32[]{:S(2)}, u32[]{:S(2)}) collective-permute-start(bf16[4,3584]{1,0:T(4,128)(2,1)} %param.6), channel_id=1, source_target_pairs={{0,5},{1,4},{2,7},{3,6},{4,1},{5,0},{6,3},{7,2},{8,13},{9,12},{10,... | collective-permute-start | bytes 86024 | tf_op jit(solution)/shard_map/ppermute | solution.py:20
  5.2 1.9 %collective-permute-start.1 = (bf16[4,896]{1,0:T(4,128)(2,1)S(1)}, bf16[4,896]{1,0:T(4,128)(2,1)S(1)}, u32[]{:S(2)}, u32[]{:S(2)}) collective-permute-start(bf16[4,896]{1,0:T(4,128)(2,1)S(1)} %fusion.17), channel_id=1, source_target_pairs={{0,1},{1,0},{2,3},{3,2},{4,5},{5,4},{6,7},{7,6},{8,9},{9,8},{10,11... | collective-permute-start | bytes 21512 | tf_op jit(solution)/shard_map/ppermute | solution.py:28
  7.2 4.3 %collective-permute-start.3 = (bf16[4,4,896]{2,1,0:T(4,128)(2,1)S(1)}, bf16[4,4,896]{2,1,0:T(4,128)(2,1)S(1)}, u32[]{:S(2)}, u32[]{:S(2)}) collective-permute-start(bf16[4,4,896]{2,1,0:T(4,128)(2,1)S(1)} %pad_maximum_fusion.1), channel_id=1, source_target_pairs={{0,9},{1,8},{2,11},{3,10},{4,13},{5,12},{6,15},{7,14},{8,1},{9,0},... | collective-permute-start | bytes 86024 | tf_op jit(solution)/shard_map/ppermute | solution.py:20
  11.2 4.4 %copy-start.1 = (f32[4,2]{0,1:T(2,128)S(1)}, f32[4,2]{0,1:T(2,128)}, u32[]{:S(2)}) copy-start(f32[4,2]{0,1:T(2,128)} %param.8) | copy-start | bytes 100
  11.6 14.3 %copy-start.2 = (s32[4,2]{0,1:T(2,128)S(1)}, s32[4,2]{0,1:T(2,128)}, u32[]{:S(2)}) copy-start(s32[4,2]{0,1:T(2,128)} %param.7) | copy-start | bytes 100
  12.0 5.6 %collective-permute-start.4 = (bf16[32,1024]{1,0:T(8,128)(2,1)S(1)}, bf16[32,1024]{1,0:T(8,128)(2,1)S(1)}, u32[]{:S(2)}, u32[]{:S(2)}) collective-permute-start(bf16[32,1024]{1,0:T(8,128)(2,1)S(1)} %get-tuple-element.59), channel_id=1, source_target_pairs={{0,6},{1,7},{2,4},{3,5},{4,2},{5,3},{6,0},{7,1},{8,14},{9,15},{10,... | collective-permute-start | bytes 196616 | tf_op jit(solution)/shard_map/ppermute | solution.py:20
  14.2 4.3 %collective-permute-start.5 = (bf16[32,1024]{1,0:T(8,128)(2,1)S(1)}, bf16[32,1024]{1,0:T(8,128)(2,1)S(1)}, u32[]{:S(2)}, u32[]{:S(2)}) collective-permute-start(bf16[32,1024]{1,0:T(8,128)(2,1)S(1)} %get-tuple-element.59), channel_id=1, source_target_pairs={{0,4},{1,5},{2,6},{3,7},{4,0},{5,1},{6,2},{7,3},{8,12},{9,13},{10,... | collective-permute-start | bytes 196616 | tf_op jit(solution)/shard_map/ppermute | solution.py:20
  14.5 4.3 %collective-permute-start.6 = (bf16[32,1024]{1,0:T(8,128)(2,1)S(1)}, bf16[32,1024]{1,0:T(8,128)(2,1)S(1)}, u32[]{:S(2)}, u32[]{:S(2)}) collective-permute-start(bf16[32,1024]{1,0:T(8,128)(2,1)S(1)} %get-tuple-element.59), channel_id=1, source_target_pairs={{0,2},{1,3},{2,0},{3,1},{4,6},{5,7},{6,4},{7,5},{8,10},{9,11},{10,... | collective-permute-start | bytes 196616 | tf_op jit(solution)/shard_map/ppermute | solution.py:20
  19.1 1.3 %collective-permute-start.7 = (f32[16,896]{1,0:T(8,128)S(1)}, f32[16,896]{1,0:T(8,128)S(1)}, u32[]{:S(2)}, u32[]{:S(2)}) collective-permute-start(f32[16,896]{1,0:T(8,128)S(1)} %get-tuple-element.21), channel_id=1, source_target_pairs={{0,1},{1,0},{2,3},{3,2},{4,5},{5,4},{6,7},{7,6},{8,9},{9,8},{10,11... | collective-permute-start | bytes 172040 | tf_op jit(solution)/shard_map/ppermute | solution.py:28
  19.2 3.7 %collective-permute-start.9 = (f32[16,896]{1,0:T(8,128)S(1)}, f32[16,896]{1,0:T(8,128)S(1)}, u32[]{:S(2)}, u32[]{:S(2)}) collective-permute-start(f32[16,896]{1,0:T(8,128)S(1)} %get-tuple-element.22), channel_id=1, source_target_pairs={{0,1},{1,0},{2,3},{3,2},{4,5},{5,4},{6,7},{7,6},{8,9},{9,8},{10,11... | collective-permute-start | bytes 172040 | tf_op jit(solution)/shard_map/ppermute | solution.py:28
  20.4 4.3 %collective-permute-start.8 = (bf16[4,1,4,896]{3,2,1,0:T(4,128)(2,1)S(1)}, bf16[4,1,4,896]{3,2,1,0:T(4,128)(2,1)S(1)}, u32[]{:S(2)}, u32[]{:S(2)}) collective-permute-start(bf16[4,1,4,896]{3,2,1,0:T(4,128)(2,1)S(1)} %bitcast.81), channel_id=1, source_target_pairs={{0,9},{1,8},{2,11},{3,10},{4,13},{5,12},{6,15},{7,14},{8,1},{9,0},... | collective-permute-start | bytes 86024 | tf_op jit(solution)/shard_map/ppermute | solution.py:20
  24.8 3.8 %collective-permute-start.10 = (bf16[2,4,896]{2,1,0:T(4,128)(2,1)S(1)}, bf16[2,4,896]{2,1,0:T(4,128)(2,1)S(1)}, u32[]{:S(2)}, u32[]{:S(2)}) collective-permute-start(bf16[2,4,896]{2,1,0:T(4,128)(2,1)S(1)} %get-tuple-element.25), channel_id=1, source_target_pairs={{0,2},{1,7},{2,0},{3,5},{4,6},{5,3},{6,4},{7,1},{8,10},{9,15},{10,... | collective-permute-start | bytes 43016 | tf_op jit(solution)/shard_map/ppermute | solution.py:20
  25.9 3.8 %collective-permute-start.12 = (bf16[2,4,896]{2,1,0:T(4,128)(2,1)S(1)}, bf16[2,4,896]{2,1,0:T(4,128)(2,1)S(1)}, u32[]{:S(2)}, u32[]{:S(2)}) collective-permute-start(bf16[2,4,896]{2,1,0:T(4,128)(2,1)S(1)} %get-tuple-element.26), channel_id=1, source_target_pairs={{0,4},{1,5},{2,6},{3,7},{4,0},{5,1},{6,2},{7,3},{8,12},{9,13},{10,... | collective-permute-start | bytes 43016 | tf_op jit(solution)/shard_map/ppermute | solution.py:20
  28.6 1.2 %collective-permute-start.11 = (bf16[2,4,896]{2,1,0:T(4,128)(2,1)S(1)}, bf16[2,4,896]{2,1,0:T(4,128)(2,1)S(1)}, u32[]{:S(2)}, u32[]{:S(2)}) collective-permute-start(bf16[2,4,896]{2,1,0:T(4,128)(2,1)S(1)} %collective-permute-done.10), channel_id=1, source_target_pairs={{0,1},{1,0},{2,3},{3,2},{4,5},{5,4},{6,7},{7,6},{8,9},{9,8},{10,11... | collective-permute-start | bytes 43016 | tf_op jit(solution)/shard_map/ppermute | solution.py:28

commit v11 on v9

--- a/solution.py
+++ b/solution.py
@@ -98,7 +98,7 @@
     own, shared, split = lax.optimization_barrier(
         (leaving[0], leaving[2], jnp.where(upper, leaving[masks[1]], leaving[masks[0]]))
     )
-    blocks = gathered(split, masks, False, shared, False, lambda block: block)
+    blocks = gathered(split, masks, False, shared, True, lambda block: block)
     blocks[0] = own
     return by_xor([blocks[index] for index in range(GROUP)], rank)
 

time: 30.7 us -> 30.8 us (level)
  waiting for transfers between devices: 9.38 us -> 10.2 us
  starting transfers between devices: 16.7 us -> 15.9 us
    ppermute x9, starting transfers between devices: 15.4 us -> 14.6 us  [swapped(): return lax.ppermute(value, ('ep', 'tp'), pairs)]
    ppermute x4, waiting for transfers between devices: 0.8 us -> 1.38 us  [other_core(): return lax.ppermute(value, 'tp', [(0, 1), (1, 0)])]
where the time goes in v11:
time: 30.8 us; the launch traced here: 30.5 us
  starting transfers between devices  15.9 us (52%)
  waiting for transfers between devices  10.2 us (33%)
  other arithmetic  3.48 us (11%)
  matrix products  0.67 us (2%)
    ppermute x9, starting transfers between devices, swapped(): return lax.ppermute(value, ('ep', 'tp'), pairs)  14.6 us
    ppermute x9, waiting for transfers between devices, swapped(): return lax.ppermute(value, ('ep', 'tp'), pairs)  8.78 us
    concatenate x1, other arithmetic, expert_rows(): jnp.concatenate([w_gate, w_up], axis=1)  1.68 us
    ppermute x4, waiting for transfers between devices, other_core(): return lax.ppermute(value, 'tp', [(0, 1), (1, 0)])  1.38 us
    ppermute x4, starting transfers between devices, other_core(): return lax.ppermute(value, 'tp', [(0, 1), (1, 0)])  1.29 us
    select_n x6, other arithmetic, by_xor(): jnp.where(bit, blocks[index ^ mask], blocks[index])  0.86 us
    convert_element_type x1, other arithmetic, local(): return combined.astype(jnp.bfloat16)  0.7 us
  transfers between devices with their start and end apart: 13, of which 11 were waited for; matrix products, arithmetic and copies ran while one was open for 8% of the time, Pallas kernels for 0%

profile of v11, /device:TPU:0, one launch (start us, length us, event | category | flops | bytes accessed | tf_op | source)
XLA Modules:
  0.0 30.5 jit_solution(10278273746835127373)
XLA Ops:
  0.0 3.4 %collective-permute-start = (bf16[4,3584]{1,0:T(4,128)(2,1)}, bf16[4,3584]{1,0:T(4,128)(2,1)S(1)}, u32[]{:S(2)}, u32[]{:S(2)}) collective-permute-start(bf16[4,3584]{1,0:T(4,128)(2,1)} %param.6), channel_id=1, source_target_pairs={{0,7},{1,2},{2,5},{3,0},{4,3},{5,6},{6,1},{7,4},{8,15},{9,10},{10,... | collective-permute-start | bytes 86024 | tf_op jit(solution)/shard_map/ppermute | solution.py:20
  3.4 0.8 %collective-permute-start.2 = (bf16[4,3584]{1,0:T(4,128)(2,1)}, bf16[4,3584]{1,0:T(4,128)(2,1)S(1)}, u32[]{:S(2)}, u32[]{:S(2)}) collective-permute-start(bf16[4,3584]{1,0:T(4,128)(2,1)} %param.6), channel_id=1, source_target_pairs={{0,5},{1,4},{2,7},{3,6},{4,1},{5,0},{6,3},{7,2},{8,13},{9,12},{10,... | collective-permute-start | bytes 86024 | tf_op jit(solution)/shard_map/ppermute | solution.py:20
  4.2 0.8 %select_select_fusion = bf16[4,896]{1,0:T(4,128)(2,1)S(1)} fusion(bf16[4,3584]{1,0:T(4,128)(2,1)} %param.6, pred[]{:T(512)S(6)} %gt.7, pred[]{:T(512)S(6)} %gt.6), kind=kLoop, calls=%fused_computation.59 | loop fusion | flops 10752 | bytes 35842 | tf_op jit(solution)/shard_map/jit(_where)/select_n | solution.py:36
  5.2 0.7 %collective-permute-start.1 = (bf16[4,896]{1,0:T(4,128)(2,1)S(1)}, bf16[4,896]{1,0:T(4,128)(2,1)S(1)}, u32[]{:S(2)}, u32[]{:S(2)}) collective-permute-start(bf16[4,896]{1,0:T(4,128)(2,1)S(1)} %fusion.9), channel_id=1, source_target_pairs={{0,1},{1,0},{2,3},{3,2},{4,5},{5,4},{6,7},{7,6},{8,9},{9,8},{10,11... | collective-permute-start | bytes 21512 | tf_op jit(solution)/shard_map/ppermute | solution.py:28
  5.9 1.1 %collective-permute-done.2 = bf16[4,3584]{1,0:T(4,128)(2,1)S(1)} collective-permute-done((bf16[4,3584]{1,0:T(4,128)(2,1)}, bf16[4,3584]{1,0:T(4,128)(2,1)S(1)}, u32[]{:S(2)}, u32[]{:S(2)}) %collective-permute-start.2) | collective-permute-done | bytes 28704 | tf_op jit(solution)/shard_map/ppermute | solution.py:20
  7.2 2.3 %collective-permute-start.3 = (bf16[4,4,896]{2,1,0:T(4,128)(2,1)S(1)}, bf16[4,4,896]{2,1,0:T(4,128)(2,1)S(1)}, u32[]{:S(2)}, u32[]{:S(2)}) collective-permute-start(bf16[4,4,896]{2,1,0:T(4,128)(2,1)S(1)} %pad_maximum_fusion.1), channel_id=1, source_target_pairs={{0,9},{1,8},{2,11},{3,10},{4,13},{5,12},{6,15},{7,14},{8,1},{9,0},... | collective-permute-start | bytes 86024 | tf_op jit(solution)/shard_map/ppermute | solution.py:20
  9.5 1.7 %pad_maximum_fusion = bf16[896,1024]{1,0:T(8,128)(2,1)S(1)} fusion(bf16[896,512]{1,0:T(8,128)(2,1)} %bitcast.61, bf16[896,512]{1,0:T(8,128)(2,1)} %bitcast.62), kind=kLoop, calls=%fused_computation | loop fusion | flops 3670016 | bytes 3670016 | tf_op jit(solution)/shard_map/concatenate | solution.py:122
  11.2 0.4 %collective-permute-done.3 = bf16[4,4,896]{2,1,0:T(4,128)(2,1)S(1)} collective-permute-done((bf16[4,4,896]{2,1,0:T(4,128)(2,1)S(1)}, bf16[4,4,896]{2,1,0:T(4,128)(2,1)S(1)}, u32[]{:S(2)}, u32[]{:S(2)}) %collective-permute-start.3) | collective-permute-done | bytes 28704 | tf_op jit(solution)/shard_map/ppermute | solution.py:20
  11.6 0.4 %fusion.16 = (bf16[32,1024]{1,0:T(8,128)(2,1)S(1)}, f32[32,1024]{1,0:T(8,128)S(1)}) fusion(bf16[32,896]{1,0:T(8,128)(2,1)S(1)} %reshape.24, bf16[896,1024]{1,0:T(8,128)(2,1)S(1)} %pad_maximum_fusion), kind=kOutput, calls=%fused_computation.76 | convolution fusion | flops 58753024 | bytes 2088960 | tf_op jit(solution)/shard_map/dot_general | solution.py:123
  12.0 2.2 %collective-permute-start.4 = (bf16[32,1024]{1,0:T(8,128)(2,1)S(1)}, bf16[32,1024]{1,0:T(8,128)(2,1)S(1)}, u32[]{:S(2)}, u32[]{:S(2)}) collective-permute-start(bf16[32,1024]{1,0:T(8,128)(2,1)S(1)} %get-tuple-element.63), channel_id=1, source_target_pairs={{0,6},{1,7},{2,4},{3,5},{4,2},{5,3},{6,0},{7,1},{8,14},{9,15},{10,... | collective-permute-start | bytes 196616 | tf_op jit(solution)/shard_map/ppermute | solution.py:20
  14.2 0.3 collective-permute-start.5
  14.5 1.0 %collective-permute-start.6 = (bf16[32,1024]{1,0:T(8,128)(2,1)S(1)}, bf16[32,1024]{1,0:T(8,128)(2,1)S(1)}, u32[]{:S(2)}, u32[]{:S(2)}) collective-permute-start(bf16[32,1024]{1,0:T(8,128)(2,1)S(1)} %get-tuple-element.63), channel_id=1, source_target_pairs={{0,2},{1,3},{2,0},{3,1},{4,6},{5,7},{6,4},{7,5},{8,10},{9,11},{10,... | collective-permute-start | bytes 196616 | tf_op jit(solution)/shard_map/ppermute | solution.py:20
  15.5 2.1 %collective-permute-done.4 = bf16[32,1024]{1,0:T(8,128)(2,1)S(1)} collective-permute-done((bf16[32,1024]{1,0:T(8,128)(2,1)S(1)}, bf16[32,1024]{1,0:T(8,128)(2,1)S(1)}, u32[]{:S(2)}, u32[]{:S(2)}) %collective-permute-start.4) | collective-permute-done | bytes 65568 | tf_op jit(solution)/shard_map/ppermute | solution.py:20
  17.6 0.9 %collective-permute-done.5 = bf16[32,1024]{1,0:T(8,128)(2,1)S(1)} collective-permute-done((bf16[32,1024]{1,0:T(8,128)(2,1)S(1)}, bf16[32,1024]{1,0:T(8,128)(2,1)S(1)}, u32[]{:S(2)}, u32[]{:S(2)}) %collective-permute-start.5) | collective-permute-done | bytes 65568 | tf_op jit(solution)/shard_map/ppermute | solution.py:20
  19.2 0.5 %collective-permute-start.9 = (f32[16,896]{1,0:T(8,128)S(1)}, f32[16,896]{1,0:T(8,128)S(1)}, u32[]{:S(2)}, u32[]{:S(2)}) collective-permute-start(f32[16,896]{1,0:T(8,128)S(1)} %get-tuple-element.22), channel_id=1, source_target_pairs={{0,1},{1,0},{2,3},{3,2},{4,5},{5,4},{6,7},{7,6},{8,9},{9,8},{10,11... | collective-permute-start | bytes 172040 | tf_op jit(solution)/shard_map/ppermute | solution.py:28
  19.7 0.7 %collective-permute-done.7 = f32[16,896]{1,0:T(8,128)S(1)} collective-permute-done((f32[16,896]{1,0:T(8,128)S(1)}, f32[16,896]{1,0:T(8,128)S(1)}, u32[]{:S(2)}, u32[]{:S(2)}) %collective-permute-start.7) | collective-permute-done | bytes 57376 | tf_op jit(solution)/shard_map/ppermute | solution.py:28
  20.4 2.4 %collective-permute-start.8 = (bf16[4,1,4,896]{3,2,1,0:T(4,128)(2,1)S(1)}, bf16[4,1,4,896]{3,2,1,0:T(4,128)(2,1)S(1)}, u32[]{:S(2)}, u32[]{:S(2)}) collective-permute-start(bf16[4,1,4,896]{3,2,1,0:T(4,128)(2,1)S(1)} %bitcast.73), channel_id=1, source_target_pairs={{0,9},{1,8},{2,11},{3,10},{4,13},{5,12},{6,15},{7,14},{8,1},{9,0},... | collective-permute-start | bytes 86024 | tf_op jit(solution)/shard_map/ppermute | solution.py:20
  22.9 1.8 %collective-permute-done.8 = bf16[4,1,4,896]{3,2,1,0:T(4,128)(2,1)S(1)} collective-permute-done((bf16[4,1,4,896]{3,2,1,0:T(4,128)(2,1)S(1)}, bf16[4,1,4,896]{3,2,1,0:T(4,128)(2,1)S(1)}, u32[]{:S(2)}, u32[]{:S(2)}) %collective-permute-start.8) | collective-permute-done | bytes 28704 | tf_op jit(solution)/shard_map/ppermute | solution.py:20
  24.8 1.1 %collective-permute-start.10 = (bf16[2,4,896]{2,1,0:T(4,128)(2,1)S(1)}, bf16[2,4,896]{2,1,0:T(4,128)(2,1)S(1)}, u32[]{:S(2)}, u32[]{:S(2)}) collective-permute-start(bf16[2,4,896]{2,1,0:T(4,128)(2,1)S(1)} %get-tuple-element.25), channel_id=1, source_target_pairs={{0,2},{1,7},{2,0},{3,5},{4,6},{5,3},{6,4},{7,1},{8,10},{9,15},{10,... | collective-permute-start | bytes 43016 | tf_op jit(solution)/shard_map/ppermute | solution.py:20
  25.9 1.1 %collective-permute-start.12 = (bf16[2,4,896]{2,1,0:T(4,128)(2,1)S(1)}, bf16[2,4,896]{2,1,0:T(4,128)(2,1)S(1)}, u32[]{:S(2)}, u32[]{:S(2)}) collective-permute-start(bf16[2,4,896]{2,1,0:T(4,128)(2,1)S(1)} %get-tuple-element.26), channel_id=1, source_target_pairs={{0,5},{1,4},{2,7},{3,6},{4,1},{5,0},{6,3},{7,2},{8,13},{9,12},{10,... | collective-permute-start | bytes 43016 | tf_op jit(solution)/shard_map/ppermute | solution.py:20
  27.0 1.6 %collective-permute-done.10 = bf16[2,4,896]{2,1,0:T(4,128)(2,1)S(1)} collective-permute-done((bf16[2,4,896]{2,1,0:T(4,128)(2,1)S(1)}, bf16[2,4,896]{2,1,0:T(4,128)(2,1)S(1)}, u32[]{:S(2)}, u32[]{:S(2)}) %collective-permute-start.10) | collective-permute-done | bytes 14368 | tf_op jit(solution)/shard_map/ppermute | solution.py:20
  28.6 0.5 %collective-permute-done.12 = bf16[2,4,896]{2,1,0:T(4,128)(2,1)S(1)} collective-permute-done((bf16[2,4,896]{2,1,0:T(4,128)(2,1)S(1)}, bf16[2,4,896]{2,1,0:T(4,128)(2,1)S(1)}, u32[]{:S(2)}, u32[]{:S(2)}) %collective-permute-start.12) | collective-permute-done | bytes 14368 | tf_op jit(solution)/shard_map/ppermute | solution.py:20
  29.1 0.6 %collective-permute-done.11 = bf16[2,4,896]{2,1,0:T(4,128)(2,1)S(1)} collective-permute-done((bf16[2,4,896]{2,1,0:T(4,128)(2,1)S(1)}, bf16[2,4,896]{2,1,0:T(4,128)(2,1)S(1)}, u32[]{:S(2)}, u32[]{:S(2)}) %collective-permute-start.11) | collective-permute-done | bytes 14368 | tf_op jit(solution)/shard_map/ppermute | solution.py:28
  29.8 0.7 %add_convert_fusion = bf16[4,3584]{1,0:T(4,128)(2,1)} fusion(bf16[4,896]{1,0:T(4,128)(2,1)S(1)} %get-tuple-element.60, bf16[4,896]{1,0:T(4,128)(2,1)S(1)} %get-tuple-element.65, bf16[4,896]{1,0:T(4,128)(2,1)S(1)} %get-tuple-element.56, bf16[4,896]{1,0:T(4,128)(2,1)S(1)} %get-tuple-element.67, bf16[4,896]{1,0:T(4,128)(2,1)S(1)} %get-tuple-element.59, ...), kind=kLoop, calls=%fused_computation.12 | loop fusion | flops 286720 | bytes 86048 | tf_op jit(solution)/shard_map/convert_element_type | solution.py:167
  (38 shorter events, 1.2 us)
Async XLA Ops:
  0.0 18.8 %copy-start = (bf16[1,512,896]{2,1,0:T(8,128)(2,1)S(1)}, bf16[1,512,896]{2,1,0:T(8,128)(2,1)}, u32[]{:S(2)}) copy-start(bf16[1,512,896]{2,1,0:T(8,128)(2,1)} %param.11) | copy-start | bytes 2752516
  0.0 5.2 %collective-permute-start = (bf16[4,3584]{1,0:T(4,128)(2,1)}, bf16[4,3584]{1,0:T(4,128)(2,1)S(1)}, u32[]{:S(2)}, u32[]{:S(2)}) collective-permute-start(bf16[4,3584]{1,0:T(4,128)(2,1)} %param.6), channel_id=1, source_target_pairs={{0,7},{1,2},{2,5},{3,0},{4,3},{5,6},{6,1},{7,4},{8,15},{9,10},{10,... | collective-permute-start | bytes 86024 | tf_op jit(solution)/shard_map/ppermute | solution.py:20
  3.4 3.7 %collective-permute-start.2 = (bf16[4,3584]{1,0:T(4,128)(2,1)}, bf16[4,3584]{1,0:T(4,128)(2,1)S(1)}, u32[]{:S(2)}, u32[]{:S(2)}) collective-permute-start(bf16[4,3584]{1,0:T(4,128)(2,1)} %param.6), channel_id=1, source_target_pairs={{0,5},{1,4},{2,7},{3,6},{4,1},{5,0},{6,3},{7,2},{8,13},{9,12},{10,... | collective-permute-start | bytes 86024 | tf_op jit(solution)/shard_map/ppermute | solution.py:20
  5.2 1.9 %collective-permute-start.1 = (bf16[4,896]{1,0:T(4,128)(2,1)S(1)}, bf16[4,896]{1,0:T(4,128)(2,1)S(1)}, u32[]{:S(2)}, u32[]{:S(2)}) collective-permute-start(bf16[4,896]{1,0:T(4,128)(2,1)S(1)} %fusion.9), channel_id=1, source_target_pairs={{0,1},{1,0},{2,3},{3,2},{4,5},{5,4},{6,7},{7,6},{8,9},{9,8},{10,11... | collective-permute-start | bytes 21512 | tf_op jit(solution)/shard_map/ppermute | solution.py:28
  7.2 4.3 %collective-permute-start.3 = (bf16[4,4,896]{2,1,0:T(4,128)(2,1)S(1)}, bf16[4,4,896]{2,1,0:T(4,128)(2,1)S(1)}, u32[]{:S(2)}, u32[]{:S(2)}) collective-permute-start(bf16[4,4,896]{2,1,0:T(4,128)(2,1)S(1)} %pad_maximum_fusion.1), channel_id=1, source_target_pairs={{0,9},{1,8},{2,11},{3,10},{4,13},{5,12},{6,15},{7,14},{8,1},{9,0},... | collective-permute-start | bytes 86024 | tf_op jit(solution)/shard_map/ppermute | solution.py:20
  11.2 4.4 %copy-start.1 = (f32[4,2]{0,1:T(2,128)S(1)}, f32[4,2]{0,1:T(2,128)}, u32[]{:S(2)}) copy-start(f32[4,2]{0,1:T(2,128)} %param.8) | copy-start | bytes 100
  11.6 14.3 %copy-start.2 = (s32[4,2]{0,1:T(2,128)S(1)}, s32[4,2]{0,1:T(2,128)}, u32[]{:S(2)}) copy-start(s32[4,2]{0,1:T(2,128)} %param.7) | copy-start | bytes 100
  12.0 5.6 %collective-permute-start.4 = (bf16[32,1024]{1,0:T(8,128)(2,1)S(1)}, bf16[32,1024]{1,0:T(8,128)(2,1)S(1)}, u32[]{:S(2)}, u32[]{:S(2)}) collective-permute-start(bf16[32,1024]{1,0:T(8,128)(2,1)S(1)} %get-tuple-element.63), channel_id=1, source_target_pairs={{0,6},{1,7},{2,4},{3,5},{4,2},{5,3},{6,0},{7,1},{8,14},{9,15},{10,... | collective-permute-start | bytes 196616 | tf_op jit(solution)/shard_map/ppermute | solution.py:20
  14.2 4.3 %collective-permute-start.5 = (bf16[32,1024]{1,0:T(8,128)(2,1)S(1)}, bf16[32,1024]{1,0:T(8,128)(2,1)S(1)}, u32[]{:S(2)}, u32[]{:S(2)}) collective-permute-start(bf16[32,1024]{1,0:T(8,128)(2,1)S(1)} %get-tuple-element.63), channel_id=1, source_target_pairs={{0,4},{1,5},{2,6},{3,7},{4,0},{5,1},{6,2},{7,3},{8,12},{9,13},{10,... | collective-permute-start | bytes 196616 | tf_op jit(solution)/shard_map/ppermute | solution.py:20
  14.5 4.3 %collective-permute-start.6 = (bf16[32,1024]{1,0:T(8,128)(2,1)S(1)}, bf16[32,1024]{1,0:T(8,128)(2,1)S(1)}, u32[]{:S(2)}, u32[]{:S(2)}) collective-permute-start(bf16[32,1024]{1,0:T(8,128)(2,1)S(1)} %get-tuple-element.63), channel_id=1, source_target_pairs={{0,2},{1,3},{2,0},{3,1},{4,6},{5,7},{6,4},{7,5},{8,10},{9,11},{10,... | collective-permute-start | bytes 196616 | tf_op jit(solution)/shard_map/ppermute | solution.py:20
  19.1 1.3 %collective-permute-start.7 = (f32[16,896]{1,0:T(8,128)S(1)}, f32[16,896]{1,0:T(8,128)S(1)}, u32[]{:S(2)}, u32[]{:S(2)}) collective-permute-start(f32[16,896]{1,0:T(8,128)S(1)} %get-tuple-element.21), channel_id=1, source_target_pairs={{0,1},{1,0},{2,3},{3,2},{4,5},{5,4},{6,7},{7,6},{8,9},{9,8},{10,11... | collective-permute-start | bytes 172040 | tf_op jit(solution)/shard_map/ppermute | solution.py:28
  19.2 3.7 %collective-permute-start.9 = (f32[16,896]{1,0:T(8,128)S(1)}, f32[16,896]{1,0:T(8,128)S(1)}, u32[]{:S(2)}, u32[]{:S(2)}) collective-permute-start(f32[16,896]{1,0:T(8,128)S(1)} %get-tuple-element.22), channel_id=1, source_target_pairs={{0,1},{1,0},{2,3},{3,2},{4,5},{5,4},{6,7},{7,6},{8,9},{9,8},{10,11... | collective-permute-start | bytes 172040 | tf_op jit(solution)/shard_map/ppermute | solution.py:28
  20.4 4.3 %collective-permute-start.8 = (bf16[4,1,4,896]{3,2,1,0:T(4,128)(2,1)S(1)}, bf16[4,1,4,896]{3,2,1,0:T(4,128)(2,1)S(1)}, u32[]{:S(2)}, u32[]{:S(2)}) collective-permute-start(bf16[4,1,4,896]{3,2,1,0:T(4,128)(2,1)S(1)} %bitcast.73), channel_id=1, source_target_pairs={{0,9},{1,8},{2,11},{3,10},{4,13},{5,12},{6,15},{7,14},{8,1},{9,0},... | collective-permute-start | bytes 86024 | tf_op jit(solution)/shard_map/ppermute | solution.py:20
  24.8 3.8 %collective-permute-start.10 = (bf16[2,4,896]{2,1,0:T(4,128)(2,1)S(1)}, bf16[2,4,896]{2,1,0:T(4,128)(2,1)S(1)}, u32[]{:S(2)}, u32[]{:S(2)}) collective-permute-start(bf16[2,4,896]{2,1,0:T(4,128)(2,1)S(1)} %get-tuple-element.25), channel_id=1, source_target_pairs={{0,2},{1,7},{2,0},{3,5},{4,6},{5,3},{6,4},{7,1},{8,10},{9,15},{10,... | collective-permute-start | bytes 43016 | tf_op jit(solution)/shard_map/ppermute | solution.py:20
  25.9 3.2 %collective-permute-start.12 = (bf16[2,4,896]{2,1,0:T(4,128)(2,1)S(1)}, bf16[2,4,896]{2,1,0:T(4,128)(2,1)S(1)}, u32[]{:S(2)}, u32[]{:S(2)}) collective-permute-start(bf16[2,4,896]{2,1,0:T(4,128)(2,1)S(1)} %get-tuple-element.26), channel_id=1, source_target_pairs={{0,5},{1,4},{2,7},{3,6},{4,1},{5,0},{6,3},{7,2},{8,13},{9,12},{10,... | collective-permute-start | bytes 43016 | tf_op jit(solution)/shard_map/ppermute | solution.py:20
  28.6 1.2 %collective-permute-start.11 = (bf16[2,4,896]{2,1,0:T(4,128)(2,1)S(1)}, bf16[2,4,896]{2,1,0:T(4,128)(2,1)S(1)}, u32[]{:S(2)}, u32[]{:S(2)}) collective-permute-start(bf16[2,4,896]{2,1,0:T(4,128)(2,1)S(1)} %collective-permute-done.10), channel_id=1, source_target_pairs={{0,1},{1,0},{2,3},{3,2},{4,5},{5,4},{6,7},{7,6},{8,9},{9,8},{10,11... | collective-permute-start | bytes 43016 | tf_op jit(solution)/shard_map/ppermute | solution.py:28
